TPU v7x, 32 devices: a whole 2x2x4 slice. The times are simulated.
32 devices in a mesh: dp: 4 (over y, x), seq: 8 (over z, core).
Axes of the slice: x: 2, y: 2, z: 4, core: 2. Of those that a mesh axis runs over, the one named last changes fastest.
Arguments:
- tokens: int32 [128, 1024], P('dp', 'seq'), may hold values from 0 to 255
- targets: int32 [128, 1024], P('dp', 'seq'), may hold values from 0 to 255
- counted: int32 [128, 1024], P('dp', 'seq'), may hold values from 0 to 1, as said below
- table: float32 [256, 512], P(('dp', 'seq')), may hold values from -0.625 to 0.625
- w_in: float32 [1, 512, 2048], P(None, ('dp', 'seq')), may hold values from -0.25 to 0.25
- w_out: float32 [1, 1024, 512], P(None, ('dp', 'seq')), may hold values from -0.1875 to 0.1875
- w_up: float32 [1, 512, 2048], P(None, ('dp', 'seq')), may hold values from -0.25 to 0.25
- w_down: float32 [1, 2048, 512], P(None, ('dp', 'seq')), may hold values from -0.125 to 0.125
- gains: float32 [3, 512], replicated, as said below
- conv_taps: float32 [1, 4, 512], replicated, may hold values from -3 to 3
- gate_bias: float32 [1, 1024], replicated, as said below
- m_table: float32 [256, 512], P(('dp', 'seq')), may hold values from -3.0517578e-05 to 3.0517578e-05
- m_in: float32 [1, 512, 2048], P(None, ('dp', 'seq')), may hold values from -3.0517578e-05 to 3.0517578e-05
- m_out: float32 [1, 1024, 512], P(None, ('dp', 'seq')), may hold values from -3.0517578e-05 to 3.0517578e-05
- m_up: float32 [1, 512, 2048], P(None, ('dp', 'seq')), may hold values from -3.0517578e-05 to 3.0517578e-05
- m_down: float32 [1, 2048, 512], P(None, ('dp', 'seq')), may hold values from -3.0517578e-05 to 3.0517578e-05
- m_gains: float32 [3, 512], replicated, may hold values from -0.00012207031 to 0.00012207031
- m_taps: float32 [1, 4, 512], replicated, may hold values from -0.00012207031 to 0.00012207031
- m_bias: float32 [1, 1024], replicated, may hold values from -0.00012207031 to 0.00012207031
- v_table: float32 [256, 512], P(('dp', 'seq')), may hold values from 2.6276403e-11 to 1.0510561e-10
- v_in: float32 [1, 512, 2048], P(None, ('dp', 'seq')), may hold values from 2.6276403e-11 to 1.0510561e-10
- v_out: float32 [1, 1024, 512], P(None, ('dp', 'seq')), may hold values from 2.6276403e-11 to 1.0510561e-10
- v_up: float32 [1, 512, 2048], P(None, ('dp', 'seq')), may hold values from 2.6276403e-11 to 1.0510561e-10
- v_down: float32 [1, 2048, 512], P(None, ('dp', 'seq')), may hold values from 2.6276403e-11 to 1.0510561e-10
- v_gains: float32 [3, 512], replicated, may hold values from 4.2042245e-10 to 1.6816898e-09
- v_taps: float32 [1, 4, 512], replicated, may hold values from 4.2042245e-10 to 1.6816898e-09
- v_bias: float32 [1, 1024], replicated, may hold values from 4.2042245e-10 to 1.6816898e-09
Outputs:
- loss_sum: float32 [], replicated
- count_total: float32 [], replicated
- grad_norm: float32 [], replicated
- new_table: float32 [256, 512], P(('dp', 'seq'))
- new_in: float32 [1, 512, 2048], P(None, ('dp', 'seq'))
- new_out: float32 [1, 1024, 512], P(None, ('dp', 'seq'))
- new_up: float32 [1, 512, 2048], P(None, ('dp', 'seq'))
- new_down: float32 [1, 2048, 512], P(None, ('dp', 'seq'))
- new_gains: float32 [3, 512], replicated
- new_taps: float32 [1, 4, 512], replicated
- new_bias: float32 [1, 1024], replicated
- next_m_table: float32 [256, 512], P(('dp', 'seq'))
- next_m_in: float32 [1, 512, 2048], P(None, ('dp', 'seq'))
- next_m_out: float32 [1, 1024, 512], P(None, ('dp', 'seq'))
- next_m_up: float32 [1, 512, 2048], P(None, ('dp', 'seq'))
- next_m_down: float32 [1, 2048, 512], P(None, ('dp', 'seq'))
- next_m_gains: float32 [3, 512], replicated
- next_m_taps: float32 [1, 4, 512], replicated
- next_m_bias: float32 [1, 1024], replicated
- next_v_table: float32 [256, 512], P(('dp', 'seq'))
- next_v_in: float32 [1, 512, 2048], P(None, ('dp', 'seq'))
- next_v_out: float32 [1, 1024, 512], P(None, ('dp', 'seq'))
- next_v_up: float32 [1, 512, 2048], P(None, ('dp', 'seq'))
- next_v_down: float32 [1, 2048, 512], P(None, ('dp', 'seq'))
- next_v_gains: float32 [3, 512], replicated
- next_v_taps: float32 [1, 4, 512], replicated
- next_v_bias: float32 [1, 1024], replicated
Inputs may be any that keep to these rules, and one draw needn't show every extreme that they name: `counted`: each position's chance of counting rises along the sequence. `gains`: positive. `gate_bias`: negative or zero.
All inputs are finite; a program needn't handle non-finite values.
Results may differ from a plain program's by a relative error of at most 0.0006.
The roundings to bfloat16 on the way count: a program that leaves them out, or rounds other values in their place, can miss the bound.
Values may be sent and summed in bfloat16 or wider, within the bound.
A program may use at most 384 MiB of HBM per device.

v0:
```python
import jax
import jax.numpy as jnp
from jax import lax
from jax.sharding import PartitionSpec as P

V = 256
MICRO = 2
STEP = 3


EPS = 1e-06
CLIP = 0.01
BETA_ONE = 0.5
BETA_TWO = 0.5
ADAM_EPS = 1e-08
RATE_MATRIX = 0.03
RATE_VECTOR = 0.3
WEIGHT_DECAY = 0.1


def from_behind(x, axis, by):
    devices = lax.axis_size(axis)
    pairs = [(i, i + by) for i in range(devices) if 0 <= i + by < devices]
    return lax.ppermute(x, axis, pairs)


def carried_in(part, axis, combine, identity, reverse):
    count = lax.axis_size(axis)
    place = lax.axis_index(axis)
    ahead = count - 1 - place if reverse else place
    gathered = jax.tree.map(lambda a: lax.all_gather(a, axis), part)
    state = jax.tree.map(lambda a, e: jnp.zeros_like(a) + jnp.asarray(e, a.dtype), part, identity)

    def one(lap, state):
        source = count - 1 - lap if reverse else lap
        return combine(
            state, jax.tree.map(lambda a: lax.dynamic_index_in_dim(a, source, 0, False), gathered)
        )

    return lax.fori_loop(0, ahead, one, state)


def matmul(left, right):
    return jnp.dot(left, right, preferred_element_type=jnp.float32)


def matmul_tn(left, right):
    return lax.dot_general(
        left, right, (((0,), (0,)), ((), ())), preferred_element_type=jnp.float32
    )


def matmul_nt(left, right):
    return lax.dot_general(
        left, right, (((1,), (1,)), ((), ())), preferred_element_type=jnp.float32
    )


def rms_norm(values, gain):
    return values * lax.rsqrt(jnp.mean(values * values, axis=-1, keepdims=True) + EPS) * gain


def combine(earlier, later):
    return (earlier[0] * later[0], later[0] * earlier[1] + later[1])


def gates(gate, cand):
    return (jax.nn.sigmoid(-gate), jax.nn.sigmoid(gate) * jax.nn.softplus(cand))


def conv_apply(padded, taps, length):
    total = taps[0] * padded[0:length].astype(jnp.float32)
    for k in range(1, taps.shape[0]):
        total = total + taps[k] * padded[k : k + length].astype(jnp.float32)
    return total


def adam(weight, grad, first, second, rate, decay):
    first = BETA_ONE * first + (1.0 - BETA_ONE) * grad
    second = BETA_TWO * second + (1.0 - BETA_TWO) * grad * grad
    fix_one = 1.0 - BETA_ONE**STEP
    fix_two = 1.0 - BETA_TWO**STEP
    update = first / fix_one / (jnp.sqrt(second / fix_two) + ADAM_EPS)
    return (weight - rate * (update + decay * weight), first, second)


def mixer_front(queue, rim, taps, bias, w_in):
    span, seqs, width = queue.shape
    padded = jnp.concatenate([rim, queue], axis=0)
    conv_low = conv_apply(padded, taps, span).astype(jnp.bfloat16)
    pre = matmul(conv_low.reshape(span * seqs, width), w_in).reshape(span, seqs, -1)
    hidden = bias.shape[0]
    keep, write = gates(pre[..., :hidden] + bias, pre[..., hidden:])
    return (padded, conv_low, pre, keep, write)


def block_tail(state, resid, gain_b, w_out, w_up, w_down):
    span, seqs, width = resid.shape
    state_low = state.astype(jnp.bfloat16).reshape(span * seqs, -1)
    mixed = resid + matmul(state_low, w_out).reshape(span, seqs, width)
    normed_low = rms_norm(mixed, gain_b).astype(jnp.bfloat16).reshape(span * seqs, width)
    lifted = matmul(normed_low, w_up)
    active_low = jax.nn.gelu(lifted).astype(jnp.bfloat16)
    result = mixed + matmul(active_low, w_down).reshape(span, seqs, width)
    return (result, (state_low, mixed, normed_low, lifted, active_low))


def layer_forward(resid, taps, gain_a, gain_b, bias, mats):
    span = resid.shape[0]
    kernel = taps.shape[0]
    queue = rms_norm(resid, gain_a).astype(jnp.bfloat16)
    rim = from_behind(queue[span - kernel + 1 :], "seq", 1)
    padded, conv_low, pre, keep, write = mixer_front(queue, rim, taps, bias, mats[0])
    decay, local = lax.associative_scan(combine, (keep, write), axis=0)
    ones = jnp.ones_like(local[0])
    carry_in = carried_in(
        (decay[-1], local[-1]), "seq", combine, (ones, jnp.zeros_like(ones)), False
    )[1]
    state = local + decay * carry_in[None]
    result, unused = block_tail(state, resid, gain_b, mats[1], mats[2], mats[3])
    return (result, rim, carry_in)


def layer_backward(grad, resid, rim, carry_in, taps, gain_a, gain_b, bias, mats):
    w_in, w_out, w_up, w_down = mats
    span, seqs, width = resid.shape
    kernel = taps.shape[0]
    hidden = bias.shape[0]
    normed_a, norm_back = jax.vjp(rms_norm, resid, gain_a)
    queue = normed_a.astype(jnp.bfloat16)
    padded, conv_low, pre, keep, write = mixer_front(queue, rim, taps, bias, w_in)
    decay, local = lax.associative_scan(combine, (keep, write), axis=0)
    state = local + decay * carry_in[None]
    result, (state_low, mixed, normed_low, lifted, active_low) = block_tail(
        state, resid, gain_b, w_out, w_up, w_down
    )
    grad_low = grad.astype(jnp.bfloat16).reshape(span * seqs, width)
    g_down = matmul_tn(active_low, grad_low)
    d_active = matmul_nt(grad_low, w_down)
    d_lifted_low = jax.vjp(jax.nn.gelu, lifted)[1](d_active)[0].astype(jnp.bfloat16)
    g_up = matmul_tn(normed_low, d_lifted_low)
    d_normed = matmul_nt(d_lifted_low, w_up).reshape(span, seqs, width)
    d_mixed, d_gain_b = jax.vjp(rms_norm, mixed, gain_b)[1](d_normed)
    d_mixed = grad + d_mixed
    mixed_low = d_mixed.astype(jnp.bfloat16).reshape(span * seqs, width)
    g_out = matmul_tn(state_low, mixed_low)
    d_state = matmul_nt(mixed_low, w_out).reshape(span, seqs, hidden)
    follow = jnp.concatenate([keep[1:], jnp.ones_like(keep[:1])], axis=0)
    reach, back_local = lax.associative_scan(combine, (follow, d_state), axis=0, reverse=True)
    ones = jnp.ones_like(keep[0])
    summary = (keep[0] * reach[0], keep[0] * back_local[0])
    carry_out = carried_in(summary, "seq", combine, (ones, jnp.zeros_like(ones)), True)[1]
    adjoint = back_local + reach * carry_out[None]
    before = jnp.concatenate([carry_in[None], state[:-1]], axis=0)
    d_gate, d_cand = jax.vjp(gates, pre[..., :hidden] + bias, pre[..., hidden:])[1](
        (adjoint * before, adjoint)
    )
    d_bias = jnp.sum(d_gate, axis=(0, 1))
    d_pre = (
        jnp.concatenate([d_gate, d_cand], axis=-1)
        .astype(jnp.bfloat16)
        .reshape(span * seqs, 2 * hidden)
    )
    g_in = matmul_tn(conv_low.reshape(span * seqs, width), d_pre)
    d_conv = matmul_nt(d_pre, w_in).reshape(span, seqs, width)
    beyond = from_behind(d_conv[: kernel - 1].astype(jnp.bfloat16), "seq", -1).astype(jnp.float32)
    extended = jnp.concatenate([d_conv, beyond], axis=0)
    d_queue = taps[0] * extended[kernel - 1 : kernel - 1 + span]
    tap_grads = [jnp.sum(d_conv * padded[0:span].astype(jnp.float32), axis=(0, 1))]
    for k in range(1, kernel):
        d_queue = d_queue + taps[k] * extended[kernel - 1 - k : kernel - 1 - k + span]
        tap_grads.append(jnp.sum(d_conv * padded[k : k + span].astype(jnp.float32), axis=(0, 1)))
    rounded = lax.optimization_barrier(d_queue.astype(jnp.bfloat16)).astype(jnp.float32)
    d_resid, d_gain_a = norm_back(rounded)
    return (
        d_mixed + d_resid,
        (g_in, g_out, g_up, g_down),
        (jnp.stack(tap_grads), d_gain_a, d_gain_b, d_bias),
    )


def body(
    tokens,
    targets,
    counted,
    table,
    w_in,
    w_out,
    w_up,
    w_down,
    gains,
    conv_taps,
    gate_bias,
    m_table,
    m_in,
    m_out,
    m_up,
    m_down,
    m_gains,
    m_taps,
    m_bias,
    v_table,
    v_in,
    v_out,
    v_up,
    v_down,
    v_gains,
    v_taps,
    v_bias,
):
    layers = w_in.shape[0]
    seq_dev, span = tokens.shape
    rows = seq_dev // MICRO
    width = table.shape[1]
    vocab = V
    mask = counted.astype(jnp.float32)
    count = lax.psum(jnp.sum(mask), ("dp", "seq"))
    shards = (
        w_in.astype(jnp.bfloat16),
        w_out.astype(jnp.bfloat16),
        w_up.astype(jnp.bfloat16),
        w_down.astype(jnp.bfloat16),
    )
    layer_gains = gains[: 2 * layers].reshape(layers, 2, width)
    columns = jnp.arange(vocab, dtype=jnp.int32)

    def forward_step(resid, inputs):
        pieces, taps, pair, bias = inputs
        mats = (
            lax.all_gather(pieces[0], ("dp", "seq"), axis=0, tiled=True),
            lax.all_gather(pieces[1], ("dp", "seq"), axis=0, tiled=True),
            lax.all_gather(pieces[2], ("dp", "seq"), axis=0, tiled=True),
            lax.all_gather(pieces[3], ("dp", "seq"), axis=0, tiled=True),
        )
        result, rim, carry_in = layer_forward(resid, taps, pair[0], pair[1], bias, mats)
        return (result, (resid, rim, carry_in))

    def backward_step(grad, inputs):
        saved, pieces, taps, pair, bias = inputs
        mats = (
            lax.all_gather(pieces[0], ("dp", "seq"), axis=0, tiled=True),
            lax.all_gather(pieces[1], ("dp", "seq"), axis=0, tiled=True),
            lax.all_gather(pieces[2], ("dp", "seq"), axis=0, tiled=True),
            lax.all_gather(pieces[3], ("dp", "seq"), axis=0, tiled=True),
        )
        grad, full, small = layer_backward(
            grad, saved[0], saved[1], saved[2], taps, pair[0], pair[1], bias, mats
        )
        full = (
            lax.psum_scatter(full[0], ("dp", "seq"), scatter_dimension=0, tiled=True),
            lax.psum_scatter(full[1], ("dp", "seq"), scatter_dimension=0, tiled=True),
            lax.psum_scatter(full[2], ("dp", "seq"), scatter_dimension=0, tiled=True),
            lax.psum_scatter(full[3], ("dp", "seq"), scatter_dimension=0, tiled=True),
        )
        return (grad, (full, small))

    loss = jnp.zeros((), jnp.float32)
    g_table = jnp.zeros((vocab, width), jnp.float32)
    acc_full = None
    acc_small = None
    for index in range(MICRO):
        tok = tokens[index * rows : (index + 1) * rows].T.reshape(-1)
        tgt = targets[index * rows : (index + 1) * rows].T.reshape(-1)
        weights = mask[index * rows : (index + 1) * rows].T.reshape(-1)
        tab = lax.all_gather(table.astype(jnp.bfloat16), ("dp", "seq"), axis=0, tiled=True)
        picks = tok[:, None] == columns[None, :]
        resid = matmul(picks.astype(jnp.bfloat16), tab).reshape(span, rows, width)
        final, saved = lax.scan(forward_step, resid, (shards, conv_taps, layer_gains, gate_bias))
        normed_f, final_back = jax.vjp(rms_norm, final, gains[2 * layers])
        normed_low = normed_f.astype(jnp.bfloat16).reshape(span * rows, width)
        logits = matmul_nt(normed_low, tab)
        top = jnp.max(logits, axis=-1, keepdims=True)
        lse = jnp.log(jnp.sum(jnp.exp(logits - top), axis=-1)) + top[:, 0]
        hits = (tgt[:, None] == columns[None, :]).astype(jnp.float32)
        picked = jnp.sum(hits * logits, axis=-1)
        loss = loss + jnp.sum(weights * (lse - picked))
        d_logits = ((jnp.exp(logits - lse[:, None]) - hits) * (weights / count)[:, None]).astype(
            jnp.bfloat16
        )
        g_table = g_table + matmul_tn(d_logits, normed_low)
        d_normed = matmul(d_logits, tab).reshape(span, rows, width)
        d_final, d_gain_f = final_back(d_normed)
        grad0, (full, small) = lax.scan(
            backward_step, d_final, (saved, shards, conv_taps, layer_gains, gate_bias), reverse=True
        )
        g_table = g_table + lax.dot_general(
            picks.astype(jnp.float32),
            grad0.reshape(span * rows, width),
            (((0,), (0,)), ((), ())),
            precision=lax.Precision.HIGHEST,
        )
        layer_gain_grads = jnp.stack([small[1], small[2]], axis=1).reshape(2 * layers, width)
        vectors = (jnp.concatenate([layer_gain_grads, d_gain_f[None]], axis=0), small[0], small[3])
        if index == 0:
            acc_full, acc_small = (full, vectors)
        else:
            acc_full = jax.tree.map(lambda a, b: a + b, acc_full, full)
            acc_small = jax.tree.map(lambda a, b: a + b, acc_small, vectors)
    table_shard = lax.psum_scatter(g_table, ("dp", "seq"), scatter_dimension=0, tiled=True)
    g_gains, g_taps, g_bias = lax.psum((acc_small[0], acc_small[1], acc_small[2]), ("dp", "seq"))
    matrices = (table_shard, acc_full[0], acc_full[1], acc_full[2], acc_full[3])
    squares = jnp.zeros((), jnp.float32)
    for grad in matrices:
        squares = squares + jnp.sum(grad * grad)
    squares_all, loss_all = lax.psum((squares, loss), ("dp", "seq"))
    small_squares = jnp.sum(g_gains * g_gains) + jnp.sum(g_taps * g_taps) + jnp.sum(g_bias * g_bias)
    norm = jnp.sqrt(squares_all + small_squares)
    scale = jnp.minimum(1.0, CLIP / (norm + 1e-06))
    params = (table, w_in, w_out, w_up, w_down, gains, conv_taps, gate_bias)
    grads = matrices + (g_gains, g_taps, g_bias)
    firsts = (m_table, m_in, m_out, m_up, m_down, m_gains, m_taps, m_bias)
    seconds = (v_table, v_in, v_out, v_up, v_down, v_gains, v_taps, v_bias)
    news, next_m, next_v = ([], [], [])
    for index in range(8):
        rate = RATE_MATRIX if index < 5 else RATE_VECTOR
        decay = WEIGHT_DECAY if index < 5 else 0.0
        weight, first, second = adam(
            params[index], grads[index] * scale, firsts[index], seconds[index], rate, decay
        )
        news.append(weight)
        next_m.append(first)
        next_v.append(second)
    return (
        loss_all,
        count,
        norm,
        news[0],
        news[1],
        news[2],
        news[3],
        news[4],
        news[5],
        news[6],
        news[7],
        next_m[0],
        next_m[1],
        next_m[2],
        next_m[3],
        next_m[4],
        next_m[5],
        next_m[6],
        next_m[7],
        next_v[0],
        next_v[1],
        next_v[2],
        next_v[3],
        next_v[4],
        next_v[5],
        next_v[6],
        next_v[7],
    )


def solution(mesh):
    return jax.shard_map(
        body,
        mesh=mesh,
        in_specs=(
            P("dp", "seq"),
            P("dp", "seq"),
            P("dp", "seq"),
            P(("dp", "seq"), None),
            P(None, ("dp", "seq"), None),
            P(None, ("dp", "seq"), None),
            P(None, ("dp", "seq"), None),
            P(None, ("dp", "seq"), None),
            P(),
            P(),
            P(),
            P(("dp", "seq"), None),
            P(None, ("dp", "seq"), None),
            P(None, ("dp", "seq"), None),
            P(None, ("dp", "seq"), None),
            P(None, ("dp", "seq"), None),
            P(),
            P(),
            P(),
            P(("dp", "seq"), None),
            P(None, ("dp", "seq"), None),
            P(None, ("dp", "seq"), None),
            P(None, ("dp", "seq"), None),
            P(None, ("dp", "seq"), None),
            P(),
            P(),
            P(),
        ),
        out_specs=(
            P(),
            P(),
            P(),
            P(("dp", "seq"), None),
            P(None, ("dp", "seq"), None),
            P(None, ("dp", "seq"), None),
            P(None, ("dp", "seq"), None),
            P(None, ("dp", "seq"), None),
            P(),
            P(),
            P(),
            P(("dp", "seq"), None),
            P(None, ("dp", "seq"), None),
            P(None, ("dp", "seq"), None),
            P(None, ("dp", "seq"), None),
            P(None, ("dp", "seq"), None),
            P(),
            P(),
            P(),
            P(("dp", "seq"), None),
            P(None, ("dp", "seq"), None),
            P(None, ("dp", "seq"), None),
            P(None, ("dp", "seq"), None),
            P(None, ("dp", "seq"), None),
            P(),
            P(),
            P(),
        ),
        check_vma=False,
    )
```

profile of v0, /device:TPU:0, one launch (start us, length us, event | category | flops | bytes accessed | tf_op | source)
XLA Modules:
  0.0 3584.7 jit_solution(2170979037794304297)
XLA Ops:
  13.8 44.4 %all_gather.84 = bf16[256,512]{1,0:T(8,128)(2,1)S(1)} all-gather(bf16[8,512]{1,0:T(8,128)(2,1)S(1)} %convert_element_type.234), channel_id=1, replica_groups=mesh['dp'=4,'seq'=8] {'dp','seq'}, dimensions={0}, use_global_device_ids=true | all-gather | bytes 270336 | tf_op jit(solution)/shard_map/all_gather | solution.py:265
  81.5 37.8 %psum.43 = f32[]{:T(128)} all-reduce(f32[]{:T(128)} %convert_reduce_fusion), channel_id=1, replica_groups=mesh['dp'=4,'seq'=8] {'dp','seq'}, use_global_device_ids=true, to_apply=%region_20.21 | all-reduce | flops 1 | bytes 8 | tf_op jit(solution)/shard_map/psum | solution.py:217
  148.1 25.6 fusion.217
  175.4 18.8 slice.1714
  194.2 18.5 slice.1668
  212.8 18.6 slice.1667
  233.1 18.8 slice.1791
  251.9 18.5 slice.1745
  270.4 18.5 slice.1744
  290.7 18.5 slice.1670
  309.1 18.5 slice.1666
  448.8 18.8 slice.1665
  469.2 18.5 slice.1747
  487.7 18.7 slice.1743
  628.2 18.9 slice.1742
  770.6 14.3 pad.603
  803.6 14.4 pad.602
  819.3 15.2 all_gather.86
  834.5 14.3 pad.589
  854.0 14.3 pad.588
  869.6 14.7 all_gather.87
  1007.9 14.3 pad.631
  1056.5 15.0 all_gather.91
  1071.5 14.3 pad.617
  1091.0 14.3 pad.616
  1106.7 14.7 all_gather.92
  1121.4 16.7 multiply_add_fusion.2
  1158.6 18.5 slice.1819
  1177.1 18.5 slice.1812
  1195.5 18.5 slice.1810
  1222.6 18.5 slice.1896
  1241.1 18.5 slice.1889
  1259.7 18.5 slice.1887
  1380.5 17.3 fusion.6
  1408.3 20.3 fusion.13
  1447.8 14.9 fusion.84
  1468.4 18.5 slice.1864
  1486.9 18.5 slice.1816
  1505.4 18.5 slice.1814
  1875.9 14.3 pad.659
  1890.2 14.3 pad.645
  1936.9 18.5 slice.1941
  1955.5 18.5 slice.1893
  1973.9 18.5 slice.1891
  2294.3 14.3 pad.672
  2308.6 14.3 pad.686
  2323.0 14.4 pad.687
  2337.4 14.5 pad.673
  2377.8 64.2 %rev.24 = f32[128,16,1024]{2,0,1:T(8,128)} reverse(f32[128,16,1024]{2,0,1:T(8,128)} %add.1533), dimensions={0} | reverse | bytes 16777216 | tf_op jit(solution)/shard_map/while/body/eval_jaxpr/rev | solution.py:149
  2442.1 64.2 %rev.25 = f32[128,16,1024]{2,0,1:T(8,128)} reverse(f32[128,16,1024]{2,0,1:T(8,128)} %add.1540), dimensions={0} | reverse | bytes 16777216 | tf_op jit(solution)/shard_map/while/body/eval_jaxpr/rev | solution.py:149
  2506.4 14.8 all_gather.93
  2521.1 15.3 all_gather.94
  2536.8 20.5 fusion.233
  2571.1 64.3 %rev.26 = f32[128,16,1024]{2,0,1:T(8,128)} reverse(f32[128,16,1024]{2,0,1:T(8,128)} %add.1568), dimensions={0} | reverse | bytes 16777216 | tf_op jit(solution)/shard_map/while/body/eval_jaxpr/rev | solution.py:149
  2635.4 64.3 %rev.27 = f32[128,16,1024]{2,0,1:T(8,128)} reverse(f32[128,16,1024]{2,0,1:T(8,128)} %add.1575), dimensions={0} | reverse | bytes 16777216 | tf_op jit(solution)/shard_map/while/body/eval_jaxpr/rev | solution.py:149
  2699.8 16.1 all_gather.95
  2715.9 14.8 all_gather.96
  2731.0 20.2 fusion.231
  2895.6 66.3 %reduce-scatter.6.cloned.1.call-done = f32[8,512]{1,0:T(8,128)} async-done(((f32[256,512]{1,0:T(8,128)}), f32[8,512]{1,0:T(8,128)}) %reduce-scatter.6.cloned.1.call-update) | async-done | bytes 16400 | tf_op jit(solution)/shard_map/reduce_scatter | solution.py:299
  2963.3 134.7 %reduce-scatter.10.cloned.1.call-done = f32[32,512]{1,0:T(8,128)} async-done(((f32[1024,512]{1,0:T(8,128)}), f32[32,512]{1,0:T(8,128)}) %reduce-scatter.10.cloned.1.call-update) | async-done | bytes 65552 | tf_op jit(solution)/shard_map/while/body/eval_jaxpr/reduce_scatter | solution.py:251
  3099.4 139.2 %reduce-scatter.8.cloned.1.call-done = f32[16,2048]{1,0:T(8,128)} async-done(((f32[512,2048]{1,0:T(8,128)}), f32[16,2048]{1,0:T(8,128)}) %reduce-scatter.8.cloned.1.call-update) | async-done | bytes 131088 | tf_op jit(solution)/shard_map/while/body/eval_jaxpr/reduce_scatter | solution.py:250
  3242.1 138.2 %reduce-scatter.12.cloned.1.call-done = f32[16,2048]{1,0:T(8,128)} async-done(((f32[512,2048]{1,0:T(8,128)}), f32[16,2048]{1,0:T(8,128)}) %reduce-scatter.12.cloned.1.call-update) | async-done | bytes 131088 | tf_op jit(solution)/shard_map/while/body/eval_jaxpr/reduce_scatter | solution.py:252
  3382.5 140.2 %reduce-scatter.14.cloned.1.call-done = f32[64,512]{1,0:T(8,128)} async-done(((f32[2048,512]{1,0:T(8,128)}), f32[64,512]{1,0:T(8,128)}) %reduce-scatter.14.cloned.1.call-update) | async-done | bytes 131088 | tf_op jit(solution)/shard_map/while/body/eval_jaxpr/reduce_scatter | solution.py:253
  3524.9 37.5 %all-reduce.116 = (f32[]{:T(128)}, f32[]{:T(128)}, f32[3,512]{1,0:T(4,128)S(1)}, f32[1,4,512]{2,1,0:T(4,128)S(1)}, f32[1,1024]{1,0:T(1,128)S(1)}) all-reduce(f32[]{:T(128)S(6)} %add.1512, f32[]{:T(128)S(6)} %add.1589, f32[3,512]{1,0:T(4,128)S(1)} %maximum_add_fusion, ...), channel_id=1, replica_groups=mesh['dp'=4,'seq'=8] {'dp','seq'}, use_global_device_ids=true, to_apply=%region_18.19 | all-reduce | flops 4610 | bytes 36880 | tf_op jit(solution)/shard_map/psum | solution.py:305
  (1135 shorter events, 1674.9 us)
Async XLA Ops:
  7.2 123.6 %all-gather.9.cloned.1.call-start = ((), (), s32[]{:S(2)}) async-start(), calls=%async_computation.6 | async-start | bytes 2162688 | tf_op jit(solution)/shard_map/while/body/eval_jaxpr/all_gather | solution.py:230
  8.8 1129.3 %all-gather.11.cloned.1.call-start = ((), (), s32[]{:S(2)}) async-start(), calls=%async_computation.7 | async-start | bytes 1081344 | tf_op jit(solution)/shard_map/while/body/eval_jaxpr/all_gather | solution.py:231
  10.3 1292.5 %all-gather.13.cloned.1.call-start = ((), (), s32[]{:S(2)}) async-start(), calls=%async_computation.8 | async-start | bytes 2162688 | tf_op jit(solution)/shard_map/while/body/eval_jaxpr/all_gather | solution.py:232
  12.0 1301.3 %all-gather.15.cloned.1.call-start = ((), (), s32[]{:S(2)}) async-start(), calls=%async_computation.9 | async-start | bytes 2162688 | tf_op jit(solution)/shard_map/while/body/eval_jaxpr/all_gather | solution.py:233
  13.6 50.3 %copy-start.211 = (s32[2048]{0:T(1024)}, s32[2048]{0:T(1024)S(1)}, u32[]{:S(2)}) copy-start(s32[2048]{0:T(1024)S(1)} %eq.66) | copy-start | bytes 24580
  13.8 47.5 %copy-start.209 = (s32[2048]{0:T(1024)}, s32[2048]{0:T(1024)S(1)}, u32[]{:S(2)}) copy-start(s32[2048]{0:T(1024)S(1)} %eq.74) | copy-start | bytes 24580
  74.3 56.5 %copy-start.47 = (bf16[128,16,512]{2,0,1:T(8,128)(2,1)}, bf16[128,16,512]{2,0,1:T(8,128)(2,1)S(1)}, u32[]{:S(2)}) copy-start(bf16[128,16,512]{2,0,1:T(8,128)(2,1)S(1)} %get-tuple-element.831) | copy-start | bytes 6291460
  75.6 45.8 %collective-permute-start.1 = (bf16[3,16,512]{2,0,1:T(4,128)(2,1)S(1)}, bf16[3,16,512]{2,0,1:T(4,128)(2,1)S(1)}, u32[]{:S(2)}, u32[]{:S(2)}) collective-permute-start(bf16[3,16,512]{2,0,1:T(4,128)(2,1)S(1)} %slice.2017), channel_id=1, source_target_pairs={{0,1},{1,2},{2,3},{3,4},{4,5},{5,6},{6,7},{8,9},{9,10},{10,11},{11... | collective-permute-start | bytes 147464 | tf_op jit(solution)/shard_map/while/body/eval_jaxpr/ppermute | solution.py:24
  78.0 43.4 %collective-permute-start = (bf16[3,16,512]{2,0,1:T(4,128)(2,1)S(1)}, bf16[3,16,512]{2,0,1:T(4,128)(2,1)S(1)}, u32[]{:S(2)}, u32[]{:S(2)}) collective-permute-start(bf16[3,16,512]{2,0,1:T(4,128)(2,1)S(1)} %slice.1963), channel_id=1, source_target_pairs={{0,1},{1,2},{2,3},{3,4},{4,5},{5,6},{6,7},{8,9},{9,10},{10,11},{11... | collective-permute-start | bytes 147464 | tf_op jit(solution)/shard_map/while/body/eval_jaxpr/ppermute | solution.py:24
  80.6 2881.3 %reduce-scatter.6.cloned.1.call-start = ((), (), s32[]{:S(2)}) async-start(), calls=%async_computation.5 | async-start | bytes 540672 | tf_op jit(solution)/shard_map/reduce_scatter | solution.py:299
  81.4 49.3 %copy-start.235 = (f32[1,1,512]{2,1,0:T(1,128)}, f32[1,1,512]{2,1,0:T(1,128)S(1)}, u32[]{:S(2)}) copy-start(f32[1,1,512]{2,1,0:T(1,128)S(1)} %get-tuple-element.809) | copy-start | bytes 6148
  81.4 49.3 %copy-start.237 = (f32[1,1,512]{2,1,0:T(1,128)}, f32[1,1,512]{2,1,0:T(1,128)S(1)}, u32[]{:S(2)}) copy-start(f32[1,1,512]{2,1,0:T(1,128)S(1)} %get-tuple-element.810) | copy-start | bytes 6148
  81.4 49.3 %copy-start.239 = (f32[1,1,512]{2,1,0:T(1,128)}, f32[1,1,512]{2,1,0:T(1,128)S(1)}, u32[]{:S(2)}) copy-start(f32[1,1,512]{2,1,0:T(1,128)S(1)} %get-tuple-element.811) | copy-start | bytes 6148
  81.5 49.3 %copy-start.241 = (f32[1,1,512]{2,1,0:T(1,128)}, f32[1,1,512]{2,1,0:T(1,128)S(1)}, u32[]{:S(2)}) copy-start(f32[1,1,512]{2,1,0:T(1,128)S(1)} %get-tuple-element.812) | copy-start | bytes 6148
  148.1 25.6 copy-start.19
  628.2 19.9 copy-start.176
  628.2 19.9 copy-start.177
  628.2 20.5 copy-start.131
  628.2 20.5 copy-start.132
  677.4 28.0 copy-start.106
  853.9 30.4 copy-start.174
  853.9 30.4 copy-start.175
  854.0 31.0 copy-start.139
  854.0 31.6 copy-start.172
  854.0 31.6 copy-start.173
  914.8 28.1 copy-start.107
  1149.3 129.5 %copy-start.213 = (f32[128,16]{0,1:T(8,128)}, f32[128,16]{0,1:T(8,128)S(1)}, u32[]{:S(2)}) copy-start(f32[128,16]{0,1:T(8,128)S(1)} %get-tuple-element.839) | copy-start | bytes 24580
  1377.9 19.8 copy-start.120
  1408.3 20.3 copy-start.263
  2179.7 28.1 copy-start.108
  2442.1 64.2 %copy-start.159 = (f32[1,16,1024]{2,0,1:T(1,128)S(1)}, f32[1,16,1024]{2,0,1:T(1,128)}, u32[]{:S(2)}) copy-start(f32[1,16,1024]{2,0,1:T(1,128)} %get-tuple-element.664) | copy-start | bytes 196612
  2442.1 64.3 %copy-start.158 = (f32[1,16,1024]{2,0,1:T(1,128)S(1)}, f32[1,16,1024]{2,0,1:T(1,128)}, u32[]{:S(2)}) copy-start(f32[1,16,1024]{2,0,1:T(1,128)} %get-tuple-element.665) | copy-start | bytes 196612
  2442.1 94.7 %copy-start.182 = (f32[1,16,1024]{2,0,1:T(1,128)S(1)}, f32[1,16,1024]{2,0,1:T(1,128)}, u32[]{:S(2)}) copy-start(f32[1,16,1024]{2,0,1:T(1,128)} %dynamic_slice.127) | copy-start | bytes 196612
  2442.1 94.7 %copy-start.222 = (f32[1,1024]{1,0:T(1,128)S(1)}, f32[1,1024]{1,0:T(1,128)}, u32[]{:S(2)}) copy-start(f32[1,1024]{1,0:T(1,128)} %param.46) | copy-start | bytes 12292
  2569.8 212.4 %collective-permute-start.2 = (bf16[3,16,512]{2,0,1:T(4,128)(2,1)S(1)}, bf16[3,16,512]{2,0,1:T(4,128)(2,1)S(1)}, u32[]{:S(2)}, u32[]{:S(2)}) collective-permute-start(bf16[3,16,512]{2,0,1:T(4,128)(2,1)S(1)} %copy.169), channel_id=1, source_target_pairs={{1,0},{2,1},{3,2},{4,3},{5,4},{6,5},{7,6},{9,8},{10,9},{11,10},{12... | collective-permute-start | bytes 147464 | tf_op jit(solution)/shard_map/while/body/eval_jaxpr/ppermute | solution.py:24
  2635.4 95.6 %copy-start.181 = (f32[1,16,1024]{2,0,1:T(1,128)S(1)}, f32[1,16,1024]{2,0,1:T(1,128)}, u32[]{:S(2)}) copy-start(f32[1,16,1024]{2,0,1:T(1,128)} %dynamic_slice.128) | copy-start | bytes 196612
  2771.3 11.0 collective-permute-start.3
  2825.7 272.2 %reduce-scatter.10.cloned.1.call-start = ((), (), s32[]{:S(2)}) async-start(), calls=%async_computation.11 | async-start | bytes 2162688 | tf_op jit(solution)/shard_map/while/body/eval_jaxpr/reduce_scatter | solution.py:251
  2840.5 398.1 %reduce-scatter.8.cloned.1.call-start = ((), (), s32[]{:S(2)}) async-start(), calls=%async_computation.10 | async-start | bytes 4325376 | tf_op jit(solution)/shard_map/while/body/eval_jaxpr/reduce_scatter | solution.py:250
  2856.2 524.1 %reduce-scatter.12.cloned.1.call-start = ((), (), s32[]{:S(2)}) async-start(), calls=%async_computation.12 | async-start | bytes 4325376 | tf_op jit(solution)/shard_map/while/body/eval_jaxpr/reduce_scatter | solution.py:252
  2873.8 648.9 %reduce-scatter.14.cloned.1.call-start = ((), (), s32[]{:S(2)}) async-start(), calls=%async_computation.13 | async-start | bytes 4325376 | tf_op jit(solution)/shard_map/while/body/eval_jaxpr/reduce_scatter | solution.py:253
  2893.6 673.2 %copy-start.258 = (f32[1,1024]{1,0:T(1,128)S(1)}, f32[1,1024]{1,0:T(1,128)}, u32[]{:S(2)}) copy-start(f32[1,1024]{1,0:T(1,128)} %param.54) | copy-start | bytes 12292
  2893.6 673.2 %copy-start.259 = (f32[1,1024]{1,0:T(1,128)S(1)}, f32[1,1024]{1,0:T(1,128)}, u32[]{:S(2)}) copy-start(f32[1,1024]{1,0:T(1,128)} %param.62) | copy-start | bytes 12292
  2893.6 673.9 %copy-start.228 = (f32[1,4,512]{2,1,0:T(4,128)S(1)}, f32[1,4,512]{2,1,0:T(4,128)}, u32[]{:S(2)}) copy-start(f32[1,4,512]{2,1,0:T(4,128)} %param.45) | copy-start | bytes 24580
  2893.6 673.9 %copy-start.252 = (f32[1,4,512]{2,1,0:T(4,128)S(1)}, f32[1,4,512]{2,1,0:T(4,128)}, u32[]{:S(2)}) copy-start(f32[1,4,512]{2,1,0:T(4,128)} %param.53) | copy-start | bytes 24580
  2893.7 673.9 %copy-start.253 = (f32[1,4,512]{2,1,0:T(4,128)S(1)}, f32[1,4,512]{2,1,0:T(4,128)}, u32[]{:S(2)}) copy-start(f32[1,4,512]{2,1,0:T(4,128)} %param.61) | copy-start | bytes 24580
  2893.7 674.5 %copy-start.234 = (f32[3,512]{1,0:T(4,128)S(1)}, f32[3,512]{1,0:T(4,128)}, u32[]{:S(2)}) copy-start(f32[3,512]{1,0:T(4,128)} %param.44) | copy-start | bytes 18436
  2893.7 674.5 %copy-start.254 = (f32[3,512]{1,0:T(4,128)S(1)}, f32[3,512]{1,0:T(4,128)}, u32[]{:S(2)}) copy-start(f32[3,512]{1,0:T(4,128)} %param.52) | copy-start | bytes 18436
  2893.7 674.5 %copy-start.255 = (f32[3,512]{1,0:T(4,128)S(1)}, f32[3,512]{1,0:T(4,128)}, u32[]{:S(2)}) copy-start(f32[3,512]{1,0:T(4,128)} %param.60) | copy-start | bytes 18436
  2893.7 675.1 %copy-start.223 = (f32[8,512]{1,0:T(8,128)S(1)}, f32[8,512]{1,0:T(8,128)}, u32[]{:S(2)}) copy-start(f32[8,512]{1,0:T(8,128)} %param.39) | copy-start | bytes 49156
  2893.7 675.1 %copy-start.245 = (f32[8,512]{1,0:T(8,128)S(1)}, f32[8,512]{1,0:T(8,128)}, u32[]{:S(2)}) copy-start(f32[8,512]{1,0:T(8,128)} %param.47) | copy-start | bytes 49156
  2893.7 675.1 %copy-start.246 = (f32[8,512]{1,0:T(8,128)S(1)}, f32[8,512]{1,0:T(8,128)}, u32[]{:S(2)}) copy-start(f32[8,512]{1,0:T(8,128)} %param.55) | copy-start | bytes 49156
  2893.7 676.4 %copy-start.180 = (f32[1,32,512]{2,1,0:T(8,128)S(1)}, f32[1,32,512]{2,1,0:T(8,128)}, u32[]{:S(2)}) copy-start(f32[1,32,512]{2,1,0:T(8,128)} %param.41) | copy-start | bytes 196612
  2893.8 676.4 %copy-start.224 = (f32[1,32,512]{2,1,0:T(8,128)S(1)}, f32[1,32,512]{2,1,0:T(8,128)}, u32[]{:S(2)}) copy-start(f32[1,32,512]{2,1,0:T(8,128)} %param.49) | copy-start | bytes 196612
  2893.8 676.4 %copy-start.225 = (f32[1,32,512]{2,1,0:T(8,128)S(1)}, f32[1,32,512]{2,1,0:T(8,128)}, u32[]{:S(2)}) copy-start(f32[1,32,512]{2,1,0:T(8,128)} %param.57) | copy-start | bytes 196612
  2893.8 677.9 %copy-start.135 = (f32[1,16,2048]{2,1,0:T(8,128)S(1)}, f32[1,16,2048]{2,1,0:T(8,128)}, u32[]{:S(2)}) copy-start(f32[1,16,2048]{2,1,0:T(8,128)} %param.42) | copy-start | bytes 393220
  2893.8 677.9 %copy-start.187 = (f32[1,16,2048]{2,1,0:T(8,128)S(1)}, f32[1,16,2048]{2,1,0:T(8,128)}, u32[]{:S(2)}) copy-start(f32[1,16,2048]{2,1,0:T(8,128)} %param.50) | copy-start | bytes 393220
  2893.8 677.9 %copy-start.188 = (f32[1,16,2048]{2,1,0:T(8,128)S(1)}, f32[1,16,2048]{2,1,0:T(8,128)}, u32[]{:S(2)}) copy-start(f32[1,16,2048]{2,1,0:T(8,128)} %param.58) | copy-start | bytes 393220
  2893.8 679.6 %copy-start.137 = (f32[1,64,512]{2,1,0:T(8,128)S(1)}, f32[1,64,512]{2,1,0:T(8,128)}, u32[]{:S(2)}) copy-start(f32[1,64,512]{2,1,0:T(8,128)} %param.43) | copy-start | bytes 393220
  2893.8 679.6 %copy-start.189 = (f32[1,64,512]{2,1,0:T(8,128)S(1)}, f32[1,64,512]{2,1,0:T(8,128)}, u32[]{:S(2)}) copy-start(f32[1,64,512]{2,1,0:T(8,128)} %param.51) | copy-start | bytes 393220
  2893.8 679.6 %copy-start.190 = (f32[1,64,512]{2,1,0:T(8,128)S(1)}, f32[1,64,512]{2,1,0:T(8,128)}, u32[]{:S(2)}) copy-start(f32[1,64,512]{2,1,0:T(8,128)} %param.59) | copy-start | bytes 393220
  2893.8 681.3 %copy-start.138 = (f32[1,16,2048]{2,1,0:T(8,128)S(1)}, f32[1,16,2048]{2,1,0:T(8,128)}, u32[]{:S(2)}) copy-start(f32[1,16,2048]{2,1,0:T(8,128)} %param.40) | copy-start | bytes 393220
  2893.9 681.3 %copy-start.191 = (f32[1,16,2048]{2,1,0:T(8,128)S(1)}, f32[1,16,2048]{2,1,0:T(8,128)}, u32[]{:S(2)}) copy-start(f32[1,16,2048]{2,1,0:T(8,128)} %param.48) | copy-start | bytes 393220
  2893.9 681.3 %copy-start.192 = (f32[1,16,2048]{2,1,0:T(8,128)S(1)}, f32[1,16,2048]{2,1,0:T(8,128)}, u32[]{:S(2)}) copy-start(f32[1,16,2048]{2,1,0:T(8,128)} %param.56) | copy-start | bytes 393220
  (215 other events, 1267.8 us)
Sparse Core Ops, SparseCore 0:
  11.6 59.4 all-gather.8
  74.0 52.8 all-gather.10
  129.9 55.5 all-gather.12
  188.3 55.3 all-gather.14
  2825.9 136.0 reduce-scatter.5
  2964.1 133.7 reduce-scatter.9
  3100.2 138.3 reduce-scatter.7
  3240.9 139.3 reduce-scatter.11
  3382.5 140.0 reduce-scatter.13
where the time goes:
time: 3650 us; the launch traced here: 3580 us
  local copies, waits for them, and re-layouts  1910 us (52%)
  waiting for transfers between devices  619 us (17%)
  other arithmetic  549 us (15%)
  blocking collectives  240 us (7%)
  matrix products  229 us (6%)
    slice x98, local copies, waits for them, and re-layouts, layer_backward(): lax.associative_scan(combine, (follow, d_state), axis=0, reverse=True)  498 us
    slice x88, local copies, waits for them, and re-layouts, layer_forward(): decay, local = lax.associative_scan(combine, (keep, write), axis=0)  425 us
    pad x48, local copies, waits for them, and re-layouts, layer_backward(): lax.associative_scan(combine, (follow, d_state), axis=0, reverse=True)  314 us
    pad x48, local copies, waits for them, and re-layouts, layer_forward(): decay, local = lax.associative_scan(combine, (keep, write), axis=0)  301 us
    rev x4, local copies, waits for them, and re-layouts, layer_backward(): lax.associative_scan(combine, (follow, d_state), axis=0, reverse=True)  257 us
    reduce_scatter x1, waiting for transfers between devices, backward_step(): lax.psum_scatter(full[3], ('dp', 'seq'), scatter_dimension=0, tiled=True)  140 us
    reduce_scatter x1, waiting for transfers between devices, backward_step(): lax.psum_scatter(full[0], ('dp', 'seq'), scatter_dimension=0, tiled=True)  139 us
    reduce_scatter x1, waiting for transfers between devices, backward_step(): lax.psum_scatter(full[2], ('dp', 'seq'), scatter_dimension=0, tiled=True)  138 us
  transfers between devices with their start and end apart: 13, of which 5 were waited for; matrix products, arithmetic and copies ran while one was open for 39% of the time, Pallas kernels for 0%

commit v1 on v0

--- a/solution.py
+++ b/solution.py
@@ -1,6 +1,10 @@
+import functools
+
 import jax
 import jax.numpy as jnp
 from jax import lax
+from jax.experimental import pallas as pl
+from jax.experimental.pallas import tpu as pltpu
 from jax.sharding import PartitionSpec as P
 
 V = 256
@@ -351,9 +355,832 @@
     )
 
 
+BF = jnp.bfloat16
+F32 = jnp.float32
+MIB = 1 << 20
+LANES = 128
+ROWS = 8
+GELU_A = 0.7978845608028654
+GELU_B = 0.044715
+
+
+def nn(left, right):
+    return jnp.dot(left, right, preferred_element_type=F32)
+
+
+def tn(left, right):
+    return lax.dot_general(left, right, (((0,), (0,)), ((), ())), preferred_element_type=F32)
+
+
+def nt(left, right):
+    return lax.dot_general(left, right, (((1,), (1,)), ((), ())), preferred_element_type=F32)
+
+
+def inv_rms(values):
+    return lax.rsqrt(jnp.mean(values * values, axis=-1, keepdims=True) + EPS)
+
+
+def norm_back(values, inverse, gain, grad):
+    width = values.shape[-1]
+    scaled = grad * gain
+    dot = jnp.sum(scaled * values, axis=-1, keepdims=True)
+    return inverse * scaled - values * (inverse * inverse * inverse * dot * (1.0 / width))
+
+
+def column_sum(values):
+    return jnp.sum(values, axis=0, keepdims=True)
+
+
+def swap_halves(tile):
+    return pltpu.roll(tile, ROWS // 2, tile.ndim - 2)
+
+
+def one_hot(column, vocab):
+    lane = lax.broadcasted_iota(jnp.int32, (column.shape[0], vocab), 1)
+    return (column == lane).astype(F32).astype(BF)
+
+
+def one_hot_t(row, vocab):
+    place = lax.broadcasted_iota(jnp.int32, (vocab, row.shape[1]), 0)
+    return (row == place).astype(F32).astype(BF)
+
+
+def forward_kernel(
+    ids, tab, count, gains, taps, bias, w_in, w_out, w_up, w_down,
+    keep_o, p_o, q_o, ds_o, conv_o, queue_o, g_down, g_up, g_out, g_tab, small_o,
+    tab_low, qtab, padq, tail_s, carry_s, big, state_low, active, mixed_s, normed_s,
+):
+    step = pl.program_id(0)
+    rows, hidden = keep_o.shape
+    vocab, width = tab.shape
+    ff = w_up.shape[1]
+    kernel = taps.shape[0]
+    rim = (kernel - 1) * ROWS
+    steps = rows // ROWS
+    chunk = 256
+
+    @pl.when(step == 0)
+    def _():
+        low = tab[...].astype(BF)
+        tab_low[...] = low
+        wide = low.astype(F32)
+        qtab[...] = (wide * inv_rms(wide) * gains[0:1]).astype(BF)
+        g_down[...] = jnp.zeros_like(g_down)
+        g_up[...] = jnp.zeros_like(g_up)
+        g_out[...] = jnp.zeros_like(g_out)
+        g_tab[...] = jnp.zeros_like(g_tab)
+        small_o[...] = jnp.zeros_like(small_o)
+        tail_s[...] = jnp.zeros_like(tail_s)
+        carry_s[...] = jnp.zeros_like(carry_s)
+
+    wide_ids = ids[0]
+    columns = wide_ids.T
+    hot = one_hot(columns[:, 0:1], vocab)
+    queue = nn(hot, qtab[...])
+    queue_o[...] = queue.astype(BF)
+    padq[rim:, :] = queue
+    half = (
+        lax.broadcasted_iota(jnp.int32, (rim, width), 0) % ROWS < ROWS // 2
+    )
+    before = tail_s[...].reshape(kernel - 1, ROWS, width)
+    latest = padq[rows:, :].reshape(kernel - 1, ROWS, width)
+    padq[0:rim, :] = jnp.where(
+        half, swap_halves(before).reshape(rim, width), swap_halves(latest).reshape(rim, width)
+    )
+    tail_s[...] = padq[rows:, :]
+    conv = taps[0:1] * padq[0:rows, :]
+    for k in range(1, kernel):
+        conv = conv + taps[k : k + 1] * padq[k * ROWS : k * ROWS + rows, :]
+    conv_o[...] = conv.astype(BF)
+
+    for j in range(hidden // chunk):
+        cols = slice(j * chunk, (j + 1) * chunk)
+        gate = nn(conv_o[...], w_in[:, j * chunk : (j + 1) * chunk]) + bias[0:1, cols]
+        cand = nn(conv_o[...], w_in[:, hidden + j * chunk : hidden + (j + 1) * chunk])
+        eg = jnp.exp(-jnp.abs(gate))
+        rg = pl.reciprocal(1.0 + eg)
+        sg = eg * rg
+        up = gate >= 0
+        write_gate = jnp.where(up, rg, sg)
+        keep_o[:, cols] = jnp.where(up, sg, rg)
+        ec = jnp.exp(-jnp.abs(cand))
+        rc = pl.reciprocal(1.0 + ec)
+        slope = jnp.where(cand >= 0, rc, ec * rc)
+        soft = jnp.maximum(cand, 0.0) + jnp.where(
+            ec < 1e-3, ec * (1.0 - 0.5 * ec), jnp.log(1.0 + ec)
+        )
+        p_o[:, cols] = write_gate
+        q_o[:, cols] = write_gate * slope
+        big[:, cols] = write_gate * soft
+
+    low_half = lax.broadcasted_iota(jnp.int32, (ROWS, hidden), 0) < ROWS // 2
+    carry = carry_s[...]
+    ones = jnp.where(low_half, 0.0, 1.0)
+
+    def scan_one(tau, held):
+        state, reach = held
+        at = pl.ds(pl.multiple_of(tau * ROWS, ROWS), ROWS)
+        keep = keep_o[at, :]
+        state = keep * state + big[at, 0:hidden]
+        reach = keep * reach
+        ds_o[at, :] = state
+        big[at, hidden : 2 * hidden] = reach
+        return state, reach
+
+    end, _ = lax.fori_loop(0, steps, scan_one, (carry, ones), unroll=4)
+    entry = jnp.where(low_half, 0.0, swap_halves(end))
+
+    def fix_one(pair, previous):
+        lows = []
+        for half_step in range(2):
+            at = pl.ds(pl.multiple_of(pair * 2 * ROWS + half_step * ROWS, ROWS), ROWS)
+            state = ds_o[at, :] + big[at, hidden : 2 * hidden] * entry
+            p_o[at, :] = keep_o[at, :] * (big[at, 0:hidden] - p_o[at, :] * previous)
+            previous = state
+            lows.append(state)
+        both = pl.ds(pl.multiple_of(pair * 2 * ROWS, 2 * ROWS), 2 * ROWS)
+        state_low[both, :] = jnp.concatenate(lows, axis=0).astype(BF)
+        return previous
+
+    last = lax.fori_loop(
+        0, steps // 2, fix_one, jnp.where(low_half, carry, entry), unroll=4
+    )
+    carry_s[...] = jnp.where(low_half, swap_halves(last), 0.0)
+
+    mixed = nn(hot, tab_low[...]) + nn(state_low[...], w_out[...])
+    mixed_s[...] = mixed
+    inverse_b = inv_rms(mixed)
+    normed_s[...] = (mixed * inverse_b * gains[1:2]).astype(BF)
+    for j in range(ff // chunk):
+        cols = slice(j * chunk, (j + 1) * chunk)
+        lifted = nn(normed_s[...], w_up[:, cols])
+        square = lifted * lifted
+        curve = jnp.tanh(lifted * (GELU_A + (GELU_A * GELU_B) * square))
+        cdf = 0.5 + 0.5 * curve
+        active[:, cols] = (lifted * cdf).astype(BF)
+        big[:, cols] = cdf + (0.5 * lifted) * (1.0 - curve * curve) * (
+            GELU_A + (3.0 * GELU_A * GELU_B) * square
+        )
+    result = mixed + nn(active[...], w_down[...])
+    inverse_f = inv_rms(result)
+    unit_f = result * inverse_f
+    normed_f = (unit_f * gains[2:3]).astype(BF)
+
+    logits = nt(normed_f, tab_low[...])
+    top = jnp.max(logits, axis=-1, keepdims=True)
+    powers = jnp.exp(logits - top)
+    total = jnp.sum(powers, axis=-1, keepdims=True)
+    lse = jnp.log(total) + top
+    target = columns[:, 1:2] == lax.broadcasted_iota(jnp.int32, (rows, vocab), 1)
+    picked = jnp.sum(jnp.where(target, logits, 0.0), axis=-1, keepdims=True)
+    weight = columns[:, 2:3].astype(F32)
+    loss = column_sum(weight * (lse - picked))
+    share = weight * (1.0 / jnp.sum(count[:, 0:1, 0:1]))
+    d_logits = ((powers * (1.0 / total) - jnp.where(target, 1.0, 0.0)) * share).astype(BF)
+    g_tab[...] += tn(d_logits, normed_f)
+    d_normed_f = nn(d_logits, tab_low[...])
+    small_o[2:3, :] += column_sum(d_normed_f * unit_f)
+    small_o[3:4, :] += jnp.broadcast_to(loss, (1, width))
+    d_final = norm_back(result, inverse_f, gains[2:3], d_normed_f)
+    grad_low = d_final.astype(BF)
+
+    for j in range(ff // chunk):
+        cols = slice(j * chunk, (j + 1) * chunk)
+        d_active = nt(grad_low, w_down[cols, :])
+        g_down[cols, :] += tn(active[:, cols], grad_low)
+        active[:, cols] = (d_active * big[:, cols]).astype(BF)
+    g_up[...] += tn(normed_s[...], active[...])
+    d_normed = nt(active[...], w_up[...])
+    mixed = mixed_s[...]
+    inverse_b = inv_rms(mixed)
+    small_o[1:2, :] += column_sum(d_normed * (mixed * inverse_b))
+    d_mixed = d_final + norm_back(mixed, inverse_b, gains[1:2], d_normed)
+    mixed_low = d_mixed.astype(BF)
+    rest = (d_mixed - mixed_low.astype(F32)).astype(BF)
+    g_out[...] += tn(state_low[...], mixed_low)
+    ds_o[...] = nt(mixed_low, w_out[...])
+    hot_t = one_hot_t(wide_ids[0:1, :], vocab)
+    g_tab[...] += nn(hot_t, mixed_low) + nn(hot_t, rest)
+
+
+def whole(shape):
+    zeros = (0,) * len(shape)
+    return pl.BlockSpec(shape, lambda i: zeros, pipeline_mode=pl.Buffered(1))
+
+
+def run_forward(ids, tab, count, gains, taps, bias, w_in, w_out, w_up, w_down):
+    blocks, _, rows = ids.shape
+    vocab, width = tab.shape
+    hidden = w_out.shape[0]
+    ff = w_up.shape[1]
+    kernel = taps.shape[0]
+    total = blocks * rows
+    rim = (kernel - 1) * ROWS
+    wide = pl.BlockSpec((rows, hidden), lambda i: (i, 0))
+    thin = pl.BlockSpec((rows, width), lambda i: (i, 0))
+    macs = 3 * (width * 2 * hidden // 3 + hidden * width + 2 * width * ff + vocab * width) + 4 * vocab * width
+    return pl.pallas_call(
+        forward_kernel,
+        grid=(blocks,),
+        in_specs=[pl.BlockSpec((1, ROWS, rows), lambda i: (i, 0, 0))]
+        + [whole(a.shape) for a in (tab, count, gains, taps, bias, w_in, w_out, w_up, w_down)],
+        out_specs=[wide, wide, wide, wide, thin, thin]
+        + [whole(s) for s in ((ff, width), (width, ff), (hidden, width), (vocab, width), (ROWS, width))],
+        out_shape=[jax.ShapeDtypeStruct((total, hidden), F32)] * 4
+        + [jax.ShapeDtypeStruct((total, width), BF)] * 2
+        + [
+            jax.ShapeDtypeStruct(s, F32)
+            for s in ((ff, width), (width, ff), (hidden, width), (vocab, width), (ROWS, width))
+        ],
+        scratch_shapes=[
+            pltpu.VMEM((vocab, width), BF),
+            pltpu.VMEM((vocab, width), BF),
+            pltpu.VMEM((rim + rows, width), F32),
+            pltpu.VMEM((rim, width), F32),
+            pltpu.VMEM((ROWS, hidden), F32),
+            pltpu.VMEM((rows, max(ff, 2 * hidden)), F32),
+            pltpu.VMEM((rows, hidden), BF),
+            pltpu.VMEM((rows, ff), BF),
+            pltpu.VMEM((rows, width), F32),
+            pltpu.VMEM((rows, width), BF),
+        ],
+        compiler_params=pltpu.CompilerParams(
+            dimension_semantics=("arbitrary",), vmem_limit_bytes=62 * MIB
+        ),
+        cost_estimate=pl.CostEstimate(
+            flops=2 * macs * total, bytes_accessed=total * hidden * 16, transcendentals=total * (5 * hidden + ff)
+        ),
+        name="forward_and_tail_back",
+    )(ids, tab, count, gains, taps, bias, w_in, w_out, w_up, w_down)
+
+
+def backward_kernel(
+    ids, keep, p, q, ds, conv, queue, tab, gains, taps, w_in, g_tab_in, small_in,
+    g_in, g_tab, small_o,
+    lam_s, reach_s, d_pre, ext, head_s, carry_s, hot_sum,
+):
+    step = pl.program_id(0)
+    rows, hidden = keep.shape
+    vocab, width = tab.shape
+    kernel = taps.shape[0]
+    rim = (kernel - 1) * ROWS
+    steps = rows // ROWS
+    bias_rows = hidden // width
+
+    @pl.when(step == 0)
+    def _():
+        g_in[...] = jnp.zeros_like(g_in)
+        hot_sum[...] = jnp.zeros_like(hot_sum)
+        small_o[...] = jnp.zeros_like(small_o)
+        small_o[0:ROWS, :] = small_in[...]
+        head_s[...] = jnp.zeros_like(head_s)
+        carry_s[...] = jnp.zeros_like(carry_s)
+
+    low_half = lax.broadcasted_iota(jnp.int32, (ROWS, hidden), 0) < ROWS // 2
+
+    def scan_one(i, held):
+        carry, reach = held
+        at = pl.ds(pl.multiple_of((steps - 1 - i) * ROWS, ROWS), ROWS)
+        lam = ds[at, :] + carry
+        lam_s[at, :] = lam
+        reach_s[at, :] = reach
+        k = keep[at, :]
+        return k * lam, k * reach
+
+    first, _ = lax.fori_loop(
+        0, steps, scan_one, (carry_s[...], jnp.where(low_half, 1.0, 0.0)), unroll=4
+    )
+    entry = jnp.where(low_half, swap_halves(first), 0.0)
+    reach0 = keep[0:ROWS, :] * reach_s[0:ROWS, :]
+    carry_s[...] = jnp.where(low_half, 0.0, swap_halves(first + reach0 * entry))
+
+    def fix_one(pair, sums):
+        gates, cands = [], []
+        for half_step in range(2):
+            at = pl.ds(pl.multiple_of(pair * 2 * ROWS + half_step * ROWS, ROWS), ROWS)
+            lam = lam_s[at, :] + reach_s[at, :] * entry
+            d_gate = lam * p[at, :]
+            sums = sums + d_gate
+            gates.append(d_gate)
+            cands.append(lam * q[at, :])
+        both = pl.ds(pl.multiple_of(pair * 2 * ROWS, 2 * ROWS), 2 * ROWS)
+        d_pre[both, 0:hidden] = jnp.concatenate(gates, axis=0).astype(BF)
+        d_pre[both, hidden : 2 * hidden] = jnp.concatenate(cands, axis=0).astype(BF)
+        return sums
+
+    sums = lax.fori_loop(
+        0, steps // 2, fix_one, jnp.zeros((ROWS, hidden), F32), unroll=4
+    )
+    d_bias = column_sum(sums)
+    base = ROWS + kernel
+    for r in range(bias_rows):
+        small_o[base + r : base + r + 1, :] += d_bias[:, r * width : (r + 1) * width]
+
+    g_in[...] += tn(conv[...], d_pre[...])
+    ext[0:rows, :] = nt(d_pre[...], w_in[...])
+    half = lax.broadcasted_iota(jnp.int32, (rim, width), 0) % ROWS < ROWS // 2
+    mine = ext[0:rim, :]
+    ext[rows:, :] = jnp.where(
+        half,
+        swap_halves(mine.reshape(kernel - 1, ROWS, width)).reshape(rim, width),
+        swap_halves(head_s[...].reshape(kernel - 1, ROWS, width)).reshape(rim, width),
+    )
+    head_s[...] = mine
+    known = queue[...].astype(F32)
+    d_queue = None
+    for k in range(kernel):
+        shift = (kernel - 1 - k) * ROWS
+        part = ext[shift : shift + rows, :]
+        term = taps[k : k + 1] * part
+        d_queue = term if d_queue is None else d_queue + term
+        small_o[ROWS + k : ROWS + k + 1, :] += column_sum(part * known)
+    hot_t = one_hot_t(ids[0][0:1, :], vocab)
+    hot_sum[...] += nn(hot_t, d_queue.astype(BF))
+
+    @pl.when(step == pl.num_programs(0) - 1)
+    def _():
+        wide = tab[...].astype(BF).astype(F32)
+        inverse = inv_rms(wide)
+        total = hot_sum[...]
+        small_o[0:1, :] = column_sum(total * (wide * inverse))
+        g_tab[...] = g_tab_in[...] + norm_back(wide, inverse, gains[0:1], total)
+
+
+def run_backward(ids, keep, p, q, ds, conv, queue, tab, gains, taps, w_in, g_tab, small):
+    blocks, _, rows = ids.shape
+    vocab, width = tab.shape
+    hidden = keep.shape[1]
+    kernel = taps.shape[0]
+    total = blocks * rows
+    rim = (kernel - 1) * ROWS
+    last = blocks - 1
+    wide = pl.BlockSpec((rows, hidden), lambda i: (last - i, 0))
+    thin = pl.BlockSpec((rows, width), lambda i: (last - i, 0))
+    out = ((width, 2 * hidden), (vocab, width), (2 * ROWS, width))
+    return pl.pallas_call(
+        backward_kernel,
+        grid=(blocks,),
+        in_specs=[pl.BlockSpec((1, ROWS, rows), lambda i: (last - i, 0, 0)), wide, wide, wide, wide, thin, thin]
+        + [whole(a.shape) for a in (tab, gains, taps, w_in, g_tab, small)],
+        out_specs=[whole(s) for s in out],
+        out_shape=[jax.ShapeDtypeStruct(s, F32) for s in out],
+        scratch_shapes=[
+            pltpu.VMEM((rows, hidden), F32),
+            pltpu.VMEM((rows, hidden), F32),
+            pltpu.VMEM((rows, 2 * hidden), BF),
+            pltpu.VMEM((rim + rows, width), F32),
+            pltpu.VMEM((rim, width), F32),
+            pltpu.VMEM((ROWS, hidden), F32),
+            pltpu.VMEM((vocab, width), F32),
+        ],
+        compiler_params=pltpu.CompilerParams(
+            dimension_semantics=("arbitrary",), vmem_limit_bytes=62 * MIB
+        ),
+        cost_estimate=pl.CostEstimate(
+            flops=2 * total * width * (4 * hidden + vocab), bytes_accessed=total * hidden * 16, transcendentals=0
+        ),
+        name="front_back",
+    )(ids, keep, p, q, ds, conv, queue, tab, gains, taps, w_in, g_tab, small)
+
+
+def place():
+    dp = lax.axis_index("dp")
+    seq = lax.axis_index("seq")
+    return dp // 2, dp % 2, seq // 2, seq % 2
+
+
+def device(y, x, z, core):
+    return (y * 2 + x, z * 2 + core)
+
+
+def greet(y, x, z, core, depth):
+    barrier = pltpu.get_barrier_semaphore()
+    peers = [device(1 - y, x, z, core), device(y, 1 - x, z, core)]
+    for dz in range(depth):
+        for dc in range(2):
+            if dz or dc:
+                peers.append(device(y, x, (z + dz) % depth, (core + dc) % 2))
+    for peer in peers:
+        pl.semaphore_signal(barrier, inc=1, device_id=peer, device_id_type=pl.DeviceIdType.MESH)
+    pl.semaphore_wait(barrier, len(peers))
+
+
+def remote(src, dst, send, recv, peer):
+    return pltpu.make_async_remote_copy(
+        src_ref=src,
+        dst_ref=dst,
+        send_sem=send,
+        recv_sem=recv,
+        device_id=peer,
+        device_id_type=pl.DeviceIdType.MESH,
+    )
+
+
+def in_order(items, phases, act):
+    for time in range(items + phases - 1):
+        for phase in range(phases - 1, -1, -1):
+            item = time - phase
+            if 0 <= item < items:
+                act(item, phase)
+
+
+def gather_kernel(plan, depth, ids, *refs):
+    count = 1 + max(p[0] for p in plan)
+    srcs = refs[:count]
+    ids_o = refs[count]
+    outs = refs[count + 1 : 2 * count + 1]
+    own_sem, ids_send, ids_recv, send, recv = refs[2 * count + 1 :]
+    y, x, z, core = place()
+    me = z * 2 + core
+    greet(y, x, z, core, depth)
+    started = []
+
+    own = [
+        pltpu.make_async_copy(srcs[t], outs[t].at[y, x, z, core], own_sem.at[t])
+        for t in range(count)
+    ]
+    own.append(pltpu.make_async_copy(ids.at[me], ids_o.at[me], own_sem.at[count]))
+    for copy in own:
+        copy.start()
+    spread = []
+    for dz in range(depth):
+        for dc in range(2):
+            if dz or dc:
+                pz, pc = (z + dz) % depth, (core + dc) % 2
+                at = dz * 2 + dc
+                copy = remote(
+                    ids.at[pz * 2 + pc], ids_o.at[me], ids_send.at[at], ids_recv.at[at], device(y, x, pz, pc)
+                )
+                copy.start()
+                spread.append(copy)
+    first = []
+    for i, (t, lo, hi, _) in enumerate(plan):
+        cols = pl.ds(lo, hi - lo)
+        group = []
+        for dz in range(1, depth):
+            copy = remote(
+                srcs[t].at[:, cols],
+                outs[t].at[y, x, z, core, :, cols],
+                send.at[i, dz - 1],
+                recv.at[i, dz - 1],
+                device(y, x, (z + dz) % depth, core),
+            )
+            copy.start()
+            group.append(copy)
+        first.append(group)
+    for copy in own:
+        copy.wait()
+    held = {}
+
+    def act(i, phase):
+        t, lo, hi, along_x = plan[i]
+        cols = pl.ds(lo, hi - lo)
+        out = outs[t]
+        if phase == 0:
+            for copy in first[i]:
+                copy.wait_recv()
+            started.extend(first[i])
+            if along_x:
+                part, peer = out.at[y, x, :, core, :, cols], device(y, 1 - x, z, core)
+            else:
+                part, peer = out.at[y, x, :, core, :, cols], device(1 - y, x, z, core)
+        else:
+            held[i].wait_recv()
+            started.append(held[i])
+            if phase == 1:
+                if along_x:
+                    part, peer = out.at[y, :, :, core, :, cols], device(1 - y, x, z, core)
+                else:
+                    part, peer = out.at[:, x, :, core, :, cols], device(y, 1 - x, z, core)
+            elif phase == 2:
+                part, peer = out.at[:, :, :, core, :, cols], device(y, x, z, 1 - core)
+            else:
+                return
+        at = depth - 1 + phase
+        held[i] = remote(part, part, send.at[i, at], recv.at[i, at], peer)
+        held[i].start()
+
+    in_order(len(plan), 4, act)
+    for copy in spread:
+        copy.wait_recv()
+    for copy in spread + started:
+        copy.wait_send()
+
+
+def run_gather(depth, ids, tensors):
+    plan = []
+    for t, a in enumerate(tensors):
+        cols = a.shape[1]
+        if a.dtype == F32:
+            plan.append((t, 0, cols, True))
+        else:
+            plan.append((t, 0, cols // 2, True))
+            plan.append((t, cols // 2, cols, False))
+    any_spec = pl.BlockSpec(memory_space=pl.ANY)
+    n = len(tensors)
+    return pl.pallas_call(
+        functools.partial(gather_kernel, plan, depth),
+        in_specs=[any_spec] * (n + 1),
+        out_specs=[any_spec] * (n + 1),
+        out_shape=[jax.ShapeDtypeStruct(ids.shape, ids.dtype)]
+        + [jax.ShapeDtypeStruct((2, 2, depth, 2) + a.shape, a.dtype) for a in tensors],
+        scratch_shapes=[
+            pltpu.SemaphoreType.DMA((n + 1,)),
+            pltpu.SemaphoreType.DMA((2 * depth,)),
+            pltpu.SemaphoreType.DMA((2 * depth,)),
+            pltpu.SemaphoreType.DMA((len(plan), depth + 2)),
+            pltpu.SemaphoreType.DMA((len(plan), depth + 2)),
+        ],
+        compiler_params=pltpu.CompilerParams(collective_id=0, has_side_effects=True),
+        name="gather_weights",
+    )(ids, *tensors)
+
+
+def add_into(target, other, rank):
+    lead = target.shape[: len(target.shape) - 2]
+    total = 1
+    for d in lead:
+        total *= d
+
+    def one(i, _):
+        index = []
+        for d in reversed(lead):
+            index.append(lax.rem(i, d))
+            i = lax.div(i, d)
+        index = tuple(reversed(index))
+        target[index] = target[index] + other[index]
+        return _
+
+    lax.fori_loop(0, total, one, 0)
+
+
+def reduce_kernel(plan, depth, tensors, *refs):
+    n = len(tensors)
+    items = len(plan)
+    grads = refs[:n]
+    small = refs[n]
+    outs = refs[n + 1 : 2 * n + 1]
+    small_o, norm_o = refs[2 * n + 1 : 2 * n + 3]
+    scratch = refs[2 * n + 3 :]
+    sizes = 4
+    bufs = [scratch[i * sizes : (i + 1) * sizes] for i in range(items)]
+    rest = scratch[items * sizes :]
+    small_r, square_s, square_r = rest[0:3]
+    own_sem, send, recv, small_send, small_recv, sq_send, sq_recv = rest[3:]
+    y, x, z, core = place()
+    greet(y, x, z, core, depth)
+    started = []
+    peer_of = {
+        "core": device(y, x, z, 1 - core),
+        "x": device(y, 1 - x, z, core),
+        "y": device(1 - y, x, z, core),
+    }
+
+    loads, held = [], {}
+    for i, (t, lo, hi, _) in enumerate(plan):
+        cols = pl.ds(lo, hi - lo)
+        copy = remote(
+            grads[t].at[:, :, :, 1 - core, :, cols], bufs[i][1], send.at[i, 0], recv.at[i, 0], peer_of["core"]
+        )
+        copy.start()
+        held[i] = [copy]
+        load = pltpu.make_async_copy(grads[t].at[:, :, :, core, :, cols], bufs[i][0], own_sem.at[i])
+        load.start()
+        loads.append(load)
+
+    def act(i, phase):
+        t, lo, hi, along_x = plan[i]
+        whole_b, core_b, half_b, quarter_b = bufs[i]
+        for copy in held[i]:
+            copy.wait_recv()
+        started.extend(held[i])
+        if phase == 0:
+            loads[i].wait()
+            add_into(whole_b, core_b, 3)
+            if along_x:
+                src, peer = whole_b.at[1 - y], peer_of["y"]
+            else:
+                src, peer = whole_b.at[:, 1 - x], peer_of["x"]
+            held[i] = [remote(src, half_b, send.at[i, 1], recv.at[i, 1], peer)]
+        elif phase == 1:
+            if along_x:
+                add_into(half_b, whole_b.at[y], 2)
+                src, peer = half_b.at[1 - x], peer_of["x"]
+            else:
+                add_into(half_b, whole_b.at[:, x], 2)
+                src, peer = half_b.at[1 - y], peer_of["y"]
+            held[i] = [remote(src, quarter_b.at[0], send.at[i, 2], recv.at[i, 2], peer)]
+        elif phase == 2:
+            mine = half_b.at[x] if along_x else half_b.at[y]
+            add_into(quarter_b.at[0], mine, 1)
+            held[i] = []
+            for dz in range(1, depth):
+                pz = (z + dz) % depth
+                held[i].append(
+                    remote(
+                        quarter_b.at[0, pz],
+                        quarter_b.at[1, dz],
+                        send.at[i, 2 + dz],
+                        recv.at[i, 2 + dz],
+                        device(y, x, pz, core),
+                    )
+                )
+        else:
+            total = quarter_b[0, z]
+            for dz in range(1, depth):
+                total = total + quarter_b[1, dz]
+            outs[t][:, lo:hi] = total
+            return
+        for copy in held[i]:
+            copy.start()
+
+    def everywhere(value, slots, sends, recvs):
+        slots[0] = value
+        for at, name in enumerate(("core", "x", "y")):
+            copy = remote(slots.at[2 * at], slots.at[2 * at + 1], sends.at[at], recvs.at[at], peer_of[name])
+            copy.start()
+            copy.wait()
+            slots[2 * at + 2] = slots[2 * at] + slots[2 * at + 1]
+        copies = []
+        for dz in range(1, depth):
+            copy = remote(
+                slots.at[6],
+                slots.at[7 + z],
+                sends.at[2 + dz],
+                recvs.at[2 + dz],
+                device(y, x, (z + dz) % depth, core),
+            )
+            copy.start()
+            copies.append(copy)
+        slots[7 + z] = slots[6]
+        for copy in copies:
+            copy.wait()
+        total = slots[7]
+        for dz in range(1, depth):
+            total = total + slots[7 + dz]
+        return total
+
+    in_order(items, 4, act)
+    sums = everywhere(small[...], small_r, small_send, small_recv)
+    small_o[...] = sums
+    square = jnp.zeros((1, 1), F32)
+    for out in outs:
+        value = out[...]
+        square = square + jnp.sum(jnp.sum(value * value, axis=1, keepdims=True), axis=0, keepdims=True)
+    squares = everywhere(jnp.broadcast_to(square, (ROWS, LANES)), square_r, sq_send, sq_recv)
+    norm_o[...] = squares
+    for copy in started:
+        copy.wait_send()
+
+
+def run_reduce(depth, tensors, small):
+    plan = []
+    for t, a in enumerate(tensors):
+        cols = a.shape[-1]
+        plan.append((t, 0, cols // 2, True))
+        plan.append((t, cols // 2, cols, False))
+    shapes = tuple(a.shape for a in tensors)
+    scratch = []
+    for t, lo, hi, along_x in plan:
+        rows = shapes[t][-2]
+        piece = (rows, hi - lo)
+        scratch.append(pltpu.VMEM((2, 2, depth) + piece, F32))
+        scratch.append(pltpu.VMEM((2, 2, depth) + piece, F32))
+        scratch.append(pltpu.VMEM((2, depth) + piece, F32))
+        scratch.append(pltpu.VMEM((2, depth) + piece, F32))
+    any_spec = pl.BlockSpec(memory_space=pl.ANY)
+    vmem = pl.BlockSpec(memory_space=pltpu.VMEM)
+    n = len(tensors)
+    return pl.pallas_call(
+        functools.partial(reduce_kernel, plan, depth, shapes),
+        in_specs=[any_spec] * n + [vmem],
+        out_specs=[vmem] * (n + 2),
+        out_shape=[jax.ShapeDtypeStruct(s[-2:], F32) for s in shapes]
+        + [jax.ShapeDtypeStruct(small.shape, F32), jax.ShapeDtypeStruct((ROWS, LANES), F32)],
+        scratch_shapes=scratch
+        + [
+            pltpu.VMEM((7 + depth,) + small.shape, F32),
+            pltpu.VMEM((ROWS, LANES), F32),
+            pltpu.VMEM((7 + depth, ROWS, LANES), F32),
+            pltpu.SemaphoreType.DMA((len(plan),)),
+            pltpu.SemaphoreType.DMA((len(plan), depth + 2)),
+            pltpu.SemaphoreType.DMA((len(plan), depth + 2)),
+            pltpu.SemaphoreType.DMA((depth + 2,)),
+            pltpu.SemaphoreType.DMA((depth + 2,)),
+            pltpu.SemaphoreType.DMA((depth + 2,)),
+            pltpu.SemaphoreType.DMA((depth + 2,)),
+        ],
+        compiler_params=pltpu.CompilerParams(
+            collective_id=1, has_side_effects=True, vmem_limit_bytes=60 * MIB
+        ),
+        name="reduce_grads",
+    )(*tensors, small)
+
+
+def adam_kernel(shapes, small, squares, count, *refs):
+    mats = refs[:5]
+    weights, firsts, seconds = refs[5:13], refs[13:21], refs[21:29]
+    loss_o, count_o, norm_o = refs[29:32]
+    new_w, new_m, new_v = refs[32:40], refs[40:48], refs[48:56]
+    kernel, bias_rows = shapes
+    width = small.shape[1]
+    grads = [m[...] for m in mats]
+    grads.append(small[0:3, :])
+    grads.append(small[ROWS : ROWS + kernel, :])
+    base = ROWS + kernel
+    grads.append(
+        jnp.concatenate([small[base + r : base + r + 1, :] for r in range(bias_rows)], axis=1)
+    )
+    square = squares[0:1, 0:1]
+    for grad in grads[5:]:
+        square = square + jnp.sum(jnp.sum(grad * grad, axis=1, keepdims=True), axis=0, keepdims=True)
+    norm = jnp.sqrt(square)
+    scale = jnp.minimum(1.0, CLIP / (norm + 1e-06))
+    norm_o[...] = norm
+    loss_o[...] = small[3:4, 0:1]
+    count_o[...] = jnp.sum(count[:, 0:1, 0:1], axis=0)
+    for i in range(8):
+        rate = RATE_MATRIX if i < 5 else RATE_VECTOR
+        decay = WEIGHT_DECAY if i < 5 else 0.0
+        w, m, v = adam(weights[i][...], grads[i] * scale, firsts[i][...], seconds[i][...], rate, decay)
+        new_w[i][...] = w
+        new_m[i][...] = m
+        new_v[i][...] = v
+
+
+def run_adam(shapes, mats, small, squares, count, weights, firsts, seconds):
+    one = jax.ShapeDtypeStruct((1, 1), F32)
+    like = [jax.ShapeDtypeStruct(w.shape, F32) for w in weights]
+    vmem = pl.BlockSpec(memory_space=pltpu.VMEM)
+    args = (small, squares, count) + tuple(mats) + tuple(weights) + tuple(firsts) + tuple(seconds)
+    return pl.pallas_call(
+        functools.partial(adam_kernel, shapes),
+        in_specs=[vmem] * len(args),
+        out_specs=[vmem] * 27,
+        out_shape=[one] * 3 + like * 3,
+        compiler_params=pltpu.CompilerParams(vmem_limit_bytes=40 * MIB),
+        name="adam_update",
+    )(*args)
+
+
+def spread_ids(tokens, targets, counted, depth):
+    seqs, span = tokens.shape
+    ways = 2 * depth
+
+    def one(a):
+        parts = a.reshape(ways, seqs // ways, 2, span // 2)
+        return parts.transpose(0, 3, 2, 1).reshape(ways, 1, -1)
+
+    rows = [one(tokens), one(targets), one(counted)]
+    fill = jnp.zeros((ways, ROWS - 3, rows[0].shape[-1]), jnp.int32)
+    return jnp.concatenate(rows + [fill], axis=1)
+
+
+def body_moved(depth, *args):
+    tokens, targets, counted = args[:3]
+    weights, firsts, seconds = args[3:11], args[11:19], args[19:27]
+    table, w_in, w_out, w_up, w_down, gains, conv_taps, gate_bias = weights
+    ids = spread_ids(tokens, targets, counted, depth)
+    share = jnp.sum(counted.astype(F32))
+    first = jnp.concatenate([table, jnp.broadcast_to(share, (table.shape[0], LANES))], axis=1)
+    mats = [w[0].astype(BF) for w in (w_in, w_out, w_up, w_down)]
+    got = run_gather(depth, ids, [first, mats[0], mats[1], mats[2], mats[3]])
+    ids = got[0]
+    width = table.shape[1]
+    tab = got[1][..., :width].reshape(-1, width)
+    count = got[1][..., width:].reshape(-1, table.shape[0], LANES)
+    full = [g.reshape(-1, g.shape[-1]) for g in got[2:]]
+    taps = conv_taps[0]
+    keep, p, q, ds, conv, queue, g_down, g_up, g_out, g_tab, small = run_forward(
+        ids, tab, count, gains, taps, gate_bias, *full
+    )
+    g_in, g_tab, small = run_backward(ids, keep, p, q, ds, conv, queue, tab, gains, taps, full[0], g_tab, small)
+    whole_grads = [
+        g.reshape((2, 2, depth, 2, -1, g.shape[-1])) for g in (g_tab, g_in, g_out, g_up, g_down)
+    ]
+    *mats, small, squares = run_reduce(depth, whole_grads, small)
+    flat = lambda group: [group[0]] + [a[0] for a in group[1:5]] + [group[5], group[6][0], group[7]]
+    out = run_adam(
+        (conv_taps.shape[1], gate_bias.shape[1] // width),
+        mats, small, squares, count, flat(weights), flat(firsts), flat(seconds),
+    )
+    shaped = [o.reshape(()) for o in out[:3]]
+    for i, o in enumerate(out[3:]):
+        shaped.append(o.reshape(weights[i % 8].shape))
+    return tuple(shaped)
+
+
+def choose(mesh, *args):
+    ways = mesh.shape["seq"]
+    seqs, span = args[0].shape
+    if mesh.shape["dp"] == 4 and ways == 8 and seqs == 4 * ways and span == LANES:
+        return body_moved(ways // 2, *args)
+    return body(*args)
+
+
 def solution(mesh):
     return jax.shard_map(
-        body,
+        functools.partial(choose, mesh),
         mesh=mesh,
         in_specs=(
             P("dp", "seq"),

time: 3650 us -> 438 us (0.12); the launches traced: 3580 us -> 437 us
  local copies, waits for them, and re-layouts: 1910 us -> 14.6 us
  waiting for transfers between devices: 619 us -> 0 us
  other arithmetic: 549 us -> 6.7 us
  Pallas kernels: 0 us -> 414 us
  blocking collectives: 240 us -> 0 us
  matrix products: 229 us -> 0 us
    slice x198 -> x2, local copies, waits for them, and re-layouts: 934 us -> 3.43 us  [the longest x1 1.87 us: body_moved(): tab = got[1][..., :width].reshape(-1, width)]
    reduce_scatter x5 -> x0, waiting for transfers between devices: 619 us -> none  [the longest x1 140 us: backward_step(): lax.psum_scatter(full[3], ('dp', 'seq'), scatter_dimension=0, tiled=True)]
    pad x96 -> x0, local copies, waits for them, and re-layouts: 615 us -> none  [the longest x48 314 us: layer_backward(): lax.associative_scan(combine, (follow, d_state), axis=0, reverse=True)]
    pallas_call x0 -> x5, Pallas kernels: none -> 414 us  [the longest x1 150 us: run_reduce(): pl.pallas_call(functools.partial(reduce_kernel, plan, depth, shapes), in_...]
    add x101 -> x0, other arithmetic: 261 us -> none  [the longest x28 91.3 us: layer_backward(): lax.associative_scan(combine, (follow, d_state), axis=0, reverse=True)]
    rev x4 -> x0, local copies, waits for them, and re-layouts: 257 us -> none  [layer_backward(): lax.associative_scan(combine, (follow, d_state), axis=0, reverse=True)]
    dot_general x34 -> x0, matrix products: 229 us -> none  [the longest x10 81 us: matmul_nt(): lax.dot_general(left, right, (((1,), (1,)), ((), ())), preferred_element_...]
    all_gather x9 -> x0, blocking collectives: 165 us -> none  [the longest x8 121 us: carried_in(): gathered = jax.tree.map(lambda a: lax.all_gather(a, axis), part)]
  transfers between devices with their start and end apart: 13 -> 0, of which waited for: 5 -> 0; matrix products, arithmetic and copies ran while one was open for 39% -> 0% of each run, Pallas kernels for 0% -> 0%
where the time goes in v1:
time: 438 us; the launch traced here: 437 us
  Pallas kernels  414 us (95%)
  local copies, waits for them, and re-layouts  14.6 us (3%)
  other arithmetic  6.7 us (2%)
    pallas_call x1, Pallas kernels, run_reduce(): pl.pallas_call(functools.partial(reduce_kernel, plan, depth, shapes), in_...  150 us
    pallas_call x1, Pallas kernels, run_forward(): pl.pallas_call(forward_kernel, grid=(blocks,), in_specs=[pl.BlockSpec((1,...  139 us
    pallas_call x1, Pallas kernels, run_gather(): pl.pallas_call(functools.partial(gather_kernel, plan, depth), in_specs=[a...  82.5 us
    pallas_call x1, Pallas kernels, run_backward(): pl.pallas_call(backward_kernel, grid=(blocks,), in_specs=[pl.BlockSpec((1...  41.3 us

profile of v1, /device:TPU:0, one launch (start us, length us, event | category | flops | bytes accessed | tf_op | source)
XLA Modules:
  0.0 436.7 jit_solution(18316036801738958516)
XLA Ops:
  0.7 1.3 convert_reduce_fusion
  2.0 0.1 pad.4.clone
  2.1 2.0 concatenate.7.refs_0_
  4.0 0.8 reshape.159
  4.8 0.8 reshape.161
  5.7 0.8 reshape.163
  6.5 1.5 bitcast_convert_fusion.2.refs_2_
  7.9 1.5 bitcast_convert_fusion.refs_4_
  9.5 1.6 bitcast_convert_fusion.1
  11.1 0.2 copy.59
  11.3 0.1 copy.62
  11.4 0.2 copy.58
  11.6 0.1 copy.61
  11.7 0.2 copy.57
  11.9 0.1 copy.60
  11.9 0.7 add_add_fusion.ids
  12.7 82.5 %gather_weights.1 = (s32[8,8,512]{2,1,0:T(8,128)}, f32[2,2,4,2,8,640]{5,4,3,2,1,0:T(8,128)}, bf16[2,2,4,2,16,2048]{5,4,3,2,1,0:T(8,128)(2,1)}, bf16[2,2,4,2,32,5...) custom-call(s32[8,8,512]{2,1,0:T(8,128)} %add_add_fusion.ids, ...), custom_call_target="tpu_custom_call" | custom-call | tf_op jit(solution)/shard_map/gather_weights/pallas_call | solution.py:881
  95.2 1.6 slice.7
  96.8 1.9 slice.6
  98.6 138.7 %forward_and_tail_back.1 = (f32[4096,1024]{1,0:T(8,128)}, f32[4096,1024]{1,0:T(8,128)}, f32[4096,1024]{1,0:T(8,128)}, f32[4096,1024]{1,0:T(8,128)}, bf16[4096,51...) custom-call(s32[8,8,512]{2,1,0:T(8,128)} %get-tuple-element.81.ids, ...), custom_call_target="tpu_custom_call" | custom-call | flops 80530628608 | bytes 67108864 | tf_op jit(solution)/shard_map/forward_and_tail_back/pallas_call | solution.py:582
  237.4 41.3 %front_back.1 = (f32[512,2048]{1,0:T(8,128)}, f32[256,512]{1,0:T(8,128)}, f32[16,512]{1,0:T(8,128)}) custom-call(s32[8,8,512]{2,1,0:T(8,128)} %get-tuple-element.81.ids, f32[4096,1024]{1,0:T(8,128)} %get-tuple-element.87.keep, f32[4096,1024]{1,0:T(8,128)} %get-tuple-element.88.p, f32[4096,1024]{1,0:T(8,128)} %get-tuple-element.89.q, ...), custom_call_target="tpu_custom_call" | custom-call | flops 18253611008 | bytes 67108864 | tf_op jit(solution)/shard_map/front_back/pallas_call | solution.py:720
  278.7 0.0 copy-start
  278.7 0.0 copy-start.1
  278.7 0.0 copy-start.2
  278.7 0.0 copy-start.3
  278.7 0.0 copy-start.4
  278.7 0.0 copy-start.5
  278.7 0.0 copy-start.6
  278.8 0.0 copy-start.7
  278.8 0.0 copy-start.8
  278.8 0.0 copy-start.9
  278.8 0.0 copy-start.10
  278.8 0.0 copy-start.14
  278.8 0.0 copy-start.15
  278.8 0.0 copy-start.16
  278.8 0.0 copy-start.19
  278.9 0.0 copy-start.20
  278.9 0.0 copy-start.21
  278.9 0.0 copy-start.22
  278.9 0.0 copy-start.24
  278.9 0.0 copy-start.25
  278.9 0.0 copy-start.26
  278.9 0.0 copy-start.27
  278.9 0.0 copy-start.28
  279.0 0.0 copy-start.29
  279.0 0.0 copy-start.30
  279.0 150.2 %reduce_grads.1 = (f32[8,512]{1,0:T(8,128)}, f32[16,2048]{1,0:T(8,128)}, f32[32,512]{1,0:T(8,128)}, f32[16,2048]{1,0:T(8,128)}, f32[64,512]{1,0:T(8,128)}, /*index=5*/f32[16,512]{1,0:T(8,128)}, f32[8,128]{1,0:T(8,128)}) custom-call(f32[2,2,4,2,8,512]{5,4,3,2,1,0:T(8,128)} %bitcast.87, f32[2,2,4,2,16,2048]{5,4,3,2,1,0:T(8,128)} %bitcast.78, ...), custom_call_target="tpu_custom_call" | custom-call | tf_op jit(solution)/shard_map/reduce_grads/pallas_call | solution.py:1054
  429.2 0.0 copy-done
  429.2 0.0 copy-done.1
  429.2 0.0 copy-done.2
  429.2 0.0 copy-done.3
  429.2 0.0 copy-done.4
  429.2 0.0 copy-done.5
  429.2 0.0 copy-done.6
  429.3 0.0 copy-done.7
  429.3 0.0 copy-done.8
  429.4 0.9 copy-done.11
  430.3 0.9 copy-done.12
  431.2 0.9 copy-done.13
  432.2 0.8 copy-done.17
  433.0 0.8 copy-done.18
  433.8 0.7 copy-done.23
  434.5 0.7 copy-done.31
  435.2 1.4 adam_update.1
  (24 shorter events, 0.0 us)
Async XLA Ops:
  278.7 150.5 %copy-start = (f32[1,16,2048]{2,1,0:T(8,128)S(1)}, f32[1,16,2048]{2,1,0:T(8,128)}, u32[]{:S(2)}) copy-start(f32[1,16,2048]{2,1,0:T(8,128)} %param.33) | copy-start | bytes 393220
  278.7 150.5 %copy-start.1 = (f32[1,16,2048]{2,1,0:T(8,128)S(1)}, f32[1,16,2048]{2,1,0:T(8,128)}, u32[]{:S(2)}) copy-start(f32[1,16,2048]{2,1,0:T(8,128)} %param.31) | copy-start | bytes 393220
  278.7 150.5 %copy-start.2 = (f32[1,64,512]{2,1,0:T(8,128)S(1)}, f32[1,64,512]{2,1,0:T(8,128)}, u32[]{:S(2)}) copy-start(f32[1,64,512]{2,1,0:T(8,128)} %param.34) | copy-start | bytes 393220
  278.7 150.5 %copy-start.3 = (f32[2,2,4,2,8,128]{5,4,3,2,1,0:T(8,128)S(1)}, f32[2,2,4,2,8,128]{5,4,3,2,1,0:T(8,128)}, u32[]{:S(2)}) copy-start(f32[2,2,4,2,8,128]{5,4,3,2,1,0:T(8,128)} %slice.7) | copy-start | bytes 393220
  278.7 150.5 %copy-start.4 = (f32[1,32,512]{2,1,0:T(8,128)S(1)}, f32[1,32,512]{2,1,0:T(8,128)}, u32[]{:S(2)}) copy-start(f32[1,32,512]{2,1,0:T(8,128)} %param.32) | copy-start | bytes 196612
  278.7 150.5 %copy-start.5 = (f32[1,16,2048]{2,1,0:T(8,128)S(1)}, f32[1,16,2048]{2,1,0:T(8,128)}, u32[]{:S(2)}) copy-start(f32[1,16,2048]{2,1,0:T(8,128)} %param.39) | copy-start | bytes 393220
  278.7 150.5 %copy-start.6 = (f32[1,16,2048]{2,1,0:T(8,128)S(1)}, f32[1,16,2048]{2,1,0:T(8,128)}, u32[]{:S(2)}) copy-start(f32[1,16,2048]{2,1,0:T(8,128)} %param.41) | copy-start | bytes 393220
  278.8 150.5 %copy-start.7 = (f32[1,64,512]{2,1,0:T(8,128)S(1)}, f32[1,64,512]{2,1,0:T(8,128)}, u32[]{:S(2)}) copy-start(f32[1,64,512]{2,1,0:T(8,128)} %param.42) | copy-start | bytes 393220
  278.8 150.5 %copy-start.8 = (f32[1,16,2048]{2,1,0:T(8,128)S(1)}, f32[1,16,2048]{2,1,0:T(8,128)}, u32[]{:S(2)}) copy-start(f32[1,16,2048]{2,1,0:T(8,128)} %param.47) | copy-start | bytes 393220
  278.8 150.5 %copy-start.9 = (f32[1,16,2048]{2,1,0:T(8,128)S(1)}, f32[1,16,2048]{2,1,0:T(8,128)}, u32[]{:S(2)}) copy-start(f32[1,16,2048]{2,1,0:T(8,128)} %param.49) | copy-start | bytes 393220
  278.8 150.5 %copy-start.10 = (f32[1,64,512]{2,1,0:T(8,128)S(1)}, f32[1,64,512]{2,1,0:T(8,128)}, u32[]{:S(2)}) copy-start(f32[1,64,512]{2,1,0:T(8,128)} %param.50) | copy-start | bytes 393220
  278.8 150.5 %copy-start.14 = (f32[8,512]{1,0:T(8,128)S(1)}, f32[8,512]{1,0:T(8,128)}, u32[]{:S(2)}) copy-start(f32[8,512]{1,0:T(8,128)} %refs_5_.1) | copy-start | bytes 49156
  278.8 150.5 %copy-start.15 = (f32[1,32,512]{2,1,0:T(8,128)S(1)}, f32[1,32,512]{2,1,0:T(8,128)}, u32[]{:S(2)}) copy-start(f32[1,32,512]{2,1,0:T(8,128)} %param.40) | copy-start | bytes 196612
  278.8 150.5 %copy-start.16 = (f32[1,32,512]{2,1,0:T(8,128)S(1)}, f32[1,32,512]{2,1,0:T(8,128)}, u32[]{:S(2)}) copy-start(f32[1,32,512]{2,1,0:T(8,128)} %param.48) | copy-start | bytes 196612
  278.8 150.5 %copy-start.19 = (f32[3,512]{1,0:T(4,128)S(1)}, f32[3,512]{1,0:T(4,128)}, u32[]{:S(2)}) copy-start(f32[3,512]{1,0:T(4,128)} %refs_10_.1) | copy-start | bytes 18436
  278.9 150.5 %copy-start.20 = (f32[1,4,512]{2,1,0:T(4,128)S(1)}, f32[1,4,512]{2,1,0:T(4,128)}, u32[]{:S(2)}) copy-start(f32[1,4,512]{2,1,0:T(4,128)} %param.36) | copy-start | bytes 24580
  278.9 150.5 %copy-start.21 = (f32[8,512]{1,0:T(8,128)S(1)}, f32[8,512]{1,0:T(8,128)}, u32[]{:S(2)}) copy-start(f32[8,512]{1,0:T(8,128)} %refs_13_.1) | copy-start | bytes 49156
  278.9 150.5 %copy-start.22 = (f32[8,512]{1,0:T(8,128)S(1)}, f32[8,512]{1,0:T(8,128)}, u32[]{:S(2)}) copy-start(f32[8,512]{1,0:T(8,128)} %refs_21_.1) | copy-start | bytes 49156
  278.9 150.5 %copy-start.24 = (f32[3,512]{1,0:T(4,128)S(1)}, f32[3,512]{1,0:T(4,128)}, u32[]{:S(2)}) copy-start(f32[3,512]{1,0:T(4,128)} %refs_18_.1) | copy-start | bytes 18436
  278.9 150.5 %copy-start.25 = (f32[1,4,512]{2,1,0:T(4,128)S(1)}, f32[1,4,512]{2,1,0:T(4,128)}, u32[]{:S(2)}) copy-start(f32[1,4,512]{2,1,0:T(4,128)} %param.44) | copy-start | bytes 24580
  278.9 150.5 %copy-start.26 = (f32[3,512]{1,0:T(4,128)S(1)}, f32[3,512]{1,0:T(4,128)}, u32[]{:S(2)}) copy-start(f32[3,512]{1,0:T(4,128)} %refs_26_.1) | copy-start | bytes 18436
  278.9 150.5 %copy-start.27 = (f32[1,4,512]{2,1,0:T(4,128)S(1)}, f32[1,4,512]{2,1,0:T(4,128)}, u32[]{:S(2)}) copy-start(f32[1,4,512]{2,1,0:T(4,128)} %param.52) | copy-start | bytes 24580
  278.9 150.5 %copy-start.28 = (f32[1,1024]{1,0:T(1,128)S(1)}, f32[1,1024]{1,0:T(1,128)}, u32[]{:S(2)}) copy-start(f32[1,1024]{1,0:T(1,128)} %refs_12_.1) | copy-start | bytes 12292
  279.0 150.5 %copy-start.29 = (f32[1,1024]{1,0:T(1,128)S(1)}, f32[1,1024]{1,0:T(1,128)}, u32[]{:S(2)}) copy-start(f32[1,1024]{1,0:T(1,128)} %refs_20_.1) | copy-start | bytes 12292
  279.0 150.5 %copy-start.30 = (f32[1,1024]{1,0:T(1,128)S(1)}, f32[1,1024]{1,0:T(1,128)}, u32[]{:S(2)}) copy-start(f32[1,1024]{1,0:T(1,128)} %refs_28_.1) | copy-start | bytes 12292
  429.4 0.9 copy-start.11
  430.3 0.9 copy-start.12
  431.2 0.9 copy-start.13
  432.2 0.8 copy-start.17
  433.0 0.8 copy-start.18
  433.8 0.7 copy-start.23
  434.5 0.7 copy-start.31

commit v2 on v1

--- a/solution.py
+++ b/solution.py
@@ -614,135 +614,6 @@
     )(ids, tab, count, gains, taps, bias, w_in, w_out, w_up, w_down)
 
 
-def backward_kernel(
-    ids, keep, p, q, ds, conv, queue, tab, gains, taps, w_in, g_tab_in, small_in,
-    g_in, g_tab, small_o,
-    lam_s, reach_s, d_pre, ext, head_s, carry_s, hot_sum,
-):
-    step = pl.program_id(0)
-    rows, hidden = keep.shape
-    vocab, width = tab.shape
-    kernel = taps.shape[0]
-    rim = (kernel - 1) * ROWS
-    steps = rows // ROWS
-    bias_rows = hidden // width
-
-    @pl.when(step == 0)
-    def _():
-        g_in[...] = jnp.zeros_like(g_in)
-        hot_sum[...] = jnp.zeros_like(hot_sum)
-        small_o[...] = jnp.zeros_like(small_o)
-        small_o[0:ROWS, :] = small_in[...]
-        head_s[...] = jnp.zeros_like(head_s)
-        carry_s[...] = jnp.zeros_like(carry_s)
-
-    low_half = lax.broadcasted_iota(jnp.int32, (ROWS, hidden), 0) < ROWS // 2
-
-    def scan_one(i, held):
-        carry, reach = held
-        at = pl.ds(pl.multiple_of((steps - 1 - i) * ROWS, ROWS), ROWS)
-        lam = ds[at, :] + carry
-        lam_s[at, :] = lam
-        reach_s[at, :] = reach
-        k = keep[at, :]
-        return k * lam, k * reach
-
-    first, _ = lax.fori_loop(
-        0, steps, scan_one, (carry_s[...], jnp.where(low_half, 1.0, 0.0)), unroll=4
-    )
-    entry = jnp.where(low_half, swap_halves(first), 0.0)
-    reach0 = keep[0:ROWS, :] * reach_s[0:ROWS, :]
-    carry_s[...] = jnp.where(low_half, 0.0, swap_halves(first + reach0 * entry))
-
-    def fix_one(pair, sums):
-        gates, cands = [], []
-        for half_step in range(2):
-            at = pl.ds(pl.multiple_of(pair * 2 * ROWS + half_step * ROWS, ROWS), ROWS)
-            lam = lam_s[at, :] + reach_s[at, :] * entry
-            d_gate = lam * p[at, :]
-            sums = sums + d_gate
-            gates.append(d_gate)
-            cands.append(lam * q[at, :])
-        both = pl.ds(pl.multiple_of(pair * 2 * ROWS, 2 * ROWS), 2 * ROWS)
-        d_pre[both, 0:hidden] = jnp.concatenate(gates, axis=0).astype(BF)
-        d_pre[both, hidden : 2 * hidden] = jnp.concatenate(cands, axis=0).astype(BF)
-        return sums
-
-    sums = lax.fori_loop(
-        0, steps // 2, fix_one, jnp.zeros((ROWS, hidden), F32), unroll=4
-    )
-    d_bias = column_sum(sums)
-    base = ROWS + kernel
-    for r in range(bias_rows):
-        small_o[base + r : base + r + 1, :] += d_bias[:, r * width : (r + 1) * width]
-
-    g_in[...] += tn(conv[...], d_pre[...])
-    ext[0:rows, :] = nt(d_pre[...], w_in[...])
-    half = lax.broadcasted_iota(jnp.int32, (rim, width), 0) % ROWS < ROWS // 2
-    mine = ext[0:rim, :]
-    ext[rows:, :] = jnp.where(
-        half,
-        swap_halves(mine.reshape(kernel - 1, ROWS, width)).reshape(rim, width),
-        swap_halves(head_s[...].reshape(kernel - 1, ROWS, width)).reshape(rim, width),
-    )
-    head_s[...] = mine
-    known = queue[...].astype(F32)
-    d_queue = None
-    for k in range(kernel):
-        shift = (kernel - 1 - k) * ROWS
-        part = ext[shift : shift + rows, :]
-        term = taps[k : k + 1] * part
-        d_queue = term if d_queue is None else d_queue + term
-        small_o[ROWS + k : ROWS + k + 1, :] += column_sum(part * known)
-    hot_t = one_hot_t(ids[0][0:1, :], vocab)
-    hot_sum[...] += nn(hot_t, d_queue.astype(BF))
-
-    @pl.when(step == pl.num_programs(0) - 1)
-    def _():
-        wide = tab[...].astype(BF).astype(F32)
-        inverse = inv_rms(wide)
-        total = hot_sum[...]
-        small_o[0:1, :] = column_sum(total * (wide * inverse))
-        g_tab[...] = g_tab_in[...] + norm_back(wide, inverse, gains[0:1], total)
-
-
-def run_backward(ids, keep, p, q, ds, conv, queue, tab, gains, taps, w_in, g_tab, small):
-    blocks, _, rows = ids.shape
-    vocab, width = tab.shape
-    hidden = keep.shape[1]
-    kernel = taps.shape[0]
-    total = blocks * rows
-    rim = (kernel - 1) * ROWS
-    last = blocks - 1
-    wide = pl.BlockSpec((rows, hidden), lambda i: (last - i, 0))
-    thin = pl.BlockSpec((rows, width), lambda i: (last - i, 0))
-    out = ((width, 2 * hidden), (vocab, width), (2 * ROWS, width))
-    return pl.pallas_call(
-        backward_kernel,
-        grid=(blocks,),
-        in_specs=[pl.BlockSpec((1, ROWS, rows), lambda i: (last - i, 0, 0)), wide, wide, wide, wide, thin, thin]
-        + [whole(a.shape) for a in (tab, gains, taps, w_in, g_tab, small)],
-        out_specs=[whole(s) for s in out],
-        out_shape=[jax.ShapeDtypeStruct(s, F32) for s in out],
-        scratch_shapes=[
-            pltpu.VMEM((rows, hidden), F32),
-            pltpu.VMEM((rows, hidden), F32),
-            pltpu.VMEM((rows, 2 * hidden), BF),
-            pltpu.VMEM((rim + rows, width), F32),
-            pltpu.VMEM((rim, width), F32),
-            pltpu.VMEM((ROWS, hidden), F32),
-            pltpu.VMEM((vocab, width), F32),
-        ],
-        compiler_params=pltpu.CompilerParams(
-            dimension_semantics=("arbitrary",), vmem_limit_bytes=62 * MIB
-        ),
-        cost_estimate=pl.CostEstimate(
-            flops=2 * total * width * (4 * hidden + vocab), bytes_accessed=total * hidden * 16, transcendentals=0
-        ),
-        name="front_back",
-    )(ids, keep, p, q, ds, conv, queue, tab, gains, taps, w_in, g_tab, small)
-
-
 def place():
     dp = lax.axis_index("dp")
     seq = lax.axis_index("seq")
@@ -776,12 +647,20 @@
     )
 
 
-def in_order(items, phases, act):
-    for time in range(items + phases - 1):
+def in_order(groups, phases, act):
+    for time in range(len(groups) + phases - 1):
         for phase in range(phases - 1, -1, -1):
-            item = time - phase
-            if 0 <= item < items:
-                act(item, phase)
+            at = time - phase
+            if 0 <= at < len(groups):
+                for item in groups[at]:
+                    act(item, phase)
+
+
+def grouped(plan):
+    groups = {}
+    for i, part in enumerate(plan):
+        groups.setdefault(part[0], []).append(i)
+    return list(groups.values())
 
 
 def gather_kernel(plan, depth, ids, *refs):
@@ -860,7 +739,7 @@
         held[i] = remote(part, part, send.at[i, at], recv.at[i, at], peer)
         held[i].start()
 
-    in_order(len(plan), 4, act)
+    in_order(grouped(plan), 4, act)
     for copy in spread:
         copy.wait_recv()
     for copy in spread + started:
@@ -896,7 +775,7 @@
     )(ids, *tensors)
 
 
-def add_into(target, other, rank):
+def add_into(target, other):
     lead = target.shape[: len(target.shape) - 2]
     total = 1
     for d in lead:
@@ -914,167 +793,328 @@
     lax.fori_loop(0, total, one, 0)
 
 
-def reduce_kernel(plan, depth, tensors, *refs):
-    n = len(tensors)
-    items = len(plan)
-    grads = refs[:n]
-    small = refs[n]
-    outs = refs[n + 1 : 2 * n + 1]
-    small_o, norm_o = refs[2 * n + 1 : 2 * n + 3]
-    scratch = refs[2 * n + 3 :]
-    sizes = 4
-    bufs = [scratch[i * sizes : (i + 1) * sizes] for i in range(items)]
-    rest = scratch[items * sizes :]
-    small_r, square_s, square_r = rest[0:3]
-    own_sem, send, recv, small_send, small_recv, sq_send, sq_recv = rest[3:]
-    y, x, z, core = place()
-    greet(y, x, z, core, depth)
-    started = []
-    peer_of = {
-        "core": device(y, x, z, 1 - core),
-        "x": device(y, 1 - x, z, core),
-        "y": device(1 - y, x, z, core),
-    }
-
-    loads, held = [], {}
-    for i, (t, lo, hi, _) in enumerate(plan):
-        cols = pl.ds(lo, hi - lo)
+def halves(shapes, start=0):
+    plan = []
+    for t, shape in enumerate(shapes):
+        cols = shape[-1]
+        plan.append((t + start, 0, cols // 2, True))
+        plan.append((t + start, cols // 2, cols, False))
+    return plan
+
+
+class Reduce:
+    def __init__(self, plan, depth, sources, resident, outs, bufs, loads, send, recv, at):
+        self.plan, self.depth, self.sources, self.resident = plan, depth, sources, resident
+        self.outs, self.bufs, self.loads, self.send, self.recv = outs, bufs, loads, send, recv
+        self.y, self.x, self.z, self.core = at
+
+    def sizes(shape, lo, hi, depth, resident):
+        piece = (shape[-2], hi - lo)
+        whole = pltpu.VMEM((2, 2, depth) + piece, F32)
+        own = [] if resident else [whole]
+        return own + [whole, pltpu.VMEM((2, depth) + piece, F32), pltpu.VMEM((2, depth) + piece, F32)]
+
+    def load(self, i):
+        t, lo, hi, _ = self.plan[i]
+        source = self.sources[t].at[:, :, :, self.core, :, pl.ds(lo, hi - lo)]
+        return pltpu.make_async_copy(source, self.bufs[i][0], self.loads.at[i])
+
+    def copies(self, i, phase):
+        t, lo, hi, along_x = self.plan[i]
+        y, x, z, core = self.y, self.x, self.z, self.core
+        whole, half, quarter = self.bufs[i][-3:]
+        by_x, by_y = device(y, 1 - x, z, core), device(1 - y, x, z, core)
+        if phase == 0:
+            source = self.sources[t].at[:, :, :, 1 - core, :, pl.ds(lo, hi - lo)]
+            moves = [(source, whole, device(y, x, z, 1 - core))]
+        elif phase == 1:
+            moves = [(whole.at[1 - y], half, by_y) if along_x else (whole.at[:, 1 - x], half, by_x)]
+        elif phase == 2:
+            moves = [(half.at[1 - x], quarter.at[0], by_x) if along_x else (half.at[1 - y], quarter.at[0], by_y)]
+        else:
+            moves = []
+            for dz in range(1, self.depth):
+                pz = (z + dz) % self.depth
+                moves.append((quarter.at[0, pz], quarter.at[1, dz], device(y, x, pz, core)))
+        return [
+            remote(src, dst, self.send.at[i, phase + n], self.recv.at[i, phase + n], peer)
+            for n, (src, dst, peer) in enumerate(moves)
+        ]
+
+    def begin(self, i):
+        for copy in self.copies(i, 0):
+            copy.start()
+        if not self.resident:
+            self.load(i).start()
+
+    def act(self, i, phase):
+        t, lo, hi, along_x = self.plan[i]
+        y, x, z, core = self.y, self.x, self.z, self.core
+        whole, half, quarter = self.bufs[i][-3:]
+        for copy in self.copies(i, phase):
+            copy.wait_recv()
+        if phase == 0:
+            if self.resident:
+                add_into(whole, self.sources[t].at[:, :, :, core, :, pl.ds(lo, hi - lo)])
+            else:
+                self.load(i).wait()
+                add_into(whole, self.bufs[i][0])
+        elif phase == 1:
+            add_into(half, whole.at[y] if along_x else whole.at[:, x])
+        elif phase == 2:
+            add_into(quarter.at[0], half.at[x] if along_x else half.at[y])
+        else:
+            total = quarter[0, z]
+            for dz in range(1, self.depth):
+                total = total + quarter[1, dz]
+            self.outs[t][:, lo:hi] = total
+            return
+        for copy in self.copies(i, phase + 1):
+            copy.start()
+
+    def finish(self):
+        for i in range(len(self.plan)):
+            for phase in range(4):
+                for copy in self.copies(i, phase):
+                    copy.wait_send()
+
+
+def everywhere(value, slots, sends, recvs, depth, at):
+    y, x, z, core = at
+    slots[0] = value
+    peers = (device(y, x, z, 1 - core), device(y, 1 - x, z, core), device(1 - y, x, z, core))
+    for n, peer in enumerate(peers):
+        copy = remote(slots.at[2 * n], slots.at[2 * n + 1], sends.at[n], recvs.at[n], peer)
+        copy.start()
+        copy.wait()
+        slots[2 * n + 2] = slots[2 * n] + slots[2 * n + 1]
+    copies = []
+    for dz in range(1, depth):
         copy = remote(
-            grads[t].at[:, :, :, 1 - core, :, cols], bufs[i][1], send.at[i, 0], recv.at[i, 0], peer_of["core"]
+            slots.at[6], slots.at[7 + z], sends.at[2 + dz], recvs.at[2 + dz], device(y, x, (z + dz) % depth, core)
         )
         copy.start()
-        held[i] = [copy]
-        load = pltpu.make_async_copy(grads[t].at[:, :, :, core, :, cols], bufs[i][0], own_sem.at[i])
-        load.start()
-        loads.append(load)
-
-    def act(i, phase):
-        t, lo, hi, along_x = plan[i]
-        whole_b, core_b, half_b, quarter_b = bufs[i]
-        for copy in held[i]:
-            copy.wait_recv()
-        started.extend(held[i])
-        if phase == 0:
-            loads[i].wait()
-            add_into(whole_b, core_b, 3)
-            if along_x:
-                src, peer = whole_b.at[1 - y], peer_of["y"]
-            else:
-                src, peer = whole_b.at[:, 1 - x], peer_of["x"]
-            held[i] = [remote(src, half_b, send.at[i, 1], recv.at[i, 1], peer)]
-        elif phase == 1:
-            if along_x:
-                add_into(half_b, whole_b.at[y], 2)
-                src, peer = half_b.at[1 - x], peer_of["x"]
-            else:
-                add_into(half_b, whole_b.at[:, x], 2)
-                src, peer = half_b.at[1 - y], peer_of["y"]
-            held[i] = [remote(src, quarter_b.at[0], send.at[i, 2], recv.at[i, 2], peer)]
-        elif phase == 2:
-            mine = half_b.at[x] if along_x else half_b.at[y]
-            add_into(quarter_b.at[0], mine, 1)
-            held[i] = []
-            for dz in range(1, depth):
-                pz = (z + dz) % depth
-                held[i].append(
-                    remote(
-                        quarter_b.at[0, pz],
-                        quarter_b.at[1, dz],
-                        send.at[i, 2 + dz],
-                        recv.at[i, 2 + dz],
-                        device(y, x, pz, core),
-                    )
-                )
-        else:
-            total = quarter_b[0, z]
-            for dz in range(1, depth):
-                total = total + quarter_b[1, dz]
-            outs[t][:, lo:hi] = total
-            return
-        for copy in held[i]:
-            copy.start()
-
-    def everywhere(value, slots, sends, recvs):
-        slots[0] = value
-        for at, name in enumerate(("core", "x", "y")):
-            copy = remote(slots.at[2 * at], slots.at[2 * at + 1], sends.at[at], recvs.at[at], peer_of[name])
-            copy.start()
-            copy.wait()
-            slots[2 * at + 2] = slots[2 * at] + slots[2 * at + 1]
-        copies = []
-        for dz in range(1, depth):
-            copy = remote(
-                slots.at[6],
-                slots.at[7 + z],
-                sends.at[2 + dz],
-                recvs.at[2 + dz],
-                device(y, x, (z + dz) % depth, core),
-            )
-            copy.start()
-            copies.append(copy)
-        slots[7 + z] = slots[6]
-        for copy in copies:
-            copy.wait()
-        total = slots[7]
-        for dz in range(1, depth):
-            total = total + slots[7 + dz]
-        return total
-
-    in_order(items, 4, act)
-    sums = everywhere(small[...], small_r, small_send, small_recv)
-    small_o[...] = sums
-    square = jnp.zeros((1, 1), F32)
-    for out in outs:
-        value = out[...]
-        square = square + jnp.sum(jnp.sum(value * value, axis=1, keepdims=True), axis=0, keepdims=True)
-    squares = everywhere(jnp.broadcast_to(square, (ROWS, LANES)), square_r, sq_send, sq_recv)
-    norm_o[...] = squares
-    for copy in started:
-        copy.wait_send()
-
-
-def run_reduce(depth, tensors, small):
-    plan = []
-    for t, a in enumerate(tensors):
-        cols = a.shape[-1]
-        plan.append((t, 0, cols // 2, True))
-        plan.append((t, cols // 2, cols, False))
-    shapes = tuple(a.shape for a in tensors)
-    scratch = []
-    for t, lo, hi, along_x in plan:
-        rows = shapes[t][-2]
-        piece = (rows, hi - lo)
-        scratch.append(pltpu.VMEM((2, 2, depth) + piece, F32))
-        scratch.append(pltpu.VMEM((2, 2, depth) + piece, F32))
-        scratch.append(pltpu.VMEM((2, depth) + piece, F32))
-        scratch.append(pltpu.VMEM((2, depth) + piece, F32))
+        copies.append(copy)
+    slots[7 + z] = slots[6]
+    for copy in copies:
+        copy.wait()
+    total = slots[7]
+    for dz in range(1, depth):
+        total = total + slots[7 + dz]
+    return total
+
+
+SCHEDULE = {1: [(0, 0)], 2: [(1, 0)], 3: [(2, 0)], 4: [(0, 1)], 6: [(1, 1), (0, 2)], 7: [(2, 1)]}
+LEFT_OVER = [(1, 2), (2, 2), (0, 3), (1, 3), (2, 3)]
+
+
+def backward_kernel(
+    depth, early, late, early_bufs, late_bufs, *refs
+):
+    ids, keep, p, q, ds, conv, queue, tab, gains, taps, w_in, g_tab_in, small_in = refs[:13]
+    n_early, n_late = len(grouped(early)), len(grouped(late))
+    sources = refs[13 : 13 + n_early]
+    outs = refs[13 + n_early : 13 + 2 * n_early + n_late]
+    small_o, squares_o = refs[13 + 2 * n_early + n_late : 15 + 2 * n_early + n_late]
+    scratch = refs[15 + 2 * n_early + n_late :]
+    small, g_in, g_tab, lam_s, reach_s, d_pre, ext, head_s, carry_s, hot_sum = scratch[:10]
+    loads, early_send, early_recv, late_send, late_recv, slots, sq_slots, sends, recvs, sq_sends, sq_recvs = scratch[10:21]
+    at = 21
+    held = []
+    for n in early_bufs + late_bufs:
+        held.append(scratch[at : at + n])
+        at += n
+    spot = place()
+    first_sums = Reduce(
+        early, depth, sources, False, outs[:n_early], held[: len(early)], loads, early_send, early_recv, spot
+    )
+    last_sums = Reduce(
+        late, depth, (g_in, g_tab), True, outs[n_early:], held[len(early) :], None, late_send, late_recv, spot
+    )
+    early_groups, late_groups = grouped(early), grouped(late)
+    step = pl.program_id(0)
+    rows, hidden = keep.shape
+    vocab, width = tab.shape
+    kernel = taps.shape[0]
+    rim = (kernel - 1) * ROWS
+    steps = rows // ROWS
+    bias_rows = hidden // width
+
+    @pl.when(step == 0)
+    def _():
+        greet(*spot, depth)
+        for i in range(len(early)):
+            first_sums.begin(i)
+        g_in[...] = jnp.zeros_like(g_in)
+        hot_sum[...] = jnp.zeros_like(hot_sum)
+        small[...] = jnp.zeros_like(small)
+        small[0:ROWS, :] = small_in[...]
+        head_s[...] = jnp.zeros_like(head_s)
+        carry_s[...] = jnp.zeros_like(carry_s)
+
+    for when, acts in SCHEDULE.items():
+
+        @pl.when(step == when)
+        def _(acts=acts):
+            for group, phase in acts:
+                for i in early_groups[group]:
+                    first_sums.act(i, phase)
+
+    low_half = lax.broadcasted_iota(jnp.int32, (ROWS, hidden), 0) < ROWS // 2
+
+    def scan_one(i, state):
+        carry, reach = state
+        at = pl.ds(pl.multiple_of((steps - 1 - i) * ROWS, ROWS), ROWS)
+        lam = ds[at, :] + carry
+        lam_s[at, :] = lam
+        reach_s[at, :] = reach
+        k = keep[at, :]
+        return k * lam, k * reach
+
+    first, _ = lax.fori_loop(
+        0, steps, scan_one, (carry_s[...], jnp.where(low_half, 1.0, 0.0)), unroll=4
+    )
+    entry = jnp.where(low_half, swap_halves(first), 0.0)
+    reach0 = keep[0:ROWS, :] * reach_s[0:ROWS, :]
+    carry_s[...] = jnp.where(low_half, 0.0, swap_halves(first + reach0 * entry))
+
+    def fix_one(pair, sums):
+        gates, cands = [], []
+        for half_step in range(2):
+            at = pl.ds(pl.multiple_of(pair * 2 * ROWS + half_step * ROWS, ROWS), ROWS)
+            lam = lam_s[at, :] + reach_s[at, :] * entry
+            d_gate = lam * p[at, :]
+            sums = sums + d_gate
+            gates.append(d_gate)
+            cands.append(lam * q[at, :])
+        both = pl.ds(pl.multiple_of(pair * 2 * ROWS, 2 * ROWS), 2 * ROWS)
+        d_pre[both, 0:hidden] = jnp.concatenate(gates, axis=0).astype(BF)
+        d_pre[both, hidden : 2 * hidden] = jnp.concatenate(cands, axis=0).astype(BF)
+        return sums
+
+    sums = lax.fori_loop(
+        0, steps // 2, fix_one, jnp.zeros((ROWS, hidden), F32), unroll=4
+    )
+    d_bias = column_sum(sums)
+    base = ROWS + kernel
+    for r in range(bias_rows):
+        small[base + r : base + r + 1, :] += d_bias[:, r * width : (r + 1) * width]
+
+    g_in[...] += tn(conv[...], d_pre[...]).reshape(g_in.shape)
+    ext[0:rows, :] = nt(d_pre[...], w_in[...])
+    half = lax.broadcasted_iota(jnp.int32, (rim, width), 0) % ROWS < ROWS // 2
+    mine = ext[0:rim, :]
+    ext[rows:, :] = jnp.where(
+        half,
+        swap_halves(mine.reshape(kernel - 1, ROWS, width)).reshape(rim, width),
+        swap_halves(head_s[...].reshape(kernel - 1, ROWS, width)).reshape(rim, width),
+    )
+    head_s[...] = mine
+    known = queue[...].astype(F32)
+    d_queue = None
+    for k in range(kernel):
+        shift = (kernel - 1 - k) * ROWS
+        part = ext[shift : shift + rows, :]
+        term = taps[k : k + 1] * part
+        d_queue = term if d_queue is None else d_queue + term
+        small[ROWS + k : ROWS + k + 1, :] += column_sum(part * known)
+    hot_t = one_hot_t(ids[0][0:1, :], vocab)
+    hot_sum[...] += nn(hot_t, d_queue.astype(BF))
+
+    @pl.when(step == pl.num_programs(0) - 1)
+    def _():
+        wide = tab[...].astype(BF).astype(F32)
+        inverse = inv_rms(wide)
+        total = hot_sum[...]
+        small[0:1, :] = column_sum(total * (wide * inverse))
+        g_tab[...] = (g_tab_in[...] + norm_back(wide, inverse, gains[0:1], total)).reshape(g_tab.shape)
+        for i in range(len(late)):
+            last_sums.begin(i)
+        for group, phase in LEFT_OVER[:2]:
+            for i in early_groups[group]:
+                first_sums.act(i, phase)
+        for phase in range(4):
+            for group in late_groups:
+                for i in group:
+                    last_sums.act(i, phase)
+            if phase == 0:
+                for group, stage in LEFT_OVER[2:]:
+                    for i in early_groups[group]:
+                        first_sums.act(i, stage)
+                small_o[...] = everywhere(small[...], slots, sends, recvs, depth, spot)
+        square = jnp.zeros((1, 1), F32)
+        for out in outs:
+            value = out[...]
+            square = square + jnp.sum(jnp.sum(value * value, axis=1, keepdims=True), axis=0, keepdims=True)
+        squares_o[...] = everywhere(
+            jnp.broadcast_to(square, (ROWS, LANES)), sq_slots, sq_sends, sq_recvs, depth, spot
+        )
+        first_sums.finish()
+        last_sums.finish()
+
+
+def run_backward(depth, ids, keep, p, q, ds, conv, queue, tab, gains, taps, w_in, g_tab, small, grads):
+    blocks, _, rows = ids.shape
+    vocab, width = tab.shape
+    hidden = keep.shape[1]
+    kernel = taps.shape[0]
+    total = blocks * rows
+    rim = (kernel - 1) * ROWS
+    last = blocks - 1
+    wide = pl.BlockSpec((rows, hidden), lambda i: (last - i, 0))
+    thin = pl.BlockSpec((rows, width), lambda i: (last - i, 0))
+    owners = (2, 2, depth, 2)
+    early_shapes = [g.shape for g in grads]
+    late_shapes = [owners + (width // (8 * depth), 2 * hidden), owners + (vocab // (8 * depth), width)]
+    early, late = halves(early_shapes), halves(late_shapes)
+    early_bufs = [Reduce.sizes(early_shapes[t], lo, hi, depth, False) for t, lo, hi, _ in early]
+    late_bufs = [Reduce.sizes(late_shapes[t], lo, hi, depth, True) for t, lo, hi, _ in late]
     any_spec = pl.BlockSpec(memory_space=pl.ANY)
-    vmem = pl.BlockSpec(memory_space=pltpu.VMEM)
-    n = len(tensors)
+    out = [s[-2:] for s in early_shapes + late_shapes] + [(2 * ROWS, width), (ROWS, LANES)]
+    flat = [b for group in early_bufs + late_bufs for b in group]
+    dma = lambda *shape: pltpu.SemaphoreType.DMA(shape)
     return pl.pallas_call(
-        functools.partial(reduce_kernel, plan, depth, shapes),
-        in_specs=[any_spec] * n + [vmem],
-        out_specs=[vmem] * (n + 2),
-        out_shape=[jax.ShapeDtypeStruct(s[-2:], F32) for s in shapes]
-        + [jax.ShapeDtypeStruct(small.shape, F32), jax.ShapeDtypeStruct((ROWS, LANES), F32)],
-        scratch_shapes=scratch
-        + [
-            pltpu.VMEM((7 + depth,) + small.shape, F32),
-            pltpu.VMEM((ROWS, LANES), F32),
+        functools.partial(
+            backward_kernel, depth, early, late, [len(b) for b in early_bufs], [len(b) for b in late_bufs]
+        ),
+        grid=(blocks,),
+        in_specs=[pl.BlockSpec((1, ROWS, rows), lambda i: (last - i, 0, 0)), wide, wide, wide, wide, thin, thin]
+        + [whole(a.shape) for a in (tab, gains, taps, w_in, g_tab, small)]
+        + [any_spec] * len(grads),
+        out_specs=[whole(s) for s in out],
+        out_shape=[jax.ShapeDtypeStruct(s, F32) for s in out],
+        scratch_shapes=[
+            pltpu.VMEM((2 * ROWS, width), F32),
+            pltpu.VMEM(late_shapes[0], F32),
+            pltpu.VMEM(late_shapes[1], F32),
+            pltpu.VMEM((rows, hidden), F32),
+            pltpu.VMEM((rows, hidden), F32),
+            pltpu.VMEM((rows, 2 * hidden), BF),
+            pltpu.VMEM((rim + rows, width), F32),
+            pltpu.VMEM((rim, width), F32),
+            pltpu.VMEM((ROWS, hidden), F32),
+            pltpu.VMEM((vocab, width), F32),
+            dma(len(early)),
+            dma(len(early), depth + 2),
+            dma(len(early), depth + 2),
+            dma(len(late), depth + 2),
+            dma(len(late), depth + 2),
+            pltpu.VMEM((7 + depth, 2 * ROWS, width), F32),
             pltpu.VMEM((7 + depth, ROWS, LANES), F32),
-            pltpu.SemaphoreType.DMA((len(plan),)),
-            pltpu.SemaphoreType.DMA((len(plan), depth + 2)),
-            pltpu.SemaphoreType.DMA((len(plan), depth + 2)),
-            pltpu.SemaphoreType.DMA((depth + 2,)),
-            pltpu.SemaphoreType.DMA((depth + 2,)),
-            pltpu.SemaphoreType.DMA((depth + 2,)),
-            pltpu.SemaphoreType.DMA((depth + 2,)),
-        ],
+            dma(depth + 2),
+            dma(depth + 2),
+            dma(depth + 2),
+            dma(depth + 2),
+        ]
+        + flat,
         compiler_params=pltpu.CompilerParams(
-            collective_id=1, has_side_effects=True, vmem_limit_bytes=60 * MIB
+            dimension_semantics=("arbitrary",), collective_id=1, has_side_effects=True, vmem_limit_bytes=62 * MIB
         ),
-        name="reduce_grads",
-    )(*tensors, small)
+        cost_estimate=pl.CostEstimate(
+            flops=2 * total * width * (4 * hidden + vocab), bytes_accessed=total * hidden * 16, transcendentals=0
+        ),
+        name="front_back_and_reduce",
+    )(ids, keep, p, q, ds, conv, queue, tab, gains, taps, w_in, g_tab, small, *grads)
 
 
 def adam_kernel(shapes, small, squares, count, *refs):
@@ -1154,11 +1194,11 @@
     keep, p, q, ds, conv, queue, g_down, g_up, g_out, g_tab, small = run_forward(
         ids, tab, count, gains, taps, gate_bias, *full
     )
-    g_in, g_tab, small = run_backward(ids, keep, p, q, ds, conv, queue, tab, gains, taps, full[0], g_tab, small)
-    whole_grads = [
-        g.reshape((2, 2, depth, 2, -1, g.shape[-1])) for g in (g_tab, g_in, g_out, g_up, g_down)
-    ]
-    *mats, small, squares = run_reduce(depth, whole_grads, small)
+    grads = [g.reshape((2, 2, depth, 2, -1, g.shape[-1])) for g in (g_down, g_up, g_out)]
+    r_down, r_up, r_out, r_in, r_tab, small, squares = run_backward(
+        depth, ids, keep, p, q, ds, conv, queue, tab, gains, taps, full[0], g_tab, small, grads
+    )
+    mats = [r_tab, r_in, r_out, r_up, r_down]
     flat = lambda group: [group[0]] + [a[0] for a in group[1:5]] + [group[5], group[6][0], group[7]]
     out = run_adam(
         (conv_taps.shape[1], gate_bias.shape[1] // width),

time: 438 us -> 348 us (0.79)
  Pallas kernels: 414 us -> 325 us
    pallas_call x2 -> x1, Pallas kernels: 192 us -> 124 us  [run_backward(): pl.pallas_call(functools.partial(backward_kernel, depth, early, late, [le...]
    pallas_call x1, Pallas kernels: 82.5 us -> 60.8 us  [run_gather(): pl.pallas_call(functools.partial(gather_kernel, plan, depth), in_specs=[a...]
where the time goes in v2:
time: 348 us; the launch traced here: 347 us
  Pallas kernels  325 us (93%)
  local copies, waits for them, and re-layouts  14.6 us (4%)
  other arithmetic  6.7 us (2%)
    pallas_call x1, Pallas kernels, run_forward(): pl.pallas_call(forward_kernel, grid=(blocks,), in_specs=[pl.BlockSpec((1,...  139 us
    pallas_call x1, Pallas kernels, run_backward(): pl.pallas_call(functools.partial(backward_kernel, depth, early, late, [le...  124 us
    pallas_call x1, Pallas kernels, run_gather(): pl.pallas_call(functools.partial(gather_kernel, plan, depth), in_specs=[a...  60.8 us

profile of v2, /device:TPU:0, one launch (start us, length us, event | category | flops | bytes accessed | tf_op | source)
XLA Modules:
  0.0 347.2 jit_solution(14955930734589487906)
XLA Ops:
  0.7 1.3 convert_reduce_fusion
  2.0 0.1 pad.4.clone
  2.1 2.0 concatenate.7.refs_0_
  4.0 0.8 reshape.153
  4.8 0.8 reshape.155
  5.7 0.8 reshape.157
  6.5 1.5 bitcast_convert_fusion.2.refs_2_
  7.9 1.5 bitcast_convert_fusion.refs_4_
  9.5 1.6 bitcast_convert_fusion.1
  11.1 0.2 copy.59
  11.3 0.1 copy.62
  11.4 0.2 copy.58
  11.6 0.1 copy.61
  11.7 0.2 copy.57
  11.9 0.1 copy.60
  11.9 0.7 add_add_fusion.ids
  12.7 60.8 %gather_weights.1 = (s32[8,8,512]{2,1,0:T(8,128)}, f32[2,2,4,2,8,640]{5,4,3,2,1,0:T(8,128)}, bf16[2,2,4,2,16,2048]{5,4,3,2,1,0:T(8,128)(2,1)}, bf16[2,2,4,2,32,5...) custom-call(s32[8,8,512]{2,1,0:T(8,128)} %add_add_fusion.ids, ...), custom_call_target="tpu_custom_call" | custom-call | tf_op jit(solution)/shard_map/gather_weights/pallas_call | solution.py:760
  73.5 1.6 slice.7
  75.1 1.9 slice.6
  77.0 138.7 %forward_and_tail_back.1 = (f32[4096,1024]{1,0:T(8,128)}, f32[4096,1024]{1,0:T(8,128)}, f32[4096,1024]{1,0:T(8,128)}, f32[4096,1024]{1,0:T(8,128)}, bf16[4096,51...) custom-call(s32[8,8,512]{2,1,0:T(8,128)} %get-tuple-element.78.ids.r, ...), custom_call_target="tpu_custom_call" | custom-call | flops 80530628608 | bytes 67108864 | tf_op jit(solution)/shard_map/forward_and_tail_back/pallas_call | solution.py:582
  215.6 0.0 copy-start
  215.6 0.0 copy-start.1
  215.7 0.0 copy-start.2
  215.7 0.0 copy-start.3
  215.7 0.0 copy-start.4
  215.7 0.0 copy-start.5
  215.7 0.0 copy-start.6
  215.7 0.0 copy-start.7
  215.7 0.0 copy-start.8
  215.7 0.0 copy-start.9
  215.8 0.0 copy-start.10
  215.8 0.0 copy-start.14
  215.8 0.0 copy-start.15
  215.8 0.0 copy-start.16
  215.8 0.0 copy-start.19
  215.8 0.0 copy-start.20
  215.8 0.0 copy-start.21
  215.8 0.0 copy-start.22
  215.9 0.0 copy-start.24
  215.9 0.0 copy-start.25
  215.9 0.0 copy-start.26
  215.9 0.0 copy-start.27
  215.9 0.0 copy-start.28
  215.9 0.0 copy-start.29
  215.9 0.0 copy-start.30
  215.9 123.7 %front_back_and_reduce.1 = (f32[64,512]{1,0:T(8,128)}, f32[16,2048]{1,0:T(8,128)}, f32[32,512]{1,0:T(8,128)}, f32[16,2048]{1,0:T(8,128)}, f32[8,512]{1,0:T(8,128)}, /*index=5*/f32[16,512]{1,0:T(8,128)}, f32[8,128]{1,0:T(8,128)}) custom-call(s32[8,8,512]{2,1,0:T(8,128)} %get-tuple-element.78.ids.refs_0_, f32[4096,1024]{1,0:T(8,128)} %get-tuple-element.84.refs_1_, ...), custom_call_target="tpu_custom_call" | custom-call | flops 18253611008 | bytes 67108864 | tf_op jit(solution)/shard_map/front_back_and_reduce/pallas_call | solution.py:1076
  339.7 0.0 copy-done
  339.7 0.0 copy-done.1
  339.7 0.0 copy-done.2
  339.7 0.0 copy-done.3
  339.7 0.0 copy-done.4
  339.7 0.0 copy-done.5
  339.7 0.0 copy-done.6
  339.8 0.0 copy-done.7
  339.8 0.0 copy-done.8
  339.8 0.0 copy-done.9
  339.9 0.9 copy-done.11
  340.8 0.9 copy-done.12
  341.7 0.9 copy-done.13
  342.7 0.8 copy-done.17
  343.5 0.8 copy-done.18
  344.2 0.7 copy-done.23
  345.0 0.7 copy-done.31
  345.6 1.4 adam_update.1
  (23 shorter events, 0.0 us)
Async XLA Ops:
  215.6 124.0 %copy-start = (f32[1,16,2048]{2,1,0:T(8,128)S(1)}, f32[1,16,2048]{2,1,0:T(8,128)}, u32[]{:S(2)}) copy-start(f32[1,16,2048]{2,1,0:T(8,128)} %param.33) | copy-start | bytes 393220
  215.6 124.0 %copy-start.1 = (f32[1,16,2048]{2,1,0:T(8,128)S(1)}, f32[1,16,2048]{2,1,0:T(8,128)}, u32[]{:S(2)}) copy-start(f32[1,16,2048]{2,1,0:T(8,128)} %param.31) | copy-start | bytes 393220
  215.7 124.0 %copy-start.2 = (f32[1,64,512]{2,1,0:T(8,128)S(1)}, f32[1,64,512]{2,1,0:T(8,128)}, u32[]{:S(2)}) copy-start(f32[1,64,512]{2,1,0:T(8,128)} %param.34) | copy-start | bytes 393220
  215.7 124.0 %copy-start.3 = (f32[2,2,4,2,8,128]{5,4,3,2,1,0:T(8,128)S(1)}, f32[2,2,4,2,8,128]{5,4,3,2,1,0:T(8,128)}, u32[]{:S(2)}) copy-start(f32[2,2,4,2,8,128]{5,4,3,2,1,0:T(8,128)} %slice.7) | copy-start | bytes 393220
  215.7 124.0 %copy-start.4 = (f32[1,32,512]{2,1,0:T(8,128)S(1)}, f32[1,32,512]{2,1,0:T(8,128)}, u32[]{:S(2)}) copy-start(f32[1,32,512]{2,1,0:T(8,128)} %param.32) | copy-start | bytes 196612
  215.7 124.0 %copy-start.5 = (f32[1,16,2048]{2,1,0:T(8,128)S(1)}, f32[1,16,2048]{2,1,0:T(8,128)}, u32[]{:S(2)}) copy-start(f32[1,16,2048]{2,1,0:T(8,128)} %param.39) | copy-start | bytes 393220
  215.7 124.0 %copy-start.6 = (f32[1,16,2048]{2,1,0:T(8,128)S(1)}, f32[1,16,2048]{2,1,0:T(8,128)}, u32[]{:S(2)}) copy-start(f32[1,16,2048]{2,1,0:T(8,128)} %param.41) | copy-start | bytes 393220
  215.7 124.0 %copy-start.7 = (f32[1,64,512]{2,1,0:T(8,128)S(1)}, f32[1,64,512]{2,1,0:T(8,128)}, u32[]{:S(2)}) copy-start(f32[1,64,512]{2,1,0:T(8,128)} %param.42) | copy-start | bytes 393220
  215.7 124.0 %copy-start.8 = (f32[1,16,2048]{2,1,0:T(8,128)S(1)}, f32[1,16,2048]{2,1,0:T(8,128)}, u32[]{:S(2)}) copy-start(f32[1,16,2048]{2,1,0:T(8,128)} %param.47) | copy-start | bytes 393220
  215.7 124.0 %copy-start.9 = (f32[1,16,2048]{2,1,0:T(8,128)S(1)}, f32[1,16,2048]{2,1,0:T(8,128)}, u32[]{:S(2)}) copy-start(f32[1,16,2048]{2,1,0:T(8,128)} %param.49) | copy-start | bytes 393220
  215.8 124.0 %copy-start.10 = (f32[1,64,512]{2,1,0:T(8,128)S(1)}, f32[1,64,512]{2,1,0:T(8,128)}, u32[]{:S(2)}) copy-start(f32[1,64,512]{2,1,0:T(8,128)} %param.50) | copy-start | bytes 393220
  215.8 124.0 %copy-start.14 = (f32[8,512]{1,0:T(8,128)S(1)}, f32[8,512]{1,0:T(8,128)}, u32[]{:S(2)}) copy-start(f32[8,512]{1,0:T(8,128)} %refs_5_.1) | copy-start | bytes 49156
  215.8 124.0 %copy-start.15 = (f32[1,32,512]{2,1,0:T(8,128)S(1)}, f32[1,32,512]{2,1,0:T(8,128)}, u32[]{:S(2)}) copy-start(f32[1,32,512]{2,1,0:T(8,128)} %param.40) | copy-start | bytes 196612
  215.8 124.0 %copy-start.16 = (f32[1,32,512]{2,1,0:T(8,128)S(1)}, f32[1,32,512]{2,1,0:T(8,128)}, u32[]{:S(2)}) copy-start(f32[1,32,512]{2,1,0:T(8,128)} %param.48) | copy-start | bytes 196612
  215.8 124.0 %copy-start.19 = (f32[3,512]{1,0:T(4,128)S(1)}, f32[3,512]{1,0:T(4,128)}, u32[]{:S(2)}) copy-start(f32[3,512]{1,0:T(4,128)} %refs_10_.1) | copy-start | bytes 18436
  215.8 124.0 %copy-start.20 = (f32[1,4,512]{2,1,0:T(4,128)S(1)}, f32[1,4,512]{2,1,0:T(4,128)}, u32[]{:S(2)}) copy-start(f32[1,4,512]{2,1,0:T(4,128)} %param.36) | copy-start | bytes 24580
  215.8 124.0 %copy-start.21 = (f32[8,512]{1,0:T(8,128)S(1)}, f32[8,512]{1,0:T(8,128)}, u32[]{:S(2)}) copy-start(f32[8,512]{1,0:T(8,128)} %refs_13_.1) | copy-start | bytes 49156
  215.8 124.0 %copy-start.22 = (f32[8,512]{1,0:T(8,128)S(1)}, f32[8,512]{1,0:T(8,128)}, u32[]{:S(2)}) copy-start(f32[8,512]{1,0:T(8,128)} %refs_21_.1) | copy-start | bytes 49156
  215.9 124.0 %copy-start.24 = (f32[3,512]{1,0:T(4,128)S(1)}, f32[3,512]{1,0:T(4,128)}, u32[]{:S(2)}) copy-start(f32[3,512]{1,0:T(4,128)} %refs_18_.1) | copy-start | bytes 18436
  215.9 124.0 %copy-start.25 = (f32[1,4,512]{2,1,0:T(4,128)S(1)}, f32[1,4,512]{2,1,0:T(4,128)}, u32[]{:S(2)}) copy-start(f32[1,4,512]{2,1,0:T(4,128)} %param.44) | copy-start | bytes 24580
  215.9 124.0 %copy-start.26 = (f32[3,512]{1,0:T(4,128)S(1)}, f32[3,512]{1,0:T(4,128)}, u32[]{:S(2)}) copy-start(f32[3,512]{1,0:T(4,128)} %refs_26_.1) | copy-start | bytes 18436
  215.9 124.0 %copy-start.27 = (f32[1,4,512]{2,1,0:T(4,128)S(1)}, f32[1,4,512]{2,1,0:T(4,128)}, u32[]{:S(2)}) copy-start(f32[1,4,512]{2,1,0:T(4,128)} %param.52) | copy-start | bytes 24580
  215.9 124.0 %copy-start.28 = (f32[1,1024]{1,0:T(1,128)S(1)}, f32[1,1024]{1,0:T(1,128)}, u32[]{:S(2)}) copy-start(f32[1,1024]{1,0:T(1,128)} %refs_12_.1) | copy-start | bytes 12292
  215.9 124.0 %copy-start.29 = (f32[1,1024]{1,0:T(1,128)S(1)}, f32[1,1024]{1,0:T(1,128)}, u32[]{:S(2)}) copy-start(f32[1,1024]{1,0:T(1,128)} %refs_20_.1) | copy-start | bytes 12292
  215.9 124.0 %copy-start.30 = (f32[1,1024]{1,0:T(1,128)S(1)}, f32[1,1024]{1,0:T(1,128)}, u32[]{:S(2)}) copy-start(f32[1,1024]{1,0:T(1,128)} %refs_28_.1) | copy-start | bytes 12292
  339.9 0.9 copy-start.11
  340.8 0.9 copy-start.12
  341.7 0.9 copy-start.13
  342.6 0.8 copy-start.17
  343.5 0.8 copy-start.18
  344.2 0.7 copy-start.23
  345.0 0.7 copy-start.31

commit v3 on v0

--- a/solution.py
+++ b/solution.py
@@ -1,6 +1,10 @@
+import functools
+
 import jax
 import jax.numpy as jnp
 from jax import lax
+from jax.experimental import pallas as pl
+from jax.experimental.pallas import tpu as pltpu
 from jax.sharding import PartitionSpec as P
 
 V = 256
@@ -351,9 +355,1040 @@
     )
 
 
+BF = jnp.bfloat16
+F32 = jnp.float32
+MIB = 1 << 20
+LANES = 128
+ROWS = 8
+GELU_A = 0.7978845608028654
+GELU_B = 0.044715
+
+
+def nn(left, right):
+    return jnp.dot(left, right, preferred_element_type=F32)
+
+
+def tn(left, right):
+    return lax.dot_general(left, right, (((0,), (0,)), ((), ())), preferred_element_type=F32)
+
+
+def nt(left, right):
+    return lax.dot_general(left, right, (((1,), (1,)), ((), ())), preferred_element_type=F32)
+
+
+def inv_rms(values):
+    return lax.rsqrt(jnp.mean(values * values, axis=-1, keepdims=True) + EPS)
+
+
+def norm_back(values, inverse, gain, grad):
+    width = values.shape[-1]
+    scaled = grad * gain
+    dot = jnp.sum(scaled * values, axis=-1, keepdims=True)
+    return inverse * scaled - values * (inverse * inverse * inverse * dot * (1.0 / width))
+
+
+def column_sum(values):
+    return jnp.sum(values, axis=0, keepdims=True)
+
+
+def swap_halves(tile):
+    return pltpu.roll(tile, ROWS // 2, tile.ndim - 2)
+
+
+def one_hot(column, vocab):
+    lane = lax.broadcasted_iota(jnp.int32, (column.shape[0], vocab), 1)
+    return (column == lane).astype(F32).astype(BF)
+
+
+def one_hot_t(row, vocab):
+    place = lax.broadcasted_iota(jnp.int32, (vocab, row.shape[1]), 0)
+    return (row == place).astype(F32).astype(BF)
+
+
+def whole(shape):
+    zeros = (0,) * len(shape)
+    return pl.BlockSpec(shape, lambda i: zeros, pipeline_mode=pl.Buffered(1))
+
+
+def place():
+    dp = lax.axis_index("dp")
+    seq = lax.axis_index("seq")
+    return dp // 2, dp % 2, seq // 2, seq % 2
+
+
+def device(y, x, z, core):
+    return (y * 2 + x, z * 2 + core)
+
+
+def greet(y, x, z, core, depth):
+    barrier = pltpu.get_barrier_semaphore()
+    peers = [device(1 - y, x, z, core), device(y, 1 - x, z, core), device(1 - y, 1 - x, z, core)]
+    for dz in range(depth):
+        for dc in range(2):
+            if dz or dc:
+                peers.append(device(y, x, (z + dz) % depth, (core + dc) % 2))
+    for peer in peers:
+        pl.semaphore_signal(barrier, inc=1, device_id=peer, device_id_type=pl.DeviceIdType.MESH)
+    pl.semaphore_wait(barrier, len(peers))
+
+
+def remote(src, dst, send, recv, peer):
+    return pltpu.make_async_remote_copy(
+        src_ref=src,
+        dst_ref=dst,
+        send_sem=send,
+        recv_sem=recv,
+        device_id=peer,
+        device_id_type=pl.DeviceIdType.MESH,
+    )
+
+
+def in_order(groups, phases, act):
+    for time in range(len(groups) + phases - 1):
+        for phase in range(phases - 1, -1, -1):
+            at = time - phase
+            if 0 <= at < len(groups):
+                for item in groups[at]:
+                    act(item, phase)
+
+
+def grouped(plan):
+    return [[i, i + 1] for i in range(0, len(plan), 2)]
+
+
+class Gather:
+    def __init__(self, plan, depth, sources, outs, send, recv, at):
+        self.plan, self.depth, self.sources, self.outs, self.send, self.recv = plan, depth, sources, outs, send, recv
+        self.y, self.x, self.z, self.core = at
+
+    def copies(self, i, phase):
+        t, lo, hi, along_x = self.plan[i]
+        cols = pl.ds(lo, hi - lo)
+        y, x, z, core = self.y, self.x, self.z, self.core
+        out = self.outs[t]
+        by_x, by_y = device(y, 1 - x, z, core), device(1 - y, x, z, core)
+        if phase == 0:
+            mine = out.at[y, x, z, core, :, cols]
+            source = mine if self.sources[t] is None else self.sources[t].at[:, cols]
+            moves = [(source, mine, device(y, x, (z + dz) % self.depth, core)) for dz in range(1, self.depth)]
+        elif phase == 1:
+            part = out.at[y, x, :, core, :, cols]
+            moves = [(part, part, by_x if along_x else by_y)]
+        elif phase == 2:
+            part = out.at[y, :, :, core, :, cols] if along_x else out.at[:, x, :, core, :, cols]
+            moves = [(part, part, by_y if along_x else by_x)]
+        else:
+            part = out.at[:, :, :, core, :, cols]
+            moves = [(part, part, device(y, x, z, 1 - core))]
+        base = 0 if phase == 0 else self.depth - 2 + phase
+        return [
+            remote(src, dst, self.send.at[i, base + n], self.recv.at[i, base + n], peer)
+            for n, (src, dst, peer) in enumerate(moves)
+        ]
+
+    def begin(self, i):
+        for copy in self.copies(i, 0):
+            copy.start()
+
+    def act(self, i, phase):
+        for copy in self.copies(i, phase):
+            copy.wait_recv()
+        if phase < 3:
+            for copy in self.copies(i, phase + 1):
+                copy.start()
+
+    def finish(self):
+        for i in range(len(self.plan)):
+            for phase in range(4):
+                for copy in self.copies(i, phase):
+                    copy.wait_send()
+
+
+def add_into(target, other):
+    lead = target.shape[: len(target.shape) - 2]
+    total = 1
+    for d in lead:
+        total *= d
+
+    def one(i, _):
+        index = []
+        for d in reversed(lead):
+            index.append(lax.rem(i, d))
+            i = lax.div(i, d)
+        index = tuple(reversed(index))
+        target[index] = target[index] + other[index]
+        return _
+
+    lax.fori_loop(0, total, one, 0)
+
+
+def halves(shapes, cuts=None):
+    plan = []
+    for t, shape in enumerate(shapes):
+        pieces = 2 * (cuts[t] if cuts else 1)
+        wide = shape[-1] // pieces
+        for n in range(pieces):
+            plan.append((t, n * wide, (n + 1) * wide, n % 2 == 0))
+    return plan
+
+
+class Reduce:
+    def __init__(self, plan, depth, sources, resident, outs, bufs, loads, send, recv, at):
+        self.plan, self.depth, self.sources, self.resident = plan, depth, sources, resident
+        self.outs, self.bufs, self.loads, self.send, self.recv = outs, bufs, loads, send, recv
+        self.y, self.x, self.z, self.core = at
+
+    def sizes(shape, lo, hi, depth, resident):
+        piece = (shape[-2], hi - lo)
+        whole = pltpu.VMEM((2, 2, depth) + piece, F32)
+        own = [] if resident else [whole]
+        return own + [whole, pltpu.VMEM((2, depth) + piece, F32), pltpu.VMEM((2, depth) + piece, F32)]
+
+    def load(self, i):
+        t, lo, hi, _ = self.plan[i]
+        source = self.sources[t].at[:, :, :, self.core, :, pl.ds(lo, hi - lo)]
+        return pltpu.make_async_copy(source, self.bufs[i][0], self.loads.at[i])
+
+    def copies(self, i, phase):
+        t, lo, hi, along_x = self.plan[i]
+        y, x, z, core = self.y, self.x, self.z, self.core
+        whole, half, quarter = self.bufs[i][-3:]
+        by_x, by_y = device(y, 1 - x, z, core), device(1 - y, x, z, core)
+        if phase == 0:
+            source = self.sources[t].at[:, :, :, 1 - core, :, pl.ds(lo, hi - lo)]
+            moves = [(source, whole, device(y, x, z, 1 - core))]
+        elif phase == 1:
+            moves = [(whole.at[1 - y], half, by_y) if along_x else (whole.at[:, 1 - x], half, by_x)]
+        elif phase == 2:
+            moves = [(half.at[1 - x], quarter.at[0], by_x) if along_x else (half.at[1 - y], quarter.at[0], by_y)]
+        else:
+            moves = []
+            for dz in range(1, self.depth):
+                pz = (z + dz) % self.depth
+                moves.append((quarter.at[0, pz], quarter.at[1, dz], device(y, x, pz, core)))
+        return [
+            remote(src, dst, self.send.at[i, phase + n], self.recv.at[i, phase + n], peer)
+            for n, (src, dst, peer) in enumerate(moves)
+        ]
+
+    def begin(self, i):
+        for copy in self.copies(i, 0):
+            copy.start()
+        if not self.resident:
+            self.load(i).start()
+
+    def act(self, i, phase):
+        t, lo, hi, along_x = self.plan[i]
+        y, x, z, core = self.y, self.x, self.z, self.core
+        whole, half, quarter = self.bufs[i][-3:]
+        for copy in self.copies(i, phase):
+            copy.wait_recv()
+        if phase == 0:
+            if self.resident:
+                add_into(whole, self.sources[t].at[:, :, :, core, :, pl.ds(lo, hi - lo)])
+            else:
+                self.load(i).wait()
+                add_into(whole, self.bufs[i][0])
+        elif phase == 1:
+            add_into(half, whole.at[y] if along_x else whole.at[:, x])
+        elif phase == 2:
+            add_into(quarter.at[0], half.at[x] if along_x else half.at[y])
+        else:
+            total = quarter[0, z]
+            for dz in range(1, self.depth):
+                total = total + quarter[1, dz]
+            self.outs[t][:, lo:hi] = total
+            return
+        for copy in self.copies(i, phase + 1):
+            copy.start()
+
+    def finish(self):
+        for i in range(len(self.plan)):
+            for phase in range(4):
+                for copy in self.copies(i, phase):
+                    copy.wait_send()
+
+
+class Everywhere:
+    def __init__(self, slots, sends, recvs, depth, at):
+        y, x, z, core = at
+        self.slots, self.ways = slots, 2 * depth
+        self.me, self.other = z * 2 + core, self.ways + y * 2 + x
+        self.near, self.far = [], []
+        mine = slots.at[self.me]
+        for dz in range(depth):
+            for dc in range(2):
+                if dz or dc:
+                    n = dz * 2 + dc
+                    peer = device(y, x, (z + dz) % depth, (core + dc) % 2)
+                    self.near.append(remote(mine, mine, sends.at[n], recvs.at[n], peer))
+        mine = slots.at[self.other]
+        for n, (dy, dx) in enumerate(((0, 1), (1, 0), (1, 1))):
+            n += self.ways
+            peer = device((y + dy) % 2, (x + dx) % 2, z, core)
+            self.far.append(remote(mine, mine, sends.at[n], recvs.at[n], peer))
+
+    def total(self, lo, hi):
+        value = self.slots[lo]
+        for n in range(lo + 1, hi):
+            value = value + self.slots[n]
+        return value
+
+    def begin(self, value):
+        self.slots[self.me] = value
+        for copy in self.near:
+            copy.start()
+
+    def middle(self):
+        for copy in self.near:
+            copy.wait()
+        self.slots[self.other] = self.total(0, self.ways)
+        for copy in self.far:
+            copy.start()
+
+    def end(self):
+        for copy in self.far:
+            copy.wait()
+        return self.total(self.ways, self.ways + 4)
+
+
+SCHEDULE = {
+    2: [(True, 0, 0), (True, 1, 0)], 3: [(True, 2, 0)], 4: [(True, 0, 1)], 6: [(True, 1, 1)],
+    9: [(True, 2, 1), (False, 0, 0), (False, 1, 0), (True, 0, 2)], 10: [(True, 1, 2)], 12: [(True, 2, 2)], 14: [(False, 0, 1)],
+}
+LEFT_OVER = [
+    (False, 2, 0), (None, 0, 0), (False, 1, 1), (False, 0, 2), (False, 2, 1), (True, 0, 3), (True, 1, 3), (True, 2, 3),
+    (False, 1, 2), (False, 2, 2), (False, 0, 3), (False, 1, 3), (False, 2, 3),
+]
+
+
+def backward_kernel(depth, early, late, sizes, *refs):
+    ids, keep, p, q, ds, conv, queue, tab, gains, taps, w_in, g_tab_a, g_tab_b, small_in, r_down = refs[:15]
+    sources = refs[15:17]
+    outs = tuple(refs[17:21])
+    small_o, squares_o = refs[21:23]
+    small, g_in, g_tab, d_pre, ext, head_s, carry_s, hot_sum = refs[23:31]
+    loads, early_send, early_recv, late_send, late_recv, slots, sq_slots, sends, recvs, sq_sends, sq_recvs = refs[31:42]
+    at = 42
+    held = []
+    for n in sizes:
+        held.append(refs[at : at + n])
+        at += n
+    spot = place()
+    first_sums = Reduce(
+        early, depth, sources, False, outs[:2], held[: len(early)], loads, early_send, early_recv, spot
+    )
+    last_sums = Reduce(
+        late, depth, (g_in, g_tab), True, outs[2:], held[len(early) :], None, late_send, late_recv, spot
+    )
+    smalls = Everywhere(slots, sends, recvs, depth, spot)
+    squares = Everywhere(sq_slots, sq_sends, sq_recvs, depth, spot)
+    early_groups, late_groups = grouped(early), grouped(late)
+    step = pl.program_id(0)
+    blocks = pl.num_programs(0) // 2
+    rows, hidden = keep.shape
+    vocab, width = tab.shape
+    kernel = taps.shape[0]
+    rim = (kernel - 1) * ROWS
+    steps = rows // ROWS
+    bias_rows = hidden // width
+    base = ROWS + kernel
+
+    def run(acts):
+        for is_early, group, phase in acts:
+            if is_early is None:
+                smalls.middle()
+                continue
+            sums, groups = (first_sums, early_groups) if is_early else (last_sums, late_groups)
+            for i in groups[group]:
+                sums.act(i, phase)
+
+    @pl.when(step == 0)
+    def _():
+        greet(*spot, depth)
+        for i in range(len(early)):
+            first_sums.begin(i)
+        g_in[...] = jnp.zeros_like(g_in)
+        hot_sum[...] = jnp.zeros_like(hot_sum)
+        small[...] = jnp.zeros_like(small)
+        small[0:ROWS, :] = small_in[...]
+        head_s[...] = jnp.zeros_like(head_s)
+        carry_s[...] = jnp.zeros_like(carry_s)
+
+    for when, acts in SCHEDULE.items():
+
+        @pl.when(step == when)
+        def _(acts=acts):
+            run(acts)
+
+    @pl.when(step < blocks)
+    def _():
+        low_half = lax.broadcasted_iota(jnp.int32, (ROWS, hidden), 0) < ROWS // 2
+        carry = carry_s[...]
+        block = blocks - 1 - step
+
+        def scan_one(i, reached):
+            at = pl.ds(pl.multiple_of((steps - 1 - i) * ROWS, ROWS), ROWS)
+            return keep[at, :] * (ds[at, :] + reached)
+
+        first = lax.fori_loop(0, steps, scan_one, carry, unroll=8)
+
+        def scan_two(i, state):
+            reached, total = state
+            pair = steps // 2 - 1 - i
+            gates, cands = [None, None], [None, None]
+            for half_step in (1, 0):
+                at = pl.ds(pl.multiple_of(pair * 2 * ROWS + half_step * ROWS, ROWS), ROWS)
+                lam = ds[at, :] + reached
+                reached = keep[at, :] * lam
+                gates[half_step] = lam * p[at, :]
+                cands[half_step] = lam * q[at, :]
+                total = total + gates[half_step]
+            both = pl.ds(pl.multiple_of(pair * 2 * ROWS, 2 * ROWS), 2 * ROWS)
+            d_pre[block, both, 0:hidden] = jnp.concatenate(gates, axis=0).astype(BF)
+            d_pre[block, both, hidden : 2 * hidden] = jnp.concatenate(cands, axis=0).astype(BF)
+            return reached, total
+
+        entry = jnp.where(low_half, swap_halves(first), carry)
+        last, total = lax.fori_loop(
+            0, steps // 2, scan_two, (entry, jnp.zeros((ROWS, hidden), F32)), unroll=4
+        )
+        carry_s[...] = jnp.where(low_half, 0.0, swap_halves(last))
+        d_bias = column_sum(total)
+        for r in range(bias_rows):
+            small[base + r : base + r + 1, :] += d_bias[:, r * width : (r + 1) * width]
+        g_in[...] += tn(conv[...], d_pre[block]).reshape(g_in.shape)
+
+    @pl.when(step == blocks - 1)
+    def _():
+        for group in late_groups[:2]:
+            for i in group:
+                last_sums.begin(i)
+
+    @pl.when(step >= blocks)
+    def _():
+        block = 2 * blocks - 1 - step
+        ext[0:rows, :] = nt(d_pre[block], w_in[...])
+        half = lax.broadcasted_iota(jnp.int32, (rim, width), 0) % ROWS < ROWS // 2
+        mine = ext[0:rim, :]
+        ext[rows:, :] = jnp.where(
+            half,
+            swap_halves(mine.reshape(kernel - 1, ROWS, width)).reshape(rim, width),
+            swap_halves(head_s[...].reshape(kernel - 1, ROWS, width)).reshape(rim, width),
+        )
+        head_s[...] = mine
+        known = queue[...].astype(F32)
+        d_queue = None
+        for k in range(kernel):
+            shift = (kernel - 1 - k) * ROWS
+            part = ext[shift : shift + rows, :]
+            term = taps[k : k + 1] * part
+            d_queue = term if d_queue is None else d_queue + term
+            small[ROWS + k : ROWS + k + 1, :] += column_sum(part * known)
+        hot_t = one_hot_t(ids[0][0:1, :], vocab)
+        hot_sum[...] += nn(hot_t, d_queue.astype(BF))
+
+    @pl.when(step == 2 * blocks - 1)
+    def _():
+        wide = tab[...].astype(BF).astype(F32)
+        inverse = inv_rms(wide)
+        total = hot_sum[...]
+        small[0:1, :] = column_sum(total * (wide * inverse))
+        smalls.begin(small[...])
+        g_tab[...] = (
+            g_tab_a[...] + g_tab_b[...] + norm_back(wide, inverse, gains[0:1], total)
+        ).reshape(g_tab.shape)
+        for i in late_groups[2]:
+            last_sums.begin(i)
+        run(LEFT_OVER)
+        small_o[...] = smalls.end()
+        square = jnp.zeros((1, 1), F32)
+        for out in outs + (r_down,):
+            value = out[...]
+            square = square + jnp.sum(jnp.sum(value * value, axis=1, keepdims=True), axis=0, keepdims=True)
+        squares.begin(jnp.broadcast_to(square, (ROWS, LANES)))
+        squares.middle()
+        squares_o[...] = squares.end()
+        first_sums.finish()
+        last_sums.finish()
+
+
+def run_backward(depth, ids, keep, p, q, ds, conv, queue, tab, gains, taps, w_in, g_tabs, small, r_down, grads):
+    blocks, _, rows = ids.shape
+    vocab, width = tab.shape
+    hidden = keep.shape[1]
+    kernel = taps.shape[0]
+    rim = (kernel - 1) * ROWS
+    last = blocks - 1
+    wide = pl.BlockSpec((rows, hidden), lambda i: (jnp.maximum(last - i, 0), 0))
+    front = pl.BlockSpec((rows, width), lambda i: (jnp.maximum(last - i, 0), 0))
+    back = pl.BlockSpec((rows, width), lambda i: (jnp.minimum(2 * blocks - 1 - i, last), 0))
+    back_ids = pl.BlockSpec((1, ROWS, rows), lambda i: (jnp.minimum(2 * blocks - 1 - i, last), 0, 0))
+    owners = (2, 2, depth, 2)
+    early_shapes = [g.shape for g in grads]
+    late_shapes = [owners + (width // (8 * depth), 2 * hidden), owners + (vocab // (8 * depth), width)]
+    early, late = halves(early_shapes, (2, 1)), halves(late_shapes, (2, 1))
+    bufs = [Reduce.sizes(early_shapes[t], lo, hi, depth, False) for t, lo, hi, _ in early]
+    bufs += [Reduce.sizes(late_shapes[t], lo, hi, depth, True) for t, lo, hi, _ in late]
+    any_spec = pl.BlockSpec(memory_space=pl.ANY)
+    out = [s[-2:] for s in early_shapes + late_shapes] + [(2 * ROWS, width), (ROWS, LANES)]
+    dma = lambda *shape: pltpu.SemaphoreType.DMA(shape)
+    fixed = (tab, gains, taps, w_in) + tuple(g_tabs) + (small, r_down)
+    return pl.pallas_call(
+        functools.partial(backward_kernel, depth, early, late, [len(b) for b in bufs]),
+        grid=(2 * blocks,),
+        in_specs=[back_ids, wide, wide, wide, wide, front, back]
+        + [whole(a.shape) for a in fixed]
+        + [any_spec] * len(grads),
+        out_specs=[whole(s) for s in out],
+        out_shape=[jax.ShapeDtypeStruct(s, F32) for s in out],
+        scratch_shapes=[
+            pltpu.VMEM((2 * ROWS, width), F32),
+            pltpu.VMEM(late_shapes[0], F32),
+            pltpu.VMEM(late_shapes[1], F32),
+            pltpu.VMEM((blocks, rows, 2 * hidden), BF),
+            pltpu.VMEM((rim + rows, width), F32),
+            pltpu.VMEM((rim, width), F32),
+            pltpu.VMEM((ROWS, hidden), F32),
+            pltpu.VMEM((vocab, width), F32),
+            dma(len(early)),
+            dma(len(early), depth + 2),
+            dma(len(early), depth + 2),
+            dma(len(late), depth + 2),
+            dma(len(late), depth + 2),
+            pltpu.VMEM((2 * depth + 4, 2 * ROWS, width), F32),
+            pltpu.VMEM((2 * depth + 4, ROWS, LANES), F32),
+            dma(2 * depth + 4),
+            dma(2 * depth + 4),
+            dma(2 * depth + 4),
+            dma(2 * depth + 4),
+        ]
+        + [b for group in bufs for b in group],
+        compiler_params=pltpu.CompilerParams(
+            dimension_semantics=("arbitrary",), collective_id=1, has_side_effects=True, vmem_limit_bytes=63 * MIB
+        ),
+        name="front_back_and_reduce",
+    )(ids, keep, p, q, ds, conv, queue, *fixed, *grads)
+
+
+def front_block(ids, qtab, taps, bias, w_in, keep_o, p_o, q_o, conv_o, queue_o, state_o, padq, tail_s, carry_s, big):
+    rows, hidden = keep_o.shape
+    vocab, width = qtab.shape
+    kernel = taps.shape[0]
+    rim = (kernel - 1) * ROWS
+    steps = rows // ROWS
+    chunk = 256
+    hot = one_hot(ids.T[:, 0:1], vocab)
+    queue = nn(hot, qtab[...])
+    queue_o[...] = queue.astype(BF)
+    padq[rim:, :] = queue
+    half = lax.broadcasted_iota(jnp.int32, (rim, width), 0) % ROWS < ROWS // 2
+    before = tail_s[...].reshape(kernel - 1, ROWS, width)
+    latest = padq[rows:, :].reshape(kernel - 1, ROWS, width)
+    padq[0:rim, :] = jnp.where(
+        half, swap_halves(before).reshape(rim, width), swap_halves(latest).reshape(rim, width)
+    )
+    tail_s[...] = padq[rows:, :]
+    conv = taps[0:1] * padq[0:rows, :]
+    for k in range(1, kernel):
+        conv = conv + taps[k : k + 1] * padq[k * ROWS : k * ROWS + rows, :]
+    conv_o[...] = conv.astype(BF)
+
+    for j in range(hidden // chunk):
+        cols = slice(j * chunk, (j + 1) * chunk)
+        gate = nn(conv_o[...], w_in[:, j * chunk : (j + 1) * chunk]) + bias[0:1, cols]
+        cand = nn(conv_o[...], w_in[:, hidden + j * chunk : hidden + (j + 1) * chunk])
+        eg = jnp.exp(-jnp.abs(gate))
+        rg = pl.reciprocal(1.0 + eg)
+        sg = eg * rg
+        up = gate >= 0
+        write_gate = jnp.where(up, rg, sg)
+        keep_o[:, cols] = jnp.where(up, sg, rg)
+        ec = jnp.exp(-jnp.abs(cand))
+        rc = pl.reciprocal(1.0 + ec)
+        slope = jnp.where(cand >= 0, rc, ec * rc)
+        soft = jnp.maximum(cand, 0.0) + jnp.where(
+            ec < 1e-3, ec * (1.0 - 0.5 * ec), jnp.log(1.0 + ec)
+        )
+        p_o[:, cols] = write_gate
+        q_o[:, cols] = write_gate * slope
+        big[:, cols] = write_gate * soft
+
+    low_half = lax.broadcasted_iota(jnp.int32, (ROWS, hidden), 0) < ROWS // 2
+    carry = carry_s[...]
+
+    def scan_one(tau, state):
+        at = pl.ds(pl.multiple_of(tau * ROWS, ROWS), ROWS)
+        return keep_o[at, :] * state + big[at, :]
+
+    end = lax.fori_loop(0, steps, scan_one, carry, unroll=8)
+
+    def scan_two(pair, state):
+        lows = []
+        for half_step in range(2):
+            at = pl.ds(pl.multiple_of(pair * 2 * ROWS + half_step * ROWS, ROWS), ROWS)
+            keep, write = keep_o[at, :], big[at, :]
+            p_o[at, :] = keep * (write - p_o[at, :] * state)
+            state = keep * state + write
+            lows.append(state)
+        both = pl.ds(pl.multiple_of(pair * 2 * ROWS, 2 * ROWS), 2 * ROWS)
+        state_o[both, :] = jnp.concatenate(lows, axis=0).astype(BF)
+        return state
+
+    last = lax.fori_loop(0, steps // 2, scan_two, jnp.where(low_half, carry, swap_halves(end)), unroll=4)
+    carry_s[...] = jnp.where(low_half, swap_halves(last), 0.0)
+
+
+GATHER_SCHEDULE = {1: [(0, 0), (1, 0)], 2: [(2, 0), (0, 1)], 3: [(1, 1)], 4: [(2, 1), (0, 2)], 5: [(1, 2)], 6: [(2, 2)]}
+GATHER_LAST = [(0, 3), (1, 3), (2, 3)]
+
+
+def front_kernel(
+    depth, now, later,
+    ids, table, w_in, w_out, w_up, w_down, gains, taps, bias,
+    keep_o, p_o, q_o, conv_o, queue_o, state_o, ids_o, tab_o, count_o, w_in_o, w_out_o, w_up_o, w_down_o,
+    ids_s, tab_s, count_s, in_s, out_s, up_s, down_s, qtab, padq, tail_s, carry_s, big,
+    ids_send, ids_recv, now_send, now_recv, later_send, later_recv, own_sem, in_sem,
+):
+    step = pl.program_id(0)
+    spot = place()
+    y, x, z, core = spot
+    me = z * 2 + core
+    wait_in = pltpu.make_async_copy(in_s, w_in_o, in_sem)
+    first = Gather(now, depth, [None] * 3, [tab_s, count_s, in_s], now_send, now_recv, spot)
+    rest = Gather(later, depth, [out_s, up_s, down_s], [w_out_o, w_up_o, w_down_o], later_send, later_recv, spot)
+    later_groups = grouped(later)
+    own = [
+        pltpu.make_async_copy(src, dst.at[y, x, z, core], own_sem.at[n])
+        for n, (src, dst) in enumerate(((out_s, w_out_o), (up_s, w_up_o), (down_s, w_down_o)))
+    ]
+    spread = []
+    for dz in range(depth):
+        for dc in range(2):
+            if dz or dc:
+                pz, pc = (z + dz) % depth, (core + dc) % 2
+                n = dz * 2 + dc
+                spread.append(
+                    remote(ids.at[pz * 2 + pc], ids_s.at[me], ids_send.at[n], ids_recv.at[n], device(y, x, pz, pc))
+                )
+
+    @pl.when(step == 0)
+    def _():
+        tab_s[y, x, z, core] = table[...]
+        share = jnp.zeros((1, ids.shape[2]), F32)
+        for n in range(ids.shape[0]):
+            share = share + ids[n, 2:3, :].astype(F32)
+        count_s[y, x, z, core] = jnp.broadcast_to(jnp.sum(share, axis=1, keepdims=True), count_o.shape)
+        in_s[y, x, z, core] = w_in[...].astype(BF)
+        greet(*spot, depth)
+        for i in range(len(now)):
+            first.begin(i)
+        for copy in spread:
+            copy.start()
+        out_s[...] = w_out[...].astype(BF)
+        up_s[...] = w_up[...].astype(BF)
+        down_s[...] = w_down[...].astype(BF)
+        for copy in own:
+            copy.start()
+        ids_s[me] = ids[me]
+        for i in range(len(now)):
+            first.act(i, 0)
+        for i in range(len(later)):
+            rest.begin(i)
+        for phase in range(1, 4):
+            for i in range(len(now)):
+                first.act(i, phase)
+        wait_in.start()
+        for copy in spread:
+            copy.wait_recv()
+        tab = tab_s[...].reshape(tab_o.shape)
+        tab_o[...] = tab
+        wide = tab.astype(BF).astype(F32)
+        qtab[...] = (wide * inv_rms(wide) * gains[0:1]).astype(BF)
+        total = jnp.zeros(count_o.shape, F32)
+        for n in range(8 * depth):
+            total = total + count_s[n // (4 * depth), n // (2 * depth) % 2, n // 2 % depth, n % 2]
+        count_o[...] = total
+        tail_s[...] = jnp.zeros_like(tail_s)
+        carry_s[...] = jnp.zeros_like(carry_s)
+        for copy in own:
+            copy.wait()
+
+    for when, acts in GATHER_SCHEDULE.items():
+
+        @pl.when(step == when)
+        def _(acts=acts):
+            for group, phase in acts:
+                for i in later_groups[group]:
+                    rest.act(i, phase)
+
+    here = ids_s[step]
+    ids_o[0] = here
+    front_block(
+        here, qtab, taps, bias, FlatRows(in_s), keep_o, p_o, q_o, conv_o, queue_o, state_o, padq, tail_s, carry_s, big
+    )
+
+    @pl.when(step == pl.num_programs(0) - 1)
+    def _():
+        for group, phase in GATHER_LAST:
+            for i in later_groups[group]:
+                rest.act(i, phase)
+        wait_in.wait()
+        for copy in spread:
+            copy.wait_send()
+        first.finish()
+        rest.finish()
+
+
+class FlatRows:
+    def __init__(self, ref):
+        self.ref = ref
+
+    def __getitem__(self, index):
+        cols = index[1]
+        part = self.ref[:, :, :, :, :, cols]
+        return part.reshape(-1, part.shape[-1])
+
+
+def run_front(depth, ids, table, mats, gains, taps, bias):
+    blocks, _, rows = ids.shape
+    w_in, w_out, w_up, w_down = mats
+    width = table.shape[1]
+    hidden = bias.shape[1]
+    kernel = taps.shape[0]
+    total = blocks * rows
+    rim = (kernel - 1) * ROWS
+    owners = (2, 2, depth, 2)
+    devices = 8 * depth
+    vocab = devices * table.shape[0]
+    cols = w_in.shape[1]
+    now = [(0, 0, width, True), (1, 0, LANES, False)]
+    for n in range(4):
+        now.append((2, n * cols // 4, (n + 1) * cols // 4, n % 2 == 0))
+    later = halves([a.shape for a in (w_out, w_up, w_down)])
+    wide = pl.BlockSpec((rows, hidden), lambda i: (i, 0))
+    thin = pl.BlockSpec((rows, width), lambda i: (i, 0))
+    any_spec = pl.BlockSpec(memory_space=pl.ANY)
+    dma = lambda *shape: pltpu.SemaphoreType.DMA(shape)
+    args = (ids, table, w_in, w_out, w_up, w_down, gains, taps, bias)
+    struct = jax.ShapeDtypeStruct
+    return pl.pallas_call(
+        functools.partial(front_kernel, depth, now, later),
+        grid=(blocks,),
+        in_specs=[whole(a.shape) for a in args],
+        out_specs=[wide] * 3 + [thin, thin, wide]
+        + [pl.BlockSpec((1, ROWS, rows), lambda i: (i, 0, 0)), whole((vocab, width)), whole((ROWS, LANES))]
+        + [any_spec] * 4,
+        out_shape=[struct((total, hidden), F32)] * 3
+        + [struct((total, width), BF)] * 2
+        + [struct((total, hidden), BF), struct(ids.shape, jnp.int32), struct((vocab, width), F32), struct((ROWS, LANES), F32)]
+        + [struct(owners + a.shape, BF) for a in mats],
+        scratch_shapes=[
+            pltpu.VMEM(ids.shape, jnp.int32),
+            pltpu.VMEM(owners + table.shape, F32),
+            pltpu.VMEM(owners + (ROWS, LANES), F32),
+            pltpu.VMEM(owners + w_in.shape, BF),
+            pltpu.VMEM(w_out.shape, BF),
+            pltpu.VMEM(w_up.shape, BF),
+            pltpu.VMEM(w_down.shape, BF),
+            pltpu.VMEM((vocab, width), BF),
+            pltpu.VMEM((rim + rows, width), F32),
+            pltpu.VMEM((rim, width), F32),
+            pltpu.VMEM((ROWS, hidden), F32),
+            pltpu.VMEM((rows, hidden), F32),
+            dma(2 * depth),
+            dma(2 * depth),
+            dma(len(now), depth + 2),
+            dma(len(now), depth + 2),
+            dma(len(later), depth + 2),
+            dma(len(later), depth + 2),
+            dma(3),
+            pltpu.SemaphoreType.DMA,
+        ],
+        compiler_params=pltpu.CompilerParams(
+            dimension_semantics=("arbitrary",), collective_id=0, has_side_effects=True, vmem_limit_bytes=60 * MIB
+        ),
+        name="gather_and_front",
+    )(*args)
+
+
+def tail_kernel(
+    ids, state_low, tab, count, gains, w_out, w_up, w_down,
+    mixed_o, normed_o, final_o, lifted_o, g_down, g_tab, small_o,
+    tab_low, slope_s, active,
+):
+    step = pl.program_id(0)
+    rows = state_low.shape[0]
+    vocab, width = tab.shape
+    ff = w_up.shape[1]
+    chunk = 256
+
+    @pl.when(step == 0)
+    def _():
+        tab_low[...] = tab[...].astype(BF)
+        g_down[...] = jnp.zeros_like(g_down)
+        g_tab[...] = jnp.zeros_like(g_tab)
+        small_o[...] = jnp.zeros_like(small_o)
+
+    columns = jnp.concatenate([ids[n].T for n in range(ids.shape[0])], axis=0)
+    hot = one_hot(columns[:, 0:1], vocab)
+    mixed = nn(hot, tab_low[...]) + nn(state_low[...], w_out[...])
+    mixed_o[...] = mixed
+    inverse_b = inv_rms(mixed)
+    normed_o[...] = (mixed * inverse_b * gains[1:2]).astype(BF)
+    for j in range(ff // chunk):
+        cols = slice(j * chunk, (j + 1) * chunk)
+        lifted = nn(normed_o[...], w_up[:, cols])
+        square = lifted * lifted
+        curve = jnp.tanh(lifted * (GELU_A + (GELU_A * GELU_B) * square))
+        cdf = 0.5 + 0.5 * curve
+        active[:, cols] = (lifted * cdf).astype(BF)
+        slope_s[:, cols] = cdf + (0.5 * lifted) * (1.0 - curve * curve) * (
+            GELU_A + (3.0 * GELU_A * GELU_B) * square
+        )
+    result = mixed_o[...] + nn(active[...], w_down[...])
+    inverse_f = inv_rms(result)
+    unit_f = result * inverse_f
+    normed_f = (unit_f * gains[2:3]).astype(BF)
+
+    logits = nt(normed_f, tab_low[...])
+    top = jnp.max(logits, axis=-1, keepdims=True)
+    powers = jnp.exp(logits - top)
+    total = jnp.sum(powers, axis=-1, keepdims=True)
+    lse = jnp.log(total) + top
+    target = columns[:, 1:2] == lax.broadcasted_iota(jnp.int32, (rows, vocab), 1)
+    picked = jnp.sum(jnp.where(target, logits, 0.0), axis=-1, keepdims=True)
+    weight = columns[:, 2:3].astype(F32)
+    loss = column_sum(weight * (lse - picked))
+    share = weight * (1.0 / count[0:1, 0:1])
+    d_logits = ((powers * (1.0 / total) - jnp.where(target, 1.0, 0.0)) * share).astype(BF)
+    g_tab[...] += tn(d_logits, normed_f)
+    d_normed_f = nn(d_logits, tab_low[...])
+    small_o[2:3, :] += column_sum(d_normed_f * unit_f)
+    small_o[3:4, :] += jnp.broadcast_to(loss, (1, width))
+    d_final = norm_back(result, inverse_f, gains[2:3], d_normed_f)
+    final_o[...] = d_final
+    grad_low = d_final.astype(BF)
+    for j in range(ff // chunk):
+        cols = slice(j * chunk, (j + 1) * chunk)
+        d_active = nt(grad_low, w_down[cols, :])
+        g_down[cols, :] += tn(active[:, cols], grad_low)
+        lifted_o[:, cols] = (d_active * slope_s[:, cols]).astype(BF)
+
+
+def run_tail(join, ids, state_low, tab, count, gains, w_out, w_up, w_down):
+    blocks, _, rows = ids.shape
+    rows, blocks = rows * join, blocks // join
+    vocab, width = tab.shape
+    hidden = w_out.shape[0]
+    ff = w_up.shape[1]
+    total = blocks * rows
+    block = lambda cols: pl.BlockSpec((rows, cols), lambda i: (i, 0))
+    sums = ((ff, width), (vocab, width), (ROWS, width))
+    struct = jax.ShapeDtypeStruct
+    return pl.pallas_call(
+        tail_kernel,
+        grid=(blocks,),
+        in_specs=[pl.BlockSpec((join, ROWS, rows // join), lambda i: (i, 0, 0)), block(hidden)]
+        + [whole(a.shape) for a in (tab, count, gains, w_out, w_up, w_down)],
+        out_specs=[block(width), block(width), block(width), block(ff)] + [whole(s) for s in sums],
+        out_shape=[struct((total, width), F32), struct((total, width), BF), struct((total, width), F32), struct((total, ff), BF)]
+        + [struct(s, F32) for s in sums],
+        scratch_shapes=[
+            pltpu.VMEM((vocab, width), BF),
+            pltpu.VMEM((rows, ff), F32),
+            pltpu.VMEM((rows, ff), BF),
+        ],
+        compiler_params=pltpu.CompilerParams(
+            dimension_semantics=("arbitrary",), vmem_limit_bytes=62 * MIB
+        ),
+        name="tail_and_head",
+    )(ids, state_low, tab, count, gains, w_out, w_up, w_down)
+
+
+DOWN_SCHEDULE = {1: [(0, 0), (1, 0)], 3: [(0, 1)], 4: [(1, 1)], 5: [(0, 2)], 6: [(1, 2)]}
+
+
+def mid_kernel(depth, plan, sizes, *refs):
+    ids, state_low, mixed, normed, final, lifted, gains, w_out, w_up, small_in, g_down = refs[:11]
+    ds_o, g_up, g_out, g_emb, small_o, r_down = refs[11:17]
+    loads, send, recv = refs[17:20]
+    bufs, at = [], 20
+    for n in sizes:
+        bufs.append(refs[at : at + n])
+        at += n
+    step = pl.program_id(0)
+    last = pl.num_programs(0) - 1
+    spot = place()
+    sums = Reduce(plan, depth, (g_down,), False, (r_down,), bufs, loads, send, recv, spot)
+    groups = grouped(plan)
+    vocab = g_emb.shape[0]
+
+    @pl.when(step == 0)
+    def _():
+        greet(*spot, depth)
+        for i in range(len(plan)):
+            sums.begin(i)
+        g_up[...] = jnp.zeros_like(g_up)
+        g_out[...] = jnp.zeros_like(g_out)
+        g_emb[...] = jnp.zeros_like(g_emb)
+        small_o[...] = small_in[...]
+
+    for when, acts in DOWN_SCHEDULE.items():
+
+        @pl.when(step == when)
+        def _(acts=acts):
+            for group, phase in acts:
+                for i in groups[group]:
+                    sums.act(i, phase)
+
+    d_normed = nt(lifted[...], w_up[...])
+    g_up[...] += tn(normed[...], lifted[...])
+    value = mixed[...]
+    inverse = inv_rms(value)
+    small_o[1:2, :] += column_sum(d_normed * (value * inverse))
+    d_mixed = final[...] + norm_back(value, inverse, gains[1:2], d_normed)
+    mixed_low = d_mixed.astype(BF)
+    rest = (d_mixed - mixed_low.astype(F32)).astype(BF)
+    ds_o[...] = nt(mixed_low, w_out[...])
+    g_out[...] += tn(state_low[...], mixed_low)
+    row = jnp.concatenate([ids[n, 0:1, :] for n in range(ids.shape[0])], axis=1)
+    hot_t = one_hot_t(row, vocab)
+    g_emb[...] += nn(hot_t, mixed_low) + nn(hot_t, rest)
+
+    @pl.when(step == last)
+    def _():
+        for group in groups:
+            for i in group:
+                sums.act(i, 3)
+        sums.finish()
+
+
+def run_mid(depth, ids, state_low, mixed, normed, final, lifted, gains, w_out, w_up, small, g_down, vocab):
+    blocks, _, rows = ids.shape
+    width, ff = w_up.shape
+    hidden = w_out.shape[0]
+    total = blocks * rows
+    block = lambda cols: pl.BlockSpec((rows, cols), lambda i: (i, 0))
+    plan = halves([g_down.shape], (2,))
+    bufs = [Reduce.sizes(g_down.shape, lo, hi, depth, False) for _, lo, hi, _ in plan]
+    dma = lambda *shape: pltpu.SemaphoreType.DMA(shape)
+    sums = ((width, ff), (hidden, width), (vocab, width), (ROWS, width), g_down.shape[-2:])
+    return pl.pallas_call(
+        functools.partial(mid_kernel, depth, plan, [len(b) for b in bufs]),
+        grid=(blocks,),
+        in_specs=[pl.BlockSpec((1, ROWS, rows), lambda i: (i, 0, 0)), block(hidden)]
+        + [block(width)] * 3 + [block(ff)]
+        + [whole(a.shape) for a in (gains, w_out, w_up, small)]
+        + [pl.BlockSpec(memory_space=pl.ANY)],
+        out_specs=[block(hidden)] + [whole(s) for s in sums],
+        out_shape=[jax.ShapeDtypeStruct((total, hidden), F32)] + [jax.ShapeDtypeStruct(s, F32) for s in sums],
+        scratch_shapes=[dma(len(plan)), dma(len(plan), depth + 2), dma(len(plan), depth + 2)]
+        + [b for group in bufs for b in group],
+        compiler_params=pltpu.CompilerParams(
+            dimension_semantics=("arbitrary",), collective_id=2, has_side_effects=True, vmem_limit_bytes=62 * MIB
+        ),
+        name="mid_back_and_reduce",
+    )(ids, state_low, mixed, normed, final, lifted, gains, w_out, w_up, small, g_down)
+
+
+def adam_kernel(shapes, small, squares, count, *refs):
+    mats = refs[:5]
+    weights, firsts, seconds = refs[5:13], refs[13:21], refs[21:29]
+    loss_o, count_o, norm_o = refs[29:32]
+    new_w, new_m, new_v = refs[32:40], refs[40:48], refs[48:56]
+    kernel, bias_rows = shapes
+    width = small.shape[1]
+    grads = [m[...] for m in mats]
+    grads.append(small[0:3, :])
+    grads.append(small[ROWS : ROWS + kernel, :])
+    base = ROWS + kernel
+    grads.append(
+        jnp.concatenate([small[base + r : base + r + 1, :] for r in range(bias_rows)], axis=1)
+    )
+    square = squares[0:1, 0:1]
+    for grad in grads[5:]:
+        square = square + jnp.sum(jnp.sum(grad * grad, axis=1, keepdims=True), axis=0, keepdims=True)
+    norm = jnp.sqrt(square)
+    scale = jnp.minimum(1.0, CLIP / (norm + 1e-06))
+    norm_o[...] = norm
+    loss_o[...] = small[3:4, 0:1]
+    count_o[...] = count[0:1, 0:1]
+    for i in range(8):
+        rate = RATE_MATRIX if i < 5 else RATE_VECTOR
+        decay = WEIGHT_DECAY if i < 5 else 0.0
+        w, m, v = adam(weights[i][...], grads[i] * scale, firsts[i][...], seconds[i][...], rate, decay)
+        new_w[i][...] = w
+        new_m[i][...] = m
+        new_v[i][...] = v
+
+
+def run_adam(shapes, mats, small, squares, count, weights, firsts, seconds):
+    one = jax.ShapeDtypeStruct((1, 1), F32)
+    like = [jax.ShapeDtypeStruct(w.shape, F32) for w in weights]
+    args = (small, squares, count) + tuple(mats) + tuple(weights) + tuple(firsts) + tuple(seconds)
+    return pl.pallas_call(
+        functools.partial(adam_kernel, shapes),
+        grid=(1,),
+        in_specs=[whole(a.shape) for a in args],
+        out_specs=[whole(a.shape) for a in [one] * 3 + like * 3],
+        out_shape=[one] * 3 + like * 3,
+        compiler_params=pltpu.CompilerParams(vmem_limit_bytes=60 * MIB),
+        name="adam_update",
+    )(*args)
+
+
+def spread_ids(tokens, targets, counted, depth):
+    seqs, span = tokens.shape
+    ways = 2 * depth
+    three = jnp.stack([tokens, targets, counted]).reshape(3, ways, seqs // ways, 2, span // 2)
+    rows = three.transpose(1, 0, 4, 3, 2).reshape(ways, 3, -1)
+    return jnp.pad(rows, ((0, 0), (0, ROWS - 3), (0, 0)))
+
+
+def body_moved(depth, *args):
+    tokens, targets, counted = args[:3]
+    weights, firsts, seconds = args[3:11], args[11:19], args[19:27]
+    table, w_in, w_out, w_up, w_down, gains, conv_taps, gate_bias = weights
+    width = table.shape[1]
+    taps = conv_taps[0]
+    ids = spread_ids(tokens, targets, counted, depth)
+    keep, p, q, conv, queue, state_low, ids, tab, count, *full = run_front(
+        depth, ids, table, (w_in[0], w_out[0], w_up[0], w_down[0]), gains, taps, gate_bias
+    )
+    full = [a.reshape(-1, a.shape[-1]) for a in full]
+    mixed, normed, final, lifted, g_down, g_head, small = run_tail(1, ids, state_low, tab, count, gains, *full[1:])
+    owned = lambda g: g.reshape((2, 2, depth, 2, -1, g.shape[-1]))
+    ds, g_up, g_out, g_emb, small, r_down = run_mid(
+        depth, ids, state_low, mixed, normed, final, lifted, gains, full[1], full[2], small, owned(g_down), tab.shape[0]
+    )
+    r_up, r_out, r_in, r_tab, small, squares = run_backward(
+        depth, ids, keep, p, q, ds, conv, queue, tab, gains, taps, full[0], (g_head, g_emb), small, r_down,
+        (owned(g_up), owned(g_out)),
+    )
+    mats = [r_tab, r_in, r_out, r_up, r_down]
+    flat = lambda group: [group[0]] + [a[0] for a in group[1:5]] + [group[5], group[6][0], group[7]]
+    out = run_adam(
+        (conv_taps.shape[1], gate_bias.shape[1] // width),
+        mats, small, squares, count, flat(weights), flat(firsts), flat(seconds),
+    )
+    shaped = [o.reshape(()) for o in out[:3]]
+    for i, o in enumerate(out[3:]):
+        shaped.append(o.reshape(weights[i % 8].shape))
+    return tuple(shaped)
+
+
+def choose(mesh, *args):
+    ways = mesh.shape["seq"]
+    seqs, span = args[0].shape
+    if mesh.shape["dp"] == 4 and ways == 8 and seqs == 4 * ways and span == LANES:
+        return body_moved(ways // 2, *args)
+    return body(*args)
+
+
 def solution(mesh):
     return jax.shard_map(
-        body,
+        functools.partial(choose, mesh),
         mesh=mesh,
         in_specs=(
             P("dp", "seq"),

time: 3650 us -> 278 us (0.08); the launches traced: 3580 us -> 277 us
  local copies, waits for them, and re-layouts: 1910 us -> 3.76 us
  waiting for transfers between devices: 619 us -> 0 us
  other arithmetic: 549 us -> 0.01 us
  Pallas kernels: 0 us -> 273 us
  blocking collectives: 240 us -> 0 us
  matrix products: 229 us -> 0 us
    slice x198 -> x0, local copies, waits for them, and re-layouts: 934 us -> none  [the longest x98 498 us: layer_backward(): lax.associative_scan(combine, (follow, d_state), axis=0, reverse=True)]
    reduce_scatter x5 -> x0, waiting for transfers between devices: 619 us -> none  [the longest x1 140 us: backward_step(): lax.psum_scatter(full[3], ('dp', 'seq'), scatter_dimension=0, tiled=True)]
    pad x96 -> x1, local copies, waits for them, and re-layouts: 615 us -> 0.69 us  [spread_ids(): return jnp.pad(rows, ((0, 0), (0, ROWS - 3), (0, 0)))]
    pallas_call x0 -> x5, Pallas kernels: none -> 273 us  [the longest x1 87 us: run_backward(): pl.pallas_call(functools.partial(backward_kernel, depth, early, late, [le...]
    add x101 -> x0, other arithmetic: 261 us -> none  [the longest x28 91.3 us: layer_backward(): lax.associative_scan(combine, (follow, d_state), axis=0, reverse=True)]
    rev x4 -> x0, local copies, waits for them, and re-layouts: 257 us -> none  [layer_backward(): lax.associative_scan(combine, (follow, d_state), axis=0, reverse=True)]
    dot_general x34 -> x0, matrix products: 229 us -> none  [the longest x10 81 us: matmul_nt(): lax.dot_general(left, right, (((1,), (1,)), ((), ())), preferred_element_...]
    all_gather x9 -> x0, blocking collectives: 165 us -> none  [the longest x8 121 us: carried_in(): gathered = jax.tree.map(lambda a: lax.all_gather(a, axis), part)]
  transfers between devices with their start and end apart: 13 -> 0, of which waited for: 5 -> 0; matrix products, arithmetic and copies ran while one was open for 39% -> 0% of each run, Pallas kernels for 0% -> 0%
where the time goes in v3:
time: 278 us; the launch traced here: 277 us
  Pallas kernels  273 us (98%)
  local copies, waits for them, and re-layouts  3.76 us (1%)
    pallas_call x1, Pallas kernels, run_backward(): pl.pallas_call(functools.partial(backward_kernel, depth, early, late, [le...  87 us
    pallas_call x1, Pallas kernels, run_front(): pl.pallas_call(functools.partial(front_kernel, depth, now, later), grid=(...  72.1 us
    pallas_call x1, Pallas kernels, run_tail(): pl.pallas_call(tail_kernel, grid=(blocks,), in_specs=[pl.BlockSpec((join,...  64.5 us
    pallas_call x1, Pallas kernels, run_mid(): pl.pallas_call(functools.partial(mid_kernel, depth, plan, [len(b) for b i...  45.9 us

profile of v3, /device:TPU:0, one launch (start us, length us, event | category | flops | bytes accessed | tf_op | source)
XLA Modules:
  0.0 277.4 jit_solution(2489879201004941952)
XLA Ops:
  0.7 0.8 stack.12
  1.5 0.8 stack.13
  2.3 0.8 stack.14
  3.2 0.3 copy.66
  3.5 0.3 copy.67
  3.8 0.7 pad.4.ids
  4.5 72.1 %gather_and_front.1 = (f32[4096,1024]{1,0:T(8,128)}, f32[4096,1024]{1,0:T(8,128)}, f32[4096,1024]{1,0:T(8,128)}, bf16[4096,512]{1,0:T(8,128)(2,1)}, bf16[4096,51...) custom-call(s32[8,8,512]{2,1,0:T(8,128)} %pad.4.ids, ...), custom_call_target="tpu_custom_call" | custom-call | tf_op jit(solution)/shard_map/gather_and_front/pallas_call | solution.py:1075
  76.6 64.5 %tail_and_head.1 = (f32[4096,512]{1,0:T(8,128)}, bf16[4096,512]{1,0:T(8,128)(2,1)}, f32[4096,512]{1,0:T(8,128)}, bf16[4096,2048]{1,0:T(8,128)(2,1)}, f32[2048,51...) custom-call(s32[8,8,512]{2,1,0:T(8,128)} %get-tuple-element.86.ids.refs_0_, ...), custom_call_target="tpu_custom_call" | custom-call | tf_op jit(solution)/shard_map/tail_and_head/pallas_call | solution.py:1189
  141.1 45.9 %mid_back_and_reduce.1 = (f32[4096,1024]{1,0:T(8,128)}, f32[512,2048]{1,0:T(8,128)}, f32[1024,512]{1,0:T(8,128)}, f32[256,512]{1,0:T(8,128)}, f32[8,512]{1,0:T(8,128)}, /*index=5*/f32[64,512]{1,0:T(8,128)}) custom-call(s32[8,8,512]{2,1,0:T(8,128)} %get-tuple-element.86.ids.refs_0_, bf16[4096,1024]{1,0:T(8,128)(2,1)} %get-tuple-element.90.state_low.refs_1_, ...), custom_call_target="tpu_custom_call" | custom-call | tf_op jit(solution)/shard_map/mid_back_and_reduce/pallas_call | solution.py:1277
  187.0 87.0 %front_back_and_reduce.1 = (f32[16,2048]{1,0:T(8,128)}, f32[32,512]{1,0:T(8,128)}, f32[16,2048]{1,0:T(8,128)}, f32[8,512]{1,0:T(8,128)}, f32[16,512]{1,0:T(8,128)}, /*index=5*/f32[8,128]{1,0:T(8,128)}) custom-call(s32[8,8,512]{2,1,0:T(8,128)} %get-tuple-element.86.ids.refs_0_, f32[4096,1024]{1,0:T(8,128)} %get-tuple-element.87.refs_1_, ...), custom_call_target="tpu_custom_call" | custom-call | tf_op jit(solution)/shard_map/front_back_and_reduce/pallas_call | solution.py:837
  274.0 3.2 %adam_update.1 = (f32[1,1]{1,0:T(1,128)}, f32[1,1]{1,0:T(1,128)}, f32[1,1]{1,0:T(1,128)}, f32[8,512]{1,0:T(8,128)}, f32[16,2048]{1,0:T(8,128)}, /*index=5*/f32[3...) custom-call(f32[16,512]{1,0:T(8,128)} %get-tuple-element.112.small, ...), custom_call_target="tpu_custom_call" | custom-call | tf_op jit(solution)/shard_map/adam_update/pallas_call | solution.py:1330
  (4 shorter events, 0.0 us)

commit v4 on v3

--- a/solution.py
+++ b/solution.py
@@ -362,6 +362,7 @@
 ROWS = 8
 GELU_A = 0.7978845608028654
 GELU_B = 0.044715
+LOG2E = 1.4426950408889634
 
 
 def nn(left, right):
@@ -533,29 +534,36 @@
 
 
 class Reduce:
-    def __init__(self, plan, depth, sources, resident, outs, bufs, loads, send, recv, at):
-        self.plan, self.depth, self.sources, self.resident = plan, depth, sources, resident
-        self.outs, self.bufs, self.loads, self.send, self.recv = outs, bufs, loads, send, recv
+    def __init__(self, plan, depth, source, resident, out, refs, at):
+        self.plan, self.depth, self.source, self.resident, self.out = plan, depth, source, resident, out
+        self.send, self.recv = refs[:2]
+        if not resident:
+            self.loads, self.own = refs[2:4]
+        first = 2 if resident else 4
+        self.bufs = [refs[first + 3 * i : first + 3 * i + 3] for i in range(len(plan))]
         self.y, self.x, self.z, self.core = at
 
-    def sizes(shape, lo, hi, depth, resident):
-        piece = (shape[-2], hi - lo)
-        whole = pltpu.VMEM((2, 2, depth) + piece, F32)
-        own = [] if resident else [whole]
-        return own + [whole, pltpu.VMEM((2, depth) + piece, F32), pltpu.VMEM((2, depth) + piece, F32)]
+    def scratch(shape, plan, depth, resident):
+        piece = (shape[-2], plan[0][2] - plan[0][1])
+        dma = lambda *n: pltpu.SemaphoreType.DMA(n)
+        own = [] if resident else [dma(len(plan)), pltpu.VMEM((2, 2, depth) + piece, F32)]
+        each = [
+            pltpu.VMEM((2, 2, depth) + piece, F32), pltpu.VMEM((2, depth) + piece, F32), pltpu.VMEM((2, depth) + piece, F32)
+        ]
+        return [dma(len(plan), depth + 2), dma(len(plan), depth + 2)] + own + each * len(plan)
 
     def load(self, i):
         t, lo, hi, _ = self.plan[i]
-        source = self.sources[t].at[:, :, :, self.core, :, pl.ds(lo, hi - lo)]
-        return pltpu.make_async_copy(source, self.bufs[i][0], self.loads.at[i])
+        source = self.source.at[:, :, :, self.core, :, pl.ds(lo, hi - lo)]
+        return pltpu.make_async_copy(source, self.own, self.loads.at[i])
 
     def copies(self, i, phase):
         t, lo, hi, along_x = self.plan[i]
         y, x, z, core = self.y, self.x, self.z, self.core
-        whole, half, quarter = self.bufs[i][-3:]
+        whole, half, quarter = self.bufs[i]
         by_x, by_y = device(y, 1 - x, z, core), device(1 - y, x, z, core)
         if phase == 0:
-            source = self.sources[t].at[:, :, :, 1 - core, :, pl.ds(lo, hi - lo)]
+            source = self.source.at[:, :, :, 1 - core, :, pl.ds(lo, hi - lo)]
             moves = [(source, whole, device(y, x, z, 1 - core))]
         elif phase == 1:
             moves = [(whole.at[1 - y], half, by_y) if along_x else (whole.at[:, 1 - x], half, by_x)]
@@ -571,24 +579,31 @@
             for n, (src, dst, peer) in enumerate(moves)
         ]
 
-    def begin(self, i):
-        for copy in self.copies(i, 0):
-            copy.start()
+    def begin(self):
+        for i in range(len(self.plan)):
+            for copy in self.copies(i, 0):
+                copy.start()
         if not self.resident:
-            self.load(i).start()
+            self.load(0).start()
+
+    def pair(self, n, phase):
+        for i in (2 * n, 2 * n + 1):
+            self.act(i, phase)
 
     def act(self, i, phase):
         t, lo, hi, along_x = self.plan[i]
         y, x, z, core = self.y, self.x, self.z, self.core
-        whole, half, quarter = self.bufs[i][-3:]
+        whole, half, quarter = self.bufs[i]
         for copy in self.copies(i, phase):
             copy.wait_recv()
         if phase == 0:
             if self.resident:
-                add_into(whole, self.sources[t].at[:, :, :, core, :, pl.ds(lo, hi - lo)])
+                add_into(whole, self.source.at[:, :, :, core, :, pl.ds(lo, hi - lo)])
             else:
                 self.load(i).wait()
-                add_into(whole, self.bufs[i][0])
+                add_into(whole, self.own)
+                if i + 1 < len(self.plan):
+                    self.load(i + 1).start()
         elif phase == 1:
             add_into(half, whole.at[y] if along_x else whole.at[:, x])
         elif phase == 2:
@@ -597,7 +612,7 @@
             total = quarter[0, z]
             for dz in range(1, self.depth):
                 total = total + quarter[1, dz]
-            self.outs[t][:, lo:hi] = total
+            self.out[:, lo:hi] = total
             return
         for copy in self.copies(i, phase + 1):
             copy.start()
@@ -652,68 +667,104 @@
         return self.total(self.ways, self.ways + 4)
 
 
+class EverywhereHalved:
+    def __init__(self, whole, parts, sends, recvs, depth, at):
+        y, x, z, core = at
+        self.whole, self.parts, self.depth, self.core = whole, parts, depth, core
+        other = device(y, x, z, 1 - core)
+        self.first = remote(whole.at[0], whole.at[1], sends.at[0], recvs.at[0], other)
+        self.spot = (z, depth + y * 2 + x)
+        self.along, self.plane = [], []
+        mine = parts.at[z]
+        for dz in range(1, depth):
+            peer = device(y, x, (z + dz) % depth, core)
+            self.along.append(remote(mine, mine, sends.at[dz], recvs.at[dz], peer))
+        mine = parts.at[self.spot[1]]
+        for n, (dy, dx) in enumerate(((0, 1), (1, 0), (1, 1))):
+            peer = device((y + dy) % 2, (x + dx) % 2, z, core)
+            self.plane.append(remote(mine, mine, sends.at[depth + n], recvs.at[depth + n], peer))
+        mine = whole.at[2, core]
+        self.last = remote(mine, mine, sends.at[depth + 3], recvs.at[depth + 3], other)
+
+    def total(self, lo, hi):
+        value = self.parts[lo]
+        for n in range(lo + 1, hi):
+            value = value + self.parts[n]
+        return value
+
+    def step(self, n, value=None):
+        if n == 0:
+            self.whole[0] = value.reshape(self.whole.shape[1:])
+            self.first.start()
+        elif n == 1:
+            self.first.wait()
+            lower = self.whole[self.core, self.core] + self.whole[1 - self.core, self.core]
+            self.parts[self.spot[0]] = lower
+            for copy in self.along:
+                copy.start()
+        elif n == 2:
+            for copy in self.along:
+                copy.wait()
+            self.parts[self.spot[1]] = self.total(0, self.depth)
+            for copy in self.plane:
+                copy.start()
+        elif n == 3:
+            for copy in self.plane:
+                copy.wait()
+            self.whole[2, self.core] = self.total(self.depth, self.depth + 4)
+            self.last.start()
+        else:
+            self.last.wait()
+            return self.whole[2].reshape(-1, self.whole.shape[-1])
+
+
 SCHEDULE = {
-    2: [(True, 0, 0), (True, 1, 0)], 3: [(True, 2, 0)], 4: [(True, 0, 1)], 6: [(True, 1, 1)],
-    9: [(True, 2, 1), (False, 0, 0), (False, 1, 0), (True, 0, 2)], 10: [(True, 1, 2)], 12: [(True, 2, 2)], 14: [(False, 0, 1)],
+    1: [(0, 0, 0)], 3: [(0, 1, 0)], 5: [(0, 2, 0)], 7: [(0, 0, 1)], 8: [(0, 3, 0), (0, 1, 1)], 9: [(1, 0, 0)],
+    10: [(0, 0, 2), (0, 2, 1)], 11: [(0, 1, 2), (0, 3, 1)], 13: [(0, 2, 2)], 14: [(0, 3, 2), (1, 0, 1)],
 }
 LEFT_OVER = [
-    (False, 2, 0), (None, 0, 0), (False, 1, 1), (False, 0, 2), (False, 2, 1), (True, 0, 3), (True, 1, 3), (True, 2, 3),
-    (False, 1, 2), (False, 2, 2), (False, 0, 3), (False, 1, 3), (False, 2, 3),
+    (2, 0, 0), (3, 0, 1), (1, 0, 2), (2, 0, 1), (3, 0, 2), (2, 0, 2), (3, 0, 3), (0, 0, 3), (0, 1, 3), (0, 2, 3), (0, 3, 3),
+    (1, 0, 3), (2, 0, 3),
 ]
 
 
-def backward_kernel(depth, early, late, sizes, *refs):
-    ids, keep, p, q, ds, conv, queue, tab, gains, taps, w_in, g_tab_a, g_tab_b, small_in, r_down = refs[:15]
-    sources = refs[15:17]
-    outs = tuple(refs[17:21])
-    small_o, squares_o = refs[21:23]
-    small, g_in, g_tab, d_pre, ext, head_s, carry_s, hot_sum = refs[23:31]
-    loads, early_send, early_recv, late_send, late_recv, slots, sq_slots, sends, recvs, sq_sends, sq_recvs = refs[31:42]
-    at = 42
-    held = []
-    for n in sizes:
-        held.append(refs[at : at + n])
-        at += n
+def last_kernel(depth, plans, counts, *refs):
+    ids, d_pre, state_low, mixed_low, tab, gains, taps, w_in, g_tab_a, g_tab_b, small_in, r_down, r_up, g_in = refs[:14]
+    r_in, r_out, r_tab, small_o, squares_o = refs[14:19]
+    small, g_out, g_tab, qtab, ext, head_s, hot_sum = refs[19:26]
+    whole_s, part_s, sq_slots, sends, recvs, sq_sends, sq_recvs = refs[26:33]
     spot = place()
-    first_sums = Reduce(
-        early, depth, sources, False, outs[:2], held[: len(early)], loads, early_send, early_recv, spot
-    )
-    last_sums = Reduce(
-        late, depth, (g_in, g_tab), True, outs[2:], held[len(early) :], None, late_send, late_recv, spot
-    )
-    smalls = Everywhere(slots, sends, recvs, depth, spot)
+    sums, at = [], 33
+    for n, (source, out) in enumerate(((g_in, r_in), (g_out, r_out), (g_tab, r_tab))):
+        sums.append(Reduce(plans[n], depth, source, n > 0, out, refs[at : at + counts[n]], spot))
+        at += counts[n]
+    smalls = EverywhereHalved(whole_s, part_s, sends, recvs, depth, spot)
     squares = Everywhere(sq_slots, sq_sends, sq_recvs, depth, spot)
-    early_groups, late_groups = grouped(early), grouped(late)
     step = pl.program_id(0)
     blocks = pl.num_programs(0) // 2
-    rows, hidden = keep.shape
+    rows = d_pre.shape[0]
     vocab, width = tab.shape
     kernel = taps.shape[0]
     rim = (kernel - 1) * ROWS
-    steps = rows // ROWS
-    bias_rows = hidden // width
-    base = ROWS + kernel
 
     def run(acts):
-        for is_early, group, phase in acts:
-            if is_early is None:
-                smalls.middle()
-                continue
-            sums, groups = (first_sums, early_groups) if is_early else (last_sums, late_groups)
-            for i in groups[group]:
-                sums.act(i, phase)
+        for n, pair, phase in acts:
+            if n == 3:
+                smalls.step(phase)
+            else:
+                sums[n].pair(pair, phase)
 
     @pl.when(step == 0)
     def _():
         greet(*spot, depth)
-        for i in range(len(early)):
-            first_sums.begin(i)
-        g_in[...] = jnp.zeros_like(g_in)
+        sums[0].begin()
+        wide = tab[...].astype(BF).astype(F32)
+        qtab[...] = (wide * inv_rms(wide) * gains[0:1]).astype(BF)
+        g_out[...] = jnp.zeros_like(g_out)
         hot_sum[...] = jnp.zeros_like(hot_sum)
         small[...] = jnp.zeros_like(small)
         small[0:ROWS, :] = small_in[...]
         head_s[...] = jnp.zeros_like(head_s)
-        carry_s[...] = jnp.zeros_like(carry_s)
 
     for when, acts in SCHEDULE.items():
 
@@ -723,52 +774,15 @@
 
     @pl.when(step < blocks)
     def _():
-        low_half = lax.broadcasted_iota(jnp.int32, (ROWS, hidden), 0) < ROWS // 2
-        carry = carry_s[...]
-        block = blocks - 1 - step
-
-        def scan_one(i, reached):
-            at = pl.ds(pl.multiple_of((steps - 1 - i) * ROWS, ROWS), ROWS)
-            return keep[at, :] * (ds[at, :] + reached)
-
-        first = lax.fori_loop(0, steps, scan_one, carry, unroll=8)
-
-        def scan_two(i, state):
-            reached, total = state
-            pair = steps // 2 - 1 - i
-            gates, cands = [None, None], [None, None]
-            for half_step in (1, 0):
-                at = pl.ds(pl.multiple_of(pair * 2 * ROWS + half_step * ROWS, ROWS), ROWS)
-                lam = ds[at, :] + reached
-                reached = keep[at, :] * lam
-                gates[half_step] = lam * p[at, :]
-                cands[half_step] = lam * q[at, :]
-                total = total + gates[half_step]
-            both = pl.ds(pl.multiple_of(pair * 2 * ROWS, 2 * ROWS), 2 * ROWS)
-            d_pre[block, both, 0:hidden] = jnp.concatenate(gates, axis=0).astype(BF)
-            d_pre[block, both, hidden : 2 * hidden] = jnp.concatenate(cands, axis=0).astype(BF)
-            return reached, total
-
-        entry = jnp.where(low_half, swap_halves(first), carry)
-        last, total = lax.fori_loop(
-            0, steps // 2, scan_two, (entry, jnp.zeros((ROWS, hidden), F32)), unroll=4
-        )
-        carry_s[...] = jnp.where(low_half, 0.0, swap_halves(last))
-        d_bias = column_sum(total)
-        for r in range(bias_rows):
-            small[base + r : base + r + 1, :] += d_bias[:, r * width : (r + 1) * width]
-        g_in[...] += tn(conv[...], d_pre[block]).reshape(g_in.shape)
+        g_out[...] += tn(state_low[...], mixed_low[...]).reshape(g_out.shape)
 
     @pl.when(step == blocks - 1)
     def _():
-        for group in late_groups[:2]:
-            for i in group:
-                last_sums.begin(i)
+        sums[1].begin()
 
     @pl.when(step >= blocks)
     def _():
-        block = 2 * blocks - 1 - step
-        ext[0:rows, :] = nt(d_pre[block], w_in[...])
+        ext[0:rows, :] = nt(d_pre[...], w_in[...])
         half = lax.broadcasted_iota(jnp.int32, (rim, width), 0) % ROWS < ROWS // 2
         mine = ext[0:rim, :]
         ext[rows:, :] = jnp.where(
@@ -777,7 +791,8 @@
             swap_halves(head_s[...].reshape(kernel - 1, ROWS, width)).reshape(rim, width),
         )
         head_s[...] = mine
-        known = queue[...].astype(F32)
+        here = ids[0]
+        known = nn(one_hot(here.T[:, 0:1], vocab), qtab[...])
         d_queue = None
         for k in range(kernel):
             shift = (kernel - 1 - k) * ROWS
@@ -785,7 +800,7 @@
             term = taps[k : k + 1] * part
             d_queue = term if d_queue is None else d_queue + term
             small[ROWS + k : ROWS + k + 1, :] += column_sum(part * known)
-        hot_t = one_hot_t(ids[0][0:1, :], vocab)
+        hot_t = one_hot_t(here[0:1, :], vocab)
         hot_sum[...] += nn(hot_t, d_queue.astype(BF))
 
     @pl.when(step == 2 * blocks - 1)
@@ -793,94 +808,84 @@
         wide = tab[...].astype(BF).astype(F32)
         inverse = inv_rms(wide)
         total = hot_sum[...]
-        small[0:1, :] = column_sum(total * (wide * inverse))
-        smalls.begin(small[...])
         g_tab[...] = (
             g_tab_a[...] + g_tab_b[...] + norm_back(wide, inverse, gains[0:1], total)
         ).reshape(g_tab.shape)
-        for i in late_groups[2]:
-            last_sums.begin(i)
+        sums[2].begin()
+        small[0:1, :] = column_sum(total * (wide * inverse))
+        smalls.step(0, small[...])
         run(LEFT_OVER)
-        small_o[...] = smalls.end()
         square = jnp.zeros((1, 1), F32)
-        for out in outs + (r_down,):
+        for out in (r_in, r_out, r_tab, r_down, r_up):
             value = out[...]
             square = square + jnp.sum(jnp.sum(value * value, axis=1, keepdims=True), axis=0, keepdims=True)
         squares.begin(jnp.broadcast_to(square, (ROWS, LANES)))
+        small_o[...] = smalls.step(4)
         squares.middle()
         squares_o[...] = squares.end()
-        first_sums.finish()
-        last_sums.finish()
-
-
-def run_backward(depth, ids, keep, p, q, ds, conv, queue, tab, gains, taps, w_in, g_tabs, small, r_down, grads):
+        for one in sums:
+            one.finish()
+
+
+def run_last(depth, ids, d_pre, state_low, mixed_low, tab, gains, taps, w_in, g_tabs, small, done, g_in):
     blocks, _, rows = ids.shape
     vocab, width = tab.shape
-    hidden = keep.shape[1]
     kernel = taps.shape[0]
     rim = (kernel - 1) * ROWS
     last = blocks - 1
-    wide = pl.BlockSpec((rows, hidden), lambda i: (jnp.maximum(last - i, 0), 0))
-    front = pl.BlockSpec((rows, width), lambda i: (jnp.maximum(last - i, 0), 0))
-    back = pl.BlockSpec((rows, width), lambda i: (jnp.minimum(2 * blocks - 1 - i, last), 0))
-    back_ids = pl.BlockSpec((1, ROWS, rows), lambda i: (jnp.minimum(2 * blocks - 1 - i, last), 0, 0))
     owners = (2, 2, depth, 2)
-    early_shapes = [g.shape for g in grads]
-    late_shapes = [owners + (width // (8 * depth), 2 * hidden), owners + (vocab // (8 * depth), width)]
-    early, late = halves(early_shapes, (2, 1)), halves(late_shapes, (2, 1))
-    bufs = [Reduce.sizes(early_shapes[t], lo, hi, depth, False) for t, lo, hi, _ in early]
-    bufs += [Reduce.sizes(late_shapes[t], lo, hi, depth, True) for t, lo, hi, _ in late]
-    any_spec = pl.BlockSpec(memory_space=pl.ANY)
-    out = [s[-2:] for s in early_shapes + late_shapes] + [(2 * ROWS, width), (ROWS, LANES)]
+    hidden = state_low.shape[1]
+    shapes = (g_in.shape, owners + (hidden // (8 * depth), width), owners + (vocab // (8 * depth), width))
+    plans = [halves([shape], (cuts,)) for shape, cuts in zip(shapes, (4, 1, 1))]
+    back = lambda i: jnp.minimum(2 * blocks - 1 - i, last)
+    once = lambda cols: pl.BlockSpec((rows, cols), lambda i: (jnp.minimum(i, last), 0))
+    moving = [Reduce.scratch(shape, plan, depth, n > 0) for n, (shape, plan) in enumerate(zip(shapes, plans))]
+    out = [s[-2:] for s in shapes] + [(2 * ROWS, width), (ROWS, LANES)]
     dma = lambda *shape: pltpu.SemaphoreType.DMA(shape)
-    fixed = (tab, gains, taps, w_in) + tuple(g_tabs) + (small, r_down)
+    fixed = (tab, gains, taps, w_in) + tuple(g_tabs) + (small,) + tuple(done)
     return pl.pallas_call(
-        functools.partial(backward_kernel, depth, early, late, [len(b) for b in bufs]),
+        functools.partial(last_kernel, depth, plans, [len(m) for m in moving]),
         grid=(2 * blocks,),
-        in_specs=[back_ids, wide, wide, wide, wide, front, back]
+        in_specs=[
+            pl.BlockSpec((1, ROWS, rows), lambda i: (back(i), 0, 0)),
+            pl.BlockSpec((rows, d_pre.shape[1]), lambda i: (back(i), 0)),
+            once(hidden),
+            once(width),
+        ]
         + [whole(a.shape) for a in fixed]
-        + [any_spec] * len(grads),
+        + [pl.BlockSpec(memory_space=pl.ANY)],
         out_specs=[whole(s) for s in out],
         out_shape=[jax.ShapeDtypeStruct(s, F32) for s in out],
         scratch_shapes=[
             pltpu.VMEM((2 * ROWS, width), F32),
-            pltpu.VMEM(late_shapes[0], F32),
-            pltpu.VMEM(late_shapes[1], F32),
-            pltpu.VMEM((blocks, rows, 2 * hidden), BF),
+            pltpu.VMEM(shapes[1], F32),
+            pltpu.VMEM(shapes[2], F32),
+            pltpu.VMEM((vocab, width), BF),
             pltpu.VMEM((rim + rows, width), F32),
             pltpu.VMEM((rim, width), F32),
-            pltpu.VMEM((ROWS, hidden), F32),
             pltpu.VMEM((vocab, width), F32),
-            dma(len(early)),
-            dma(len(early), depth + 2),
-            dma(len(early), depth + 2),
-            dma(len(late), depth + 2),
-            dma(len(late), depth + 2),
-            pltpu.VMEM((2 * depth + 4, 2 * ROWS, width), F32),
+            pltpu.VMEM((3, 2, ROWS, width), F32),
+            pltpu.VMEM((depth + 4, ROWS, width), F32),
             pltpu.VMEM((2 * depth + 4, ROWS, LANES), F32),
-            dma(2 * depth + 4),
-            dma(2 * depth + 4),
+            dma(depth + 4),
+            dma(depth + 4),
             dma(2 * depth + 4),
             dma(2 * depth + 4),
         ]
-        + [b for group in bufs for b in group],
+        + [piece for group in moving for piece in group],
         compiler_params=pltpu.CompilerParams(
-            dimension_semantics=("arbitrary",), collective_id=1, has_side_effects=True, vmem_limit_bytes=63 * MIB
+            dimension_semantics=("arbitrary",), collective_id=1, has_side_effects=True, vmem_limit_bytes=62 * MIB
         ),
-        name="front_back_and_reduce",
-    )(ids, keep, p, q, ds, conv, queue, *fixed, *grads)
-
-
-def front_block(ids, qtab, taps, bias, w_in, keep_o, p_o, q_o, conv_o, queue_o, state_o, padq, tail_s, carry_s, big):
-    rows, hidden = keep_o.shape
-    vocab, width = qtab.shape
+        name="last_back_and_reduce",
+    )(ids, d_pre, state_low, mixed_low, *fixed, g_in)
+
+
+def conv_block(block, ids_s, qtab, taps, conv_s, padq, tail_s):
+    _, rows, width = conv_s.shape
+    vocab = qtab.shape[0]
     kernel = taps.shape[0]
     rim = (kernel - 1) * ROWS
-    steps = rows // ROWS
-    chunk = 256
-    hot = one_hot(ids.T[:, 0:1], vocab)
-    queue = nn(hot, qtab[...])
-    queue_o[...] = queue.astype(BF)
+    queue = nn(one_hot(id_column(ids_s[block], 0), vocab), qtab[...])
     padq[rim:, :] = queue
     half = lax.broadcasted_iota(jnp.int32, (rim, width), 0) % ROWS < ROWS // 2
     before = tail_s[...].reshape(kernel - 1, ROWS, width)
@@ -892,69 +897,69 @@
     conv = taps[0:1] * padq[0:rows, :]
     for k in range(1, kernel):
         conv = conv + taps[k : k + 1] * padq[k * ROWS : k * ROWS + rows, :]
-    conv_o[...] = conv.astype(BF)
-
+    conv_s[block] = conv.astype(BF)
+
+
+def id_column(ids, which):
+    turned = ids.T
+    return jnp.concatenate([turned[:, 2 * which : 2 * which + 1], turned[:, 2 * which + 1 : 2 * which + 2]], axis=0)
+
+
+def front_block(conv, bias, w_in, keep_o, p_o, q_o, state_o, carry_s, big):
+    rows, hidden = keep_o.shape
+    steps = rows // ROWS
+    chunk = 256
+    low_half = lax.broadcasted_iota(jnp.int32, (ROWS, chunk), 0) < ROWS // 2
     for j in range(hidden // chunk):
         cols = slice(j * chunk, (j + 1) * chunk)
-        gate = nn(conv_o[...], w_in[:, j * chunk : (j + 1) * chunk]) + bias[0:1, cols]
-        cand = nn(conv_o[...], w_in[:, hidden + j * chunk : hidden + (j + 1) * chunk])
-        eg = jnp.exp(-jnp.abs(gate))
-        rg = pl.reciprocal(1.0 + eg)
-        sg = eg * rg
-        up = gate >= 0
-        write_gate = jnp.where(up, rg, sg)
-        keep_o[:, cols] = jnp.where(up, sg, rg)
-        ec = jnp.exp(-jnp.abs(cand))
-        rc = pl.reciprocal(1.0 + ec)
-        slope = jnp.where(cand >= 0, rc, ec * rc)
-        soft = jnp.maximum(cand, 0.0) + jnp.where(
-            ec < 1e-3, ec * (1.0 - 0.5 * ec), jnp.log(1.0 + ec)
-        )
+        gate = nn(conv[...], w_in[:, j * chunk : (j + 1) * chunk]) + bias[0:1, cols]
+        cand = nn(conv[...], w_in[:, hidden + j * chunk : hidden + (j + 1) * chunk])
+        grown = jnp.exp2(jnp.minimum(gate * -LOG2E, 120.0))
+        write_gate = pl.reciprocal(1.0 + grown)
+        keep_o[:, cols] = grown * write_gate
+        small = jnp.exp2(jnp.abs(cand) * -LOG2E)
+        one_more = 1.0 + small
+        soft = jnp.maximum(cand, 0.0) + (jnp.log(one_more) + (small - (one_more - 1.0)))
         p_o[:, cols] = write_gate
-        q_o[:, cols] = write_gate * slope
+        q_o[:, cols] = write_gate * jnp.exp2((cand - soft) * LOG2E)
         big[:, cols] = write_gate * soft
 
-    low_half = lax.broadcasted_iota(jnp.int32, (ROWS, hidden), 0) < ROWS // 2
-    carry = carry_s[...]
-
-    def scan_one(tau, state):
-        at = pl.ds(pl.multiple_of(tau * ROWS, ROWS), ROWS)
-        return keep_o[at, :] * state + big[at, :]
-
-    end = lax.fori_loop(0, steps, scan_one, carry, unroll=8)
-
-    def scan_two(pair, state):
-        lows = []
-        for half_step in range(2):
-            at = pl.ds(pl.multiple_of(pair * 2 * ROWS + half_step * ROWS, ROWS), ROWS)
-            keep, write = keep_o[at, :], big[at, :]
-            p_o[at, :] = keep * (write - p_o[at, :] * state)
-            state = keep * state + write
-            lows.append(state)
-        both = pl.ds(pl.multiple_of(pair * 2 * ROWS, 2 * ROWS), 2 * ROWS)
-        state_o[both, :] = jnp.concatenate(lows, axis=0).astype(BF)
-        return state
-
-    last = lax.fori_loop(0, steps // 2, scan_two, jnp.where(low_half, carry, swap_halves(end)), unroll=4)
-    carry_s[...] = jnp.where(low_half, swap_halves(last), 0.0)
-
-
-GATHER_SCHEDULE = {1: [(0, 0), (1, 0)], 2: [(2, 0), (0, 1)], 3: [(1, 1)], 4: [(2, 1), (0, 2)], 5: [(1, 2)], 6: [(2, 2)]}
-GATHER_LAST = [(0, 3), (1, 3), (2, 3)]
+        carry = carry_s[:, cols]
+        end = carry
+        for tau in range(steps):
+            at = slice(tau * ROWS, (tau + 1) * ROWS)
+            end = keep_o[at, cols] * end + big[at, cols]
+        state = jnp.where(low_half, carry, swap_halves(end))
+        for tau in range(steps):
+            at = slice(tau * ROWS, (tau + 1) * ROWS)
+            change = big[at, cols] - p_o[at, cols] * state
+            p_o[at, cols] = keep_o[at, cols] * change
+            state = state + change
+            big[at, cols] = state
+        state_o[:, cols] = big[:, cols].astype(BF)
+        carry_s[:, cols] = jnp.where(low_half, swap_halves(state), 0.0)
+
+
+GATHER_SCHEDULE = {1: [(2, 0), (0, 1)], 2: [(1, 1), (3, 0), (4, 0)], 3: [(2, 1), (0, 2)], 4: [(3, 1), (1, 2)], 5: [(4, 1), (2, 2)], 6: [(3, 2)], 7: [(4, 2)]}
+GATHER_LAST = [(0, 3), (1, 3), (2, 3), (3, 3), (4, 3)]
 
 
 def front_kernel(
     depth, now, later,
     ids, table, w_in, w_out, w_up, w_down, gains, taps, bias,
-    keep_o, p_o, q_o, conv_o, queue_o, state_o, ids_o, tab_o, count_o, w_in_o, w_out_o, w_up_o, w_down_o,
-    ids_s, tab_s, count_s, in_s, out_s, up_s, down_s, qtab, padq, tail_s, carry_s, big,
+    keep_o, p_o, q_o, state_o, ids_o, tab_o, count_o, conv_o, w_in_o, w_out_o, w_up_o, w_down_o,
+    ids_s, tab_s, count_s, in_s, out_s, up_s, down_s, qtab, conv_s, padq, tail_s, carry_s, big,
     ids_send, ids_recv, now_send, now_recv, later_send, later_recv, own_sem, in_sem,
 ):
     step = pl.program_id(0)
+    blocks = pl.num_programs(0)
     spot = place()
     y, x, z, core = spot
     me = z * 2 + core
-    wait_in = pltpu.make_async_copy(in_s, w_in_o, in_sem)
+    onward = [
+        pltpu.make_async_copy(in_s, w_in_o, in_sem.at[0]),
+        pltpu.make_async_copy(conv_s, conv_o, in_sem.at[1]),
+    ]
     first = Gather(now, depth, [None] * 3, [tab_s, count_s, in_s], now_send, now_recv, spot)
     rest = Gather(later, depth, [out_s, up_s, down_s], [w_out_o, w_up_o, w_down_o], later_send, later_recv, spot)
     later_groups = grouped(later)
@@ -974,45 +979,92 @@
 
     @pl.when(step == 0)
     def _():
-        tab_s[y, x, z, core] = table[...]
-        share = jnp.zeros((1, ids.shape[2]), F32)
+        half = table.shape[1] // 2
+        tab_s[y, x, z, core] = jnp.concatenate([table[:, 0:half], table[:, half:]], axis=0).astype(BF)
+        share = jnp.zeros((2, ids.shape[2]), F32)
         for n in range(ids.shape[0]):
-            share = share + ids[n, 2:3, :].astype(F32)
-        count_s[y, x, z, core] = jnp.broadcast_to(jnp.sum(share, axis=1, keepdims=True), count_o.shape)
+            share = share + ids[n, 4:6, :].astype(F32)
+        share = jnp.sum(jnp.sum(share, axis=1, keepdims=True), axis=0, keepdims=True)
+        count_s[y, x, z, core] = jnp.broadcast_to(share, count_o.shape)
         in_s[y, x, z, core] = w_in[...].astype(BF)
+        ids_s[me] = ids[me]
         greet(*spot, depth)
-        for i in range(len(now)):
-            first.begin(i)
+        pairs = [(i, i + 1) for i in range(0, len(now), 2)]
+
+        def act(pair, phase):
+            for i in pairs[pair]:
+                first.act(i, phase)
+
+        def begin(pair):
+            for i in pairs[pair]:
+                first.begin(i)
+
+        begin(0)
         for copy in spread:
             copy.start()
+        begin(1)
+        begin(2)
+        act(0, 0)
         out_s[...] = w_out[...].astype(BF)
         up_s[...] = w_up[...].astype(BF)
         down_s[...] = w_down[...].astype(BF)
         for copy in own:
             copy.start()
-        ids_s[me] = ids[me]
-        for i in range(len(now)):
-            first.act(i, 0)
+        act(1, 0)
+        begin(3)
+        act(0, 1)
+        act(2, 0)
+        begin(4)
+        act(1, 1)
+        act(0, 2)
+        act(3, 0)
+        act(2, 1)
+        act(4, 0)
         for i in range(len(later)):
             rest.begin(i)
-        for phase in range(1, 4):
-            for i in range(len(now)):
-                first.act(i, phase)
-        wait_in.start()
+        act(1, 2)
+        act(0, 3)
+        act(3, 1)
         for copy in spread:
             copy.wait_recv()
-        tab = tab_s[...].reshape(tab_o.shape)
+        wide = tab_s[...].astype(F32).reshape(-1, 2 * ROWS, half)
+        tab = jnp.concatenate([wide[:, 0:ROWS], wide[:, ROWS:]], axis=-1).reshape(tab_o.shape)
         tab_o[...] = tab
-        wide = tab.astype(BF).astype(F32)
-        qtab[...] = (wide * inv_rms(wide) * gains[0:1]).astype(BF)
+        qtab[...] = (tab * inv_rms(tab) * gains[0:1]).astype(BF)
+        tail_s[...] = jnp.zeros_like(tail_s)
+        carry_s[...] = jnp.zeros_like(carry_s)
+
+        def convolve(lo, hi):
+            def one(block, _):
+                conv_block(block, ids_s, qtab, taps, conv_s, padq, tail_s)
+                return _
+
+            lax.fori_loop(lo, hi, one, 0)
+
+        for copy in own:
+            copy.wait()
+        convolve(0, 2)
+        act(2, 2)
+        act(4, 1)
+        convolve(2, 4)
+        for i in later_groups[0]:
+            rest.act(i, 0)
+        act(1, 3)
+        act(3, 2)
+        convolve(4, 6)
+        act(4, 2)
+        act(2, 3)
+        convolve(6, 8)
+        for i in later_groups[1]:
+            rest.act(i, 0)
+        onward[1].start()
         total = jnp.zeros(count_o.shape, F32)
         for n in range(8 * depth):
             total = total + count_s[n // (4 * depth), n // (2 * depth) % 2, n // 2 % depth, n % 2]
         count_o[...] = total
-        tail_s[...] = jnp.zeros_like(tail_s)
-        carry_s[...] = jnp.zeros_like(carry_s)
-        for copy in own:
-            copy.wait()
+        act(3, 3)
+        act(4, 3)
+        onward[0].start()
 
     for when, acts in GATHER_SCHEDULE.items():
 
@@ -1023,17 +1075,18 @@
                     rest.act(i, phase)
 
     here = ids_s[step]
-    ids_o[0] = here
-    front_block(
-        here, qtab, taps, bias, FlatRows(in_s), keep_o, p_o, q_o, conv_o, queue_o, state_o, padq, tail_s, carry_s, big
-    )
-
-    @pl.when(step == pl.num_programs(0) - 1)
+    for n in range(3):
+        ids_o[0, n : n + 1, :] = jnp.concatenate([here[2 * n : 2 * n + 1, :], here[2 * n + 1 : 2 * n + 2, :]], axis=1)
+    ids_o[0, 3:, :] = jnp.zeros((ROWS - 3, ids_o.shape[2]), jnp.int32)
+    front_block(conv_s.at[step], bias, FlatRows(in_s), keep_o, p_o, q_o, state_o, carry_s, big)
+
+    @pl.when(step == blocks - 1)
     def _():
         for group, phase in GATHER_LAST:
             for i in later_groups[group]:
                 rest.act(i, phase)
-        wait_in.wait()
+        for copy in onward:
+            copy.wait()
         for copy in spread:
             copy.wait_send()
         first.finish()
@@ -1051,7 +1104,8 @@
 
 
 def run_front(depth, ids, table, mats, gains, taps, bias):
-    blocks, _, rows = ids.shape
+    blocks, _, half = ids.shape
+    rows = 2 * half
     w_in, w_out, w_up, w_down = mats
     width = table.shape[1]
     hidden = bias.shape[1]
@@ -1062,12 +1116,11 @@
     devices = 8 * depth
     vocab = devices * table.shape[0]
     cols = w_in.shape[1]
-    now = [(0, 0, width, True), (1, 0, LANES, False)]
-    for n in range(4):
-        now.append((2, n * cols // 4, (n + 1) * cols // 4, n % 2 == 0))
-    later = halves([a.shape for a in (w_out, w_up, w_down)])
+    now = [(0, 0, width // 2, True), (1, 0, LANES, False)]
+    for n in range(8):
+        now.append((2, n * cols // 8, (n + 1) * cols // 8, n % 2 == 0))
+    later = halves([a.shape for a in (w_out, w_up, w_down)], (1, 2, 2))
     wide = pl.BlockSpec((rows, hidden), lambda i: (i, 0))
-    thin = pl.BlockSpec((rows, width), lambda i: (i, 0))
     any_spec = pl.BlockSpec(memory_space=pl.ANY)
     dma = lambda *shape: pltpu.SemaphoreType.DMA(shape)
     args = (ids, table, w_in, w_out, w_up, w_down, gains, taps, bias)
@@ -1076,22 +1129,23 @@
         functools.partial(front_kernel, depth, now, later),
         grid=(blocks,),
         in_specs=[whole(a.shape) for a in args],
-        out_specs=[wide] * 3 + [thin, thin, wide]
+        out_specs=[wide] * 4
         + [pl.BlockSpec((1, ROWS, rows), lambda i: (i, 0, 0)), whole((vocab, width)), whole((ROWS, LANES))]
-        + [any_spec] * 4,
+        + [any_spec] * 5,
         out_shape=[struct((total, hidden), F32)] * 3
-        + [struct((total, width), BF)] * 2
-        + [struct((total, hidden), BF), struct(ids.shape, jnp.int32), struct((vocab, width), F32), struct((ROWS, LANES), F32)]
+        + [struct((total, hidden), BF), struct((blocks, ROWS, rows), jnp.int32), struct((vocab, width), F32)]
+        + [struct((ROWS, LANES), F32), struct((blocks, rows, width), BF)]
         + [struct(owners + a.shape, BF) for a in mats],
         scratch_shapes=[
             pltpu.VMEM(ids.shape, jnp.int32),
-            pltpu.VMEM(owners + table.shape, F32),
+            pltpu.VMEM(owners + (2 * ROWS, width // 2), BF),
             pltpu.VMEM(owners + (ROWS, LANES), F32),
             pltpu.VMEM(owners + w_in.shape, BF),
             pltpu.VMEM(w_out.shape, BF),
             pltpu.VMEM(w_up.shape, BF),
             pltpu.VMEM(w_down.shape, BF),
             pltpu.VMEM((vocab, width), BF),
+            pltpu.VMEM((blocks, rows, width), BF),
             pltpu.VMEM((rim + rows, width), F32),
             pltpu.VMEM((rim, width), F32),
             pltpu.VMEM((ROWS, hidden), F32),
@@ -1103,7 +1157,7 @@
             dma(len(later), depth + 2),
             dma(len(later), depth + 2),
             dma(3),
-            pltpu.SemaphoreType.DMA,
+            dma(2),
         ],
         compiler_params=pltpu.CompilerParams(
             dimension_semantics=("arbitrary",), collective_id=0, has_side_effects=True, vmem_limit_bytes=60 * MIB
@@ -1206,90 +1260,143 @@
     )(ids, state_low, tab, count, gains, w_out, w_up, w_down)
 
 
-DOWN_SCHEDULE = {1: [(0, 0), (1, 0)], 3: [(0, 1)], 4: [(1, 1)], 5: [(0, 2)], 6: [(1, 2)]}
-
-
-def mid_kernel(depth, plan, sizes, *refs):
-    ids, state_low, mixed, normed, final, lifted, gains, w_out, w_up, small_in, g_down = refs[:11]
-    ds_o, g_up, g_out, g_emb, small_o, r_down = refs[11:17]
-    loads, send, recv = refs[17:20]
-    bufs, at = [], 20
-    for n in sizes:
-        bufs.append(refs[at : at + n])
-        at += n
+MID_SCHEDULE = {
+    3: [(0, 0, 0), (0, 1, 0)], 8: [(0, 0, 1)], 9: [(0, 1, 1), (1, 0, 0), (1, 1, 0), (0, 0, 2)],
+    10: [(0, 1, 2)], 11: [(1, 0, 1)], 12: [(1, 1, 1)], 13: [(1, 0, 2), (1, 1, 2)],
+}
+MID_LAST = [(0, 0, 3), (0, 1, 3), (1, 0, 3), (1, 1, 3)]
+
+
+def mid_kernel(depth, plans, counts, *refs):
+    ids, mixed, normed, final, lifted, keep, p, q, conv, gains, w_out, w_up, small_in, g_down = refs[:14]
+    d_pre, mixed_o, g_in, g_emb, small_o, r_down, r_up = refs[14:21]
+    g_up, ds, cand, carry_s = refs[21:25]
     step = pl.program_id(0)
-    last = pl.num_programs(0) - 1
+    blocks = pl.num_programs(0) // 2
     spot = place()
-    sums = Reduce(plan, depth, (g_down,), False, (r_down,), bufs, loads, send, recv, spot)
-    groups = grouped(plan)
-    vocab = g_emb.shape[0]
+    sums, at = [], 25
+    for n, (source, out) in enumerate(((g_down, r_down), (g_up, r_up))):
+        sums.append(Reduce(plans[n], depth, source, n > 0, out, refs[at : at + counts[n]], spot))
+        at += counts[n]
+    vocab, width = g_emb.shape
+    rows, hidden = keep.shape
+    steps = rows // ROWS
+    chunk = 256
+
+    def run(acts):
+        for n, pair, phase in acts:
+            sums[n].pair(pair, phase)
 
     @pl.when(step == 0)
     def _():
         greet(*spot, depth)
-        for i in range(len(plan)):
-            sums.begin(i)
+        sums[0].begin()
         g_up[...] = jnp.zeros_like(g_up)
-        g_out[...] = jnp.zeros_like(g_out)
+        g_in[...] = jnp.zeros_like(g_in)
         g_emb[...] = jnp.zeros_like(g_emb)
         small_o[...] = small_in[...]
-
-    for when, acts in DOWN_SCHEDULE.items():
+        carry_s[...] = jnp.zeros_like(carry_s)
+
+    for when, acts in MID_SCHEDULE.items():
 
         @pl.when(step == when)
         def _(acts=acts):
-            for group, phase in acts:
-                for i in groups[group]:
-                    sums.act(i, phase)
-
-    d_normed = nt(lifted[...], w_up[...])
-    g_up[...] += tn(normed[...], lifted[...])
-    value = mixed[...]
-    inverse = inv_rms(value)
-    small_o[1:2, :] += column_sum(d_normed * (value * inverse))
-    d_mixed = final[...] + norm_back(value, inverse, gains[1:2], d_normed)
-    mixed_low = d_mixed.astype(BF)
-    rest = (d_mixed - mixed_low.astype(F32)).astype(BF)
-    ds_o[...] = nt(mixed_low, w_out[...])
-    g_out[...] += tn(state_low[...], mixed_low)
-    row = jnp.concatenate([ids[n, 0:1, :] for n in range(ids.shape[0])], axis=1)
-    hot_t = one_hot_t(row, vocab)
-    g_emb[...] += nn(hot_t, mixed_low) + nn(hot_t, rest)
-
-    @pl.when(step == last)
+            run(acts)
+
+    @pl.when(step < blocks)
     def _():
-        for group in groups:
-            for i in group:
-                sums.act(i, 3)
-        sums.finish()
-
-
-def run_mid(depth, ids, state_low, mixed, normed, final, lifted, gains, w_out, w_up, small, g_down, vocab):
+        g_up[...] += tn(normed[...], lifted[...]).reshape(g_up.shape)
+
+    @pl.when(step == blocks - 1)
+    def _():
+        sums[1].begin()
+
+    @pl.when(step >= blocks)
+    def _():
+        d_normed = nt(lifted[...], w_up[...])
+        value = mixed[...]
+        inverse = inv_rms(value)
+        small_o[1:2, :] += column_sum(d_normed * (value * inverse))
+        d_mixed = final[...] + norm_back(value, inverse, gains[1:2], d_normed)
+        mixed_low = d_mixed.astype(BF)
+        rest = (d_mixed - mixed_low.astype(F32)).astype(BF)
+        ds[...] = nt(mixed_low, w_out[...])
+        hot_t = one_hot_t(ids[0][0:1, :], vocab)
+        g_emb[...] += nn(hot_t, mixed_low) + nn(hot_t, rest)
+        mixed_o[...] = mixed_low
+
+        low_half = lax.broadcasted_iota(jnp.int32, (ROWS, chunk), 0) < ROWS // 2
+        for j in range(hidden // chunk):
+            cols = slice(j * chunk, (j + 1) * chunk)
+            carry = carry_s[:, cols]
+            first = carry
+            for tau in reversed(range(steps)):
+                at = slice(tau * ROWS, (tau + 1) * ROWS)
+                first = keep[at, cols] * (ds[at, cols] + first)
+            reached = jnp.where(low_half, swap_halves(first), carry)
+            total = jnp.zeros((ROWS, chunk), F32)
+            for tau in reversed(range(steps)):
+                at = slice(tau * ROWS, (tau + 1) * ROWS)
+                lam = ds[at, cols] + reached
+                reached = keep[at, cols] * lam
+                d_gate = lam * p[at, cols]
+                ds[at, cols] = d_gate
+                cand[at, :] = lam * q[at, cols]
+                total = total + d_gate
+            d_pre[:, j * chunk : (j + 1) * chunk] = ds[:, cols].astype(BF)
+            d_pre[:, hidden + j * chunk : hidden + (j + 1) * chunk] = cand[...].astype(BF)
+            carry_s[:, cols] = jnp.where(low_half, 0.0, swap_halves(reached))
+            at = j * chunk
+            row = 4 + at // width
+            small_o[row : row + 1, at % width : at % width + chunk] += column_sum(total)
+            for start in (at, hidden + at):
+                g_in[:, start : start + chunk] += tn(conv[...], d_pre[:, start : start + chunk])
+
+    @pl.when(step == 2 * blocks - 1)
+    def _():
+        run(MID_LAST)
+        for one in sums:
+            one.finish()
+
+
+def run_mid(depth, ids, mixed, normed, final, lifted, keep, p, q, conv, gains, w_out, w_up, small, g_down, vocab):
     blocks, _, rows = ids.shape
     width, ff = w_up.shape
     hidden = w_out.shape[0]
     total = blocks * rows
-    block = lambda cols: pl.BlockSpec((rows, cols), lambda i: (i, 0))
-    plan = halves([g_down.shape], (2,))
-    bufs = [Reduce.sizes(g_down.shape, lo, hi, depth, False) for _, lo, hi, _ in plan]
-    dma = lambda *shape: pltpu.SemaphoreType.DMA(shape)
-    sums = ((width, ff), (hidden, width), (vocab, width), (ROWS, width), g_down.shape[-2:])
+    last = blocks - 1
+    owners = (2, 2, depth, 2)
+    back = lambda cols: pl.BlockSpec((rows, cols), lambda i: (jnp.minimum(2 * blocks - 1 - i, last), 0))
+    once = pl.BlockSpec((rows, width), lambda i: (jnp.minimum(i, last), 0))
+    both = pl.BlockSpec((rows, ff), lambda i: (jnp.minimum(i, 2 * blocks - 1 - i), 0))
+    up_shape = owners + (width // (8 * depth), ff)
+    shapes = (g_down.shape, up_shape)
+    plans = [halves([shape], (2,)) for shape in shapes]
+    moving = [Reduce.scratch(shape, plan, depth, n > 0) for n, (shape, plan) in enumerate(zip(shapes, plans))]
+    sums = ((width, 2 * hidden), (vocab, width), small.shape, g_down.shape[-2:], up_shape[-2:])
     return pl.pallas_call(
-        functools.partial(mid_kernel, depth, plan, [len(b) for b in bufs]),
-        grid=(blocks,),
-        in_specs=[pl.BlockSpec((1, ROWS, rows), lambda i: (i, 0, 0)), block(hidden)]
-        + [block(width)] * 3 + [block(ff)]
+        functools.partial(mid_kernel, depth, plans, [len(m) for m in moving]),
+        grid=(2 * blocks,),
+        in_specs=[
+            pl.BlockSpec((1, ROWS, rows), lambda i: (jnp.minimum(2 * blocks - 1 - i, last), 0, 0)),
+            back(width), once, back(width), both, back(hidden), back(hidden), back(hidden), back(width),
+        ]
         + [whole(a.shape) for a in (gains, w_out, w_up, small)]
         + [pl.BlockSpec(memory_space=pl.ANY)],
-        out_specs=[block(hidden)] + [whole(s) for s in sums],
-        out_shape=[jax.ShapeDtypeStruct((total, hidden), F32)] + [jax.ShapeDtypeStruct(s, F32) for s in sums],
-        scratch_shapes=[dma(len(plan)), dma(len(plan), depth + 2), dma(len(plan), depth + 2)]
-        + [b for group in bufs for b in group],
+        out_specs=[back(2 * hidden), back(width)] + [whole(s) for s in sums],
+        out_shape=[jax.ShapeDtypeStruct((total, 2 * hidden), BF), jax.ShapeDtypeStruct((total, width), BF)] + [jax.ShapeDtypeStruct(s, F32) for s in sums],
+        scratch_shapes=[
+            pltpu.VMEM(up_shape, F32),
+            pltpu.VMEM((rows, hidden), F32),
+            pltpu.VMEM((rows, 256), F32),
+            pltpu.VMEM((ROWS, hidden), F32),
+        ]
+        + [piece for group in moving for piece in group],
         compiler_params=pltpu.CompilerParams(
-            dimension_semantics=("arbitrary",), collective_id=2, has_side_effects=True, vmem_limit_bytes=62 * MIB
+            dimension_semantics=("arbitrary",), collective_id=2, has_side_effects=True, vmem_limit_bytes=63 * MIB
         ),
         name="mid_back_and_reduce",
-    )(ids, state_low, mixed, normed, final, lifted, gains, w_out, w_up, small, g_down)
+    )(ids, mixed, normed, final, lifted, keep, p, q, conv, gains, w_out, w_up, small, g_down)
 
 
 def adam_kernel(shapes, small, squares, count, *refs):
@@ -1298,14 +1405,10 @@
     loss_o, count_o, norm_o = refs[29:32]
     new_w, new_m, new_v = refs[32:40], refs[40:48], refs[48:56]
     kernel, bias_rows = shapes
-    width = small.shape[1]
     grads = [m[...] for m in mats]
     grads.append(small[0:3, :])
     grads.append(small[ROWS : ROWS + kernel, :])
-    base = ROWS + kernel
-    grads.append(
-        jnp.concatenate([small[base + r : base + r + 1, :] for r in range(bias_rows)], axis=1)
-    )
+    grads.append(jnp.concatenate([small[4 + r : 5 + r, :] for r in range(bias_rows)], axis=1))
     square = squares[0:1, 0:1]
     for grad in grads[5:]:
         square = square + jnp.sum(jnp.sum(grad * grad, axis=1, keepdims=True), axis=0, keepdims=True)
@@ -1342,8 +1445,8 @@
     seqs, span = tokens.shape
     ways = 2 * depth
     three = jnp.stack([tokens, targets, counted]).reshape(3, ways, seqs // ways, 2, span // 2)
-    rows = three.transpose(1, 0, 4, 3, 2).reshape(ways, 3, -1)
-    return jnp.pad(rows, ((0, 0), (0, ROWS - 3), (0, 0)))
+    rows = three.transpose(1, 0, 4, 3, 2).reshape(ways, 6, -1)
+    return jnp.pad(rows, ((0, 0), (0, ROWS - 6), (0, 0)))
 
 
 def body_moved(depth, *args):
@@ -1353,18 +1456,19 @@
     width = table.shape[1]
     taps = conv_taps[0]
     ids = spread_ids(tokens, targets, counted, depth)
-    keep, p, q, conv, queue, state_low, ids, tab, count, *full = run_front(
+    keep, p, q, state_low, ids, tab, count, conv, *full = run_front(
         depth, ids, table, (w_in[0], w_out[0], w_up[0], w_down[0]), gains, taps, gate_bias
     )
+    conv = conv.reshape(-1, width)
     full = [a.reshape(-1, a.shape[-1]) for a in full]
     mixed, normed, final, lifted, g_down, g_head, small = run_tail(1, ids, state_low, tab, count, gains, *full[1:])
     owned = lambda g: g.reshape((2, 2, depth, 2, -1, g.shape[-1]))
-    ds, g_up, g_out, g_emb, small, r_down = run_mid(
-        depth, ids, state_low, mixed, normed, final, lifted, gains, full[1], full[2], small, owned(g_down), tab.shape[0]
+    d_pre, mixed_low, g_in, g_emb, small, r_down, r_up = run_mid(
+        depth, ids, mixed, normed, final, lifted, keep, p, q, conv, gains, full[1], full[2], small, owned(g_down),
+        tab.shape[0],
     )
-    r_up, r_out, r_in, r_tab, small, squares = run_backward(
-        depth, ids, keep, p, q, ds, conv, queue, tab, gains, taps, full[0], (g_head, g_emb), small, r_down,
-        (owned(g_up), owned(g_out)),
+    r_in, r_out, r_tab, small, squares = run_last(
+        depth, ids, d_pre, state_low, mixed_low, tab, gains, taps, full[0], (g_head, g_emb), small, (r_down, r_up), owned(g_in)
     )
     mats = [r_tab, r_in, r_out, r_up, r_down]
     flat = lambda group: [group[0]] + [a[0] for a in group[1:5]] + [group[5], group[6][0], group[7]]

time: 278 us -> 268 us (0.964)
  Pallas kernels: 273 us -> 263 us
    pallas_call x1, Pallas kernels: 72.1 us -> 61.8 us  [run_front(): pl.pallas_call(functools.partial(front_kernel, depth, now, later), grid=(...]
where the time goes in v4:
time: 268 us
  Pallas kernels  263 us (98%)
  local copies, waits for them, and re-layouts  3.73 us (1%)
    pallas_call x1, Pallas kernels, run_mid(): pl.pallas_call(functools.partial(mid_kernel, depth, plans, [len(m) for m...  70.9 us
    pallas_call x1, Pallas kernels, run_tail(): pl.pallas_call(tail_kernel, grid=(blocks,), in_specs=[pl.BlockSpec((join,...  64.7 us
    pallas_call x1, Pallas kernels, run_last(): pl.pallas_call(functools.partial(last_kernel, depth, plans, [len(m) for m...  62.4 us
    pallas_call x1, Pallas kernels, run_front(): pl.pallas_call(functools.partial(front_kernel, depth, now, later), grid=(...  61.8 us

profile of v4, /device:TPU:0, one launch (start us, length us, event | category | flops | bytes accessed | tf_op | source)
XLA Modules:
  0.0 267.7 jit_solution(5419065720825583534)
XLA Ops:
  0.7 0.8 stack.12
  1.5 0.8 stack.13
  2.3 0.8 stack.14
  3.2 0.3 copy.66
  3.5 0.3 copy.67
  3.8 0.7 pad.4.ids
  4.5 61.8 %gather_and_front.1 = (f32[4096,1024]{1,0:T(8,128)}, f32[4096,1024]{1,0:T(8,128)}, f32[4096,1024]{1,0:T(8,128)}, bf16[4096,1024]{1,0:T(8,128)(2,1)}, s32[8,8,512...) custom-call(s32[8,8,256]{2,1,0:T(8,128)} %pad.4.ids, ...), custom_call_target="tpu_custom_call" | custom-call | tf_op jit(solution)/shard_map/gather_and_front/pallas_call | solution.py:1128
  66.2 64.7 %tail_and_head.1 = (f32[4096,512]{1,0:T(8,128)}, bf16[4096,512]{1,0:T(8,128)(2,1)}, f32[4096,512]{1,0:T(8,128)}, bf16[4096,2048]{1,0:T(8,128)(2,1)}, f32[2048,51...) custom-call(s32[8,8,512]{2,1,0:T(8,128)} %get-tuple-element.85.ids.refs_0_, ...), custom_call_target="tpu_custom_call" | custom-call | tf_op jit(solution)/shard_map/tail_and_head/pallas_call | solution.py:1243
  130.9 70.9 %mid_back_and_reduce.1 = (bf16[4096,2048]{1,0:T(8,128)(2,1)}, bf16[4096,512]{1,0:T(8,128)(2,1)}, f32[512,2048]{1,0:T(8,128)}, f32[256,512]{1,0:T(8,128)}, f32[8,...) custom-call(s32[8,8,512]{2,1,0:T(8,128)} %get-tuple-element.85.ids.refs_0_, ...), custom_call_target="tpu_custom_call" | custom-call | tf_op jit(solution)/shard_map/mid_back_and_reduce/pallas_call | solution.py:1377
  201.9 62.4 %last_back_and_reduce.1 = (f32[16,2048]{1,0:T(8,128)}, f32[32,512]{1,0:T(8,128)}, f32[8,512]{1,0:T(8,128)}, f32[16,512]{1,0:T(8,128)}, f32[8,128]{1,0:T(8,128)}) custom-call(s32[8,8,512]{2,1,0:T(8,128)} %get-tuple-element.85.ids.refs_0_, bf16[4096,2048]{1,0:T(8,128)(2,1)} %get-tuple-element.102.refs_1_, ...), custom_call_target="tpu_custom_call" | custom-call | tf_op jit(solution)/shard_map/last_back_and_reduce/pallas_call | solution.py:846
  264.3 3.2 %adam_update.1 = (f32[1,1]{1,0:T(1,128)}, f32[1,1]{1,0:T(1,128)}, f32[1,1]{1,0:T(1,128)}, f32[8,512]{1,0:T(8,128)}, f32[16,2048]{1,0:T(8,128)}, /*index=5*/f32[3...) custom-call(f32[16,512]{1,0:T(8,128)} %get-tuple-element.111.small, ...), custom_call_target="tpu_custom_call" | custom-call | tf_op jit(solution)/shard_map/adam_update/pallas_call | solution.py:1433
  (4 shorter events, 0.0 us)

commit v5 on v4

--- a/solution.py
+++ b/solution.py
@@ -396,14 +396,25 @@
     return pltpu.roll(tile, ROWS // 2, tile.ndim - 2)
 
 
-def one_hot(column, vocab):
-    lane = lax.broadcasted_iota(jnp.int32, (column.shape[0], vocab), 1)
-    return (column == lane).astype(F32).astype(BF)
-
-
-def one_hot_t(row, vocab):
-    place = lax.broadcasted_iota(jnp.int32, (vocab, row.shape[1]), 0)
-    return (row == place).astype(F32).astype(BF)
+def spread_steps(tile, row, start, cols):
+    parts = []
+    for tau in range(LANES // 2):
+        piece = tile[row : row + ROWS, start + tau : start + tau + 1]
+        parts.append(jnp.broadcast_to(piece, (ROWS, cols)))
+    return jnp.concatenate(parts, axis=0)
+
+
+def hits(tile, start, vocab):
+    lane = lax.broadcasted_iota(jnp.int32, (ROWS, vocab), 1)
+    parts = []
+    for tau in range(LANES // 2):
+        piece = tile[0:ROWS, start + tau : start + tau + 1]
+        parts.append((piece == lane).astype(F32))
+    return jnp.concatenate(parts, axis=0)
+
+
+def one_hot(tile, vocab):
+    return hits(tile, 0, vocab).astype(BF)
 
 
 def whole(shape):
@@ -506,21 +517,11 @@
 
 
 def add_into(target, other):
-    lead = target.shape[: len(target.shape) - 2]
-    total = 1
-    for d in lead:
-        total *= d
-
-    def one(i, _):
-        index = []
-        for d in reversed(lead):
-            index.append(lax.rem(i, d))
-            i = lax.div(i, d)
-        index = tuple(reversed(index))
+    lead = [()]
+    for d in target.shape[: len(target.shape) - 2]:
+        lead = [index + (n,) for index in lead for n in range(d)]
+    for index in lead:
         target[index] = target[index] + other[index]
-        return _
-
-    lax.fori_loop(0, total, one, 0)
 
 
 def halves(shapes, cuts=None):
@@ -546,7 +547,7 @@
     def scratch(shape, plan, depth, resident):
         piece = (shape[-2], plan[0][2] - plan[0][1])
         dma = lambda *n: pltpu.SemaphoreType.DMA(n)
-        own = [] if resident else [dma(len(plan)), pltpu.VMEM((2, 2, depth) + piece, F32)]
+        own = [] if resident else [dma(len(plan)), pltpu.VMEM((len(plan), 2, 2, depth) + piece, F32)]
         each = [
             pltpu.VMEM((2, 2, depth) + piece, F32), pltpu.VMEM((2, depth) + piece, F32), pltpu.VMEM((2, depth) + piece, F32)
         ]
@@ -555,7 +556,7 @@
     def load(self, i):
         t, lo, hi, _ = self.plan[i]
         source = self.source.at[:, :, :, self.core, :, pl.ds(lo, hi - lo)]
-        return pltpu.make_async_copy(source, self.own, self.loads.at[i])
+        return pltpu.make_async_copy(source, self.own.at[i], self.loads.at[i])
 
     def copies(self, i, phase):
         t, lo, hi, along_x = self.plan[i]
@@ -583,8 +584,8 @@
         for i in range(len(self.plan)):
             for copy in self.copies(i, 0):
                 copy.start()
-        if not self.resident:
-            self.load(0).start()
+            if not self.resident:
+                self.load(i).start()
 
     def pair(self, n, phase):
         for i in (2 * n, 2 * n + 1):
@@ -601,9 +602,7 @@
                 add_into(whole, self.source.at[:, :, :, core, :, pl.ds(lo, hi - lo)])
             else:
                 self.load(i).wait()
-                add_into(whole, self.own)
-                if i + 1 < len(self.plan):
-                    self.load(i + 1).start()
+                add_into(whole, self.own.at[i])
         elif phase == 1:
             add_into(half, whole.at[y] if along_x else whole.at[:, x])
         elif phase == 2:
@@ -719,12 +718,12 @@
 
 
 SCHEDULE = {
-    1: [(0, 0, 0)], 3: [(0, 1, 0)], 5: [(0, 2, 0)], 7: [(0, 0, 1)], 8: [(0, 3, 0), (0, 1, 1)], 9: [(1, 0, 0)],
-    10: [(0, 0, 2), (0, 2, 1)], 11: [(0, 1, 2), (0, 3, 1)], 13: [(0, 2, 2)], 14: [(0, 3, 2), (1, 0, 1)],
+    0: [(0, 0, 0)], 1: [(0, 1, 0)], 5: [(0, 0, 1), (0, 2, 0)], 8: [(0, 1, 1), (0, 3, 0)], 9: [(0, 0, 2), (0, 2, 1)],
+    10: [(0, 1, 2), (1, 0, 0)], 11: [(0, 3, 1), (0, 2, 2), (1, 1, 0)], 13: [(0, 3, 2), (1, 0, 1)], 14: [(1, 1, 1)], 15: [(1, 0, 2)],
 }
 LEFT_OVER = [
-    (2, 0, 0), (3, 0, 1), (1, 0, 2), (2, 0, 1), (3, 0, 2), (2, 0, 2), (3, 0, 3), (0, 0, 3), (0, 1, 3), (0, 2, 3), (0, 3, 3),
-    (1, 0, 3), (2, 0, 3),
+    (2, 0, 0), (3, 0, 1), (1, 1, 2), (2, 0, 1), (3, 0, 2), (2, 0, 2), (0, 0, 3), (0, 1, 3), (0, 2, 3), (3, 0, 3), (0, 3, 3),
+    (1, 0, 3), (1, 1, 3), (2, 0, 3),
 ]
 
 
@@ -792,7 +791,8 @@
         )
         head_s[...] = mine
         here = ids[0]
-        known = nn(one_hot(here.T[:, 0:1], vocab), qtab[...])
+        hot = one_hot(here, vocab)
+        known = nn(hot, qtab[...])
         d_queue = None
         for k in range(kernel):
             shift = (kernel - 1 - k) * ROWS
@@ -800,8 +800,7 @@
             term = taps[k : k + 1] * part
             d_queue = term if d_queue is None else d_queue + term
             small[ROWS + k : ROWS + k + 1, :] += column_sum(part * known)
-        hot_t = one_hot_t(here[0:1, :], vocab)
-        hot_sum[...] += nn(hot_t, d_queue.astype(BF))
+        hot_sum[...] += tn(hot, d_queue.astype(BF))
 
     @pl.when(step == 2 * blocks - 1)
     def _():
@@ -828,7 +827,8 @@
 
 
 def run_last(depth, ids, d_pre, state_low, mixed_low, tab, gains, taps, w_in, g_tabs, small, done, g_in):
-    blocks, _, rows = ids.shape
+    blocks = ids.shape[0]
+    rows = d_pre.shape[0] // blocks
     vocab, width = tab.shape
     kernel = taps.shape[0]
     rim = (kernel - 1) * ROWS
@@ -836,7 +836,7 @@
     owners = (2, 2, depth, 2)
     hidden = state_low.shape[1]
     shapes = (g_in.shape, owners + (hidden // (8 * depth), width), owners + (vocab // (8 * depth), width))
-    plans = [halves([shape], (cuts,)) for shape, cuts in zip(shapes, (4, 1, 1))]
+    plans = [halves([shape], (cuts,)) for shape, cuts in zip(shapes, (4, 2, 1))]
     back = lambda i: jnp.minimum(2 * blocks - 1 - i, last)
     once = lambda cols: pl.BlockSpec((rows, cols), lambda i: (jnp.minimum(i, last), 0))
     moving = [Reduce.scratch(shape, plan, depth, n > 0) for n, (shape, plan) in enumerate(zip(shapes, plans))]
@@ -847,7 +847,7 @@
         functools.partial(last_kernel, depth, plans, [len(m) for m in moving]),
         grid=(2 * blocks,),
         in_specs=[
-            pl.BlockSpec((1, ROWS, rows), lambda i: (back(i), 0, 0)),
+            pl.BlockSpec((1,) + ids.shape[1:], lambda i: (back(i), 0, 0)),
             pl.BlockSpec((rows, d_pre.shape[1]), lambda i: (back(i), 0)),
             once(hidden),
             once(width),
@@ -885,7 +885,7 @@
     vocab = qtab.shape[0]
     kernel = taps.shape[0]
     rim = (kernel - 1) * ROWS
-    queue = nn(one_hot(id_column(ids_s[block], 0), vocab), qtab[...])
+    queue = nn(one_hot(ids_s[block], vocab), qtab[...])
     padq[rim:, :] = queue
     half = lax.broadcasted_iota(jnp.int32, (rim, width), 0) % ROWS < ROWS // 2
     before = tail_s[...].reshape(kernel - 1, ROWS, width)
@@ -898,11 +898,6 @@
     for k in range(1, kernel):
         conv = conv + taps[k : k + 1] * padq[k * ROWS : k * ROWS + rows, :]
     conv_s[block] = conv.astype(BF)
-
-
-def id_column(ids, which):
-    turned = ids.T
-    return jnp.concatenate([turned[:, 2 * which : 2 * which + 1], turned[:, 2 * which + 1 : 2 * which + 2]], axis=0)
 
 
 def front_block(conv, bias, w_in, keep_o, p_o, q_o, state_o, carry_s, big):
@@ -940,15 +935,15 @@
         carry_s[:, cols] = jnp.where(low_half, swap_halves(state), 0.0)
 
 
-GATHER_SCHEDULE = {1: [(2, 0), (0, 1)], 2: [(1, 1), (3, 0), (4, 0)], 3: [(2, 1), (0, 2)], 4: [(3, 1), (1, 2)], 5: [(4, 1), (2, 2)], 6: [(3, 2)], 7: [(4, 2)]}
+GATHER_SCHEDULE = {1: [(0, 1), (3, 0)], 2: [(1, 1), (4, 0)], 3: [(2, 1), (0, 2)], 4: [(3, 1), (1, 2)], 5: [(4, 1), (2, 2)], 6: [(3, 2)], 7: [(4, 2)]}
 GATHER_LAST = [(0, 3), (1, 3), (2, 3), (3, 3), (4, 3)]
 
 
 def front_kernel(
     depth, now, later,
-    ids, table, w_in, w_out, w_up, w_down, gains, taps, bias,
+    tokens, targets, counted, table, w_in, w_out, w_up, w_down, gains, taps, bias,
     keep_o, p_o, q_o, state_o, ids_o, tab_o, count_o, conv_o, w_in_o, w_out_o, w_up_o, w_down_o,
-    ids_s, tab_s, count_s, in_s, out_s, up_s, down_s, qtab, conv_s, padq, tail_s, carry_s, big,
+    ids, ids_s, tab_s, count_s, in_s, out_s, up_s, down_s, qtab, conv_s, padq, tail_s, carry_s, big,
     ids_send, ids_recv, now_send, now_recv, later_send, later_recv, own_sem, in_sem,
 ):
     step = pl.program_id(0)
@@ -981,12 +976,19 @@
     def _():
         half = table.shape[1] // 2
         tab_s[y, x, z, core] = jnp.concatenate([table[:, 0:half], table[:, half:]], axis=0).astype(BF)
-        share = jnp.zeros((2, ids.shape[2]), F32)
-        for n in range(ids.shape[0]):
-            share = share + ids[n, 4:6, :].astype(F32)
+        share = counted[...].astype(F32)
         share = jnp.sum(jnp.sum(share, axis=1, keepdims=True), axis=0, keepdims=True)
         count_s[y, x, z, core] = jnp.broadcast_to(share, count_o.shape)
         in_s[y, x, z, core] = w_in[...].astype(BF)
+        seqs, span = tokens.shape
+        seqs //= 2 * depth
+        for n in range(2 * depth):
+            parts = []
+            for array in (tokens, targets, counted):
+                mine = array[n * seqs : (n + 1) * seqs, :]
+                parts.append(jnp.concatenate([mine[:, 0 : span // 2], mine[:, span // 2 :]], axis=0))
+            top = jnp.concatenate([parts[0], parts[1]], axis=1)
+            ids[n] = jnp.concatenate([top, jnp.concatenate([parts[2], parts[2]], axis=1)], axis=0)
         ids_s[me] = ids[me]
         greet(*spot, depth)
         pairs = [(i, i + 1) for i in range(0, len(now), 2)]
@@ -1015,12 +1017,14 @@
         act(0, 1)
         act(2, 0)
         begin(4)
+        for i in (0, 1, 2, 3):
+            rest.begin(i)
         act(1, 1)
         act(0, 2)
         act(3, 0)
         act(2, 1)
         act(4, 0)
-        for i in range(len(later)):
+        for i in range(4, len(later)):
             rest.begin(i)
         act(1, 2)
         act(0, 3)
@@ -1065,6 +1069,8 @@
         act(3, 3)
         act(4, 3)
         onward[0].start()
+        for i in later_groups[2]:
+            rest.act(i, 0)
 
     for when, acts in GATHER_SCHEDULE.items():
 
@@ -1074,10 +1080,7 @@
                 for i in later_groups[group]:
                     rest.act(i, phase)
 
-    here = ids_s[step]
-    for n in range(3):
-        ids_o[0, n : n + 1, :] = jnp.concatenate([here[2 * n : 2 * n + 1, :], here[2 * n + 1 : 2 * n + 2, :]], axis=1)
-    ids_o[0, 3:, :] = jnp.zeros((ROWS - 3, ids_o.shape[2]), jnp.int32)
+    ids_o[0] = ids_s[step]
     front_block(conv_s.at[step], bias, FlatRows(in_s), keep_o, p_o, q_o, state_o, carry_s, big)
 
     @pl.when(step == blocks - 1)
@@ -1104,8 +1107,10 @@
 
 
 def run_front(depth, ids, table, mats, gains, taps, bias):
-    blocks, _, half = ids.shape
-    rows = 2 * half
+    blocks = 2 * depth
+    seqs, span = ids[0].shape
+    rows = seqs * span // blocks
+    tile = (blocks, 2 * ROWS, LANES)
     w_in, w_out, w_up, w_down = mats
     width = table.shape[1]
     hidden = bias.shape[1]
@@ -1123,21 +1128,22 @@
     wide = pl.BlockSpec((rows, hidden), lambda i: (i, 0))
     any_spec = pl.BlockSpec(memory_space=pl.ANY)
     dma = lambda *shape: pltpu.SemaphoreType.DMA(shape)
-    args = (ids, table, w_in, w_out, w_up, w_down, gains, taps, bias)
+    args = tuple(ids) + (table, w_in, w_out, w_up, w_down, gains, taps, bias)
     struct = jax.ShapeDtypeStruct
     return pl.pallas_call(
         functools.partial(front_kernel, depth, now, later),
         grid=(blocks,),
         in_specs=[whole(a.shape) for a in args],
         out_specs=[wide] * 4
-        + [pl.BlockSpec((1, ROWS, rows), lambda i: (i, 0, 0)), whole((vocab, width)), whole((ROWS, LANES))]
+        + [pl.BlockSpec((1,) + tile[1:], lambda i: (i, 0, 0)), whole((vocab, width)), whole((ROWS, LANES))]
         + [any_spec] * 5,
         out_shape=[struct((total, hidden), F32)] * 3
-        + [struct((total, hidden), BF), struct((blocks, ROWS, rows), jnp.int32), struct((vocab, width), F32)]
+        + [struct((total, hidden), BF), struct(tile, jnp.int32), struct((vocab, width), F32)]
         + [struct((ROWS, LANES), F32), struct((blocks, rows, width), BF)]
         + [struct(owners + a.shape, BF) for a in mats],
         scratch_shapes=[
-            pltpu.VMEM(ids.shape, jnp.int32),
+            pltpu.VMEM(tile, jnp.int32),
+            pltpu.VMEM(tile, jnp.int32),
             pltpu.VMEM(owners + (2 * ROWS, width // 2), BF),
             pltpu.VMEM(owners + (ROWS, LANES), F32),
             pltpu.VMEM(owners + w_in.shape, BF),
@@ -1184,8 +1190,8 @@
         g_tab[...] = jnp.zeros_like(g_tab)
         small_o[...] = jnp.zeros_like(small_o)
 
-    columns = jnp.concatenate([ids[n].T for n in range(ids.shape[0])], axis=0)
-    hot = one_hot(columns[:, 0:1], vocab)
+    here = ids[0]
+    hot = one_hot(here, vocab)
     mixed = nn(hot, tab_low[...]) + nn(state_low[...], w_out[...])
     mixed_o[...] = mixed
     inverse_b = inv_rms(mixed)
@@ -1210,12 +1216,12 @@
     powers = jnp.exp(logits - top)
     total = jnp.sum(powers, axis=-1, keepdims=True)
     lse = jnp.log(total) + top
-    target = columns[:, 1:2] == lax.broadcasted_iota(jnp.int32, (rows, vocab), 1)
-    picked = jnp.sum(jnp.where(target, logits, 0.0), axis=-1, keepdims=True)
-    weight = columns[:, 2:3].astype(F32)
-    loss = column_sum(weight * (lse - picked))
+    target = hits(here, LANES // 2, vocab)
+    picked = jnp.sum(target * logits, axis=-1, keepdims=True)
+    weight = spread_steps(here, ROWS, 0, vocab).astype(F32)
+    loss = column_sum(weight[:, 0:1] * (lse - picked))
     share = weight * (1.0 / count[0:1, 0:1])
-    d_logits = ((powers * (1.0 / total) - jnp.where(target, 1.0, 0.0)) * share).astype(BF)
+    d_logits = ((powers * (1.0 / total) - target) * share).astype(BF)
     g_tab[...] += tn(d_logits, normed_f)
     d_normed_f = nn(d_logits, tab_low[...])
     small_o[2:3, :] += column_sum(d_normed_f * unit_f)
@@ -1230,9 +1236,9 @@
         lifted_o[:, cols] = (d_active * slope_s[:, cols]).astype(BF)
 
 
-def run_tail(join, ids, state_low, tab, count, gains, w_out, w_up, w_down):
-    blocks, _, rows = ids.shape
-    rows, blocks = rows * join, blocks // join
+def run_tail(ids, state_low, tab, count, gains, w_out, w_up, w_down):
+    blocks = ids.shape[0]
+    rows = state_low.shape[0] // blocks
     vocab, width = tab.shape
     hidden = w_out.shape[0]
     ff = w_up.shape[1]
@@ -1243,7 +1249,7 @@
     return pl.pallas_call(
         tail_kernel,
         grid=(blocks,),
-        in_specs=[pl.BlockSpec((join, ROWS, rows // join), lambda i: (i, 0, 0)), block(hidden)]
+        in_specs=[pl.BlockSpec((1,) + ids.shape[1:], lambda i: (i, 0, 0)), block(hidden)]
         + [whole(a.shape) for a in (tab, count, gains, w_out, w_up, w_down)],
         out_specs=[block(width), block(width), block(width), block(ff)] + [whole(s) for s in sums],
         out_shape=[struct((total, width), F32), struct((total, width), BF), struct((total, width), F32), struct((total, ff), BF)]
@@ -1261,10 +1267,10 @@
 
 
 MID_SCHEDULE = {
-    3: [(0, 0, 0), (0, 1, 0)], 8: [(0, 0, 1)], 9: [(0, 1, 1), (1, 0, 0), (1, 1, 0), (0, 0, 2)],
-    10: [(0, 1, 2)], 11: [(1, 0, 1)], 12: [(1, 1, 1)], 13: [(1, 0, 2), (1, 1, 2)],
+    2: [(0, 0, 0)], 3: [(0, 1, 0)], 8: [(0, 0, 1)], 9: [(0, 1, 1), (1, 0, 0)], 10: [(1, 1, 0), (0, 0, 2), (0, 1, 2)],
+    11: [(1, 0, 1)], 12: [(1, 1, 1)], 13: [(1, 0, 2)], 14: [(1, 1, 2), (0, 0, 3), (0, 1, 3)],
 }
-MID_LAST = [(0, 0, 3), (0, 1, 3), (1, 0, 3), (1, 1, 3)]
+MID_LAST = [(1, 0, 3), (1, 1, 3)]
 
 
 def mid_kernel(depth, plans, counts, *refs):
@@ -1321,8 +1327,8 @@
         mixed_low = d_mixed.astype(BF)
         rest = (d_mixed - mixed_low.astype(F32)).astype(BF)
         ds[...] = nt(mixed_low, w_out[...])
-        hot_t = one_hot_t(ids[0][0:1, :], vocab)
-        g_emb[...] += nn(hot_t, mixed_low) + nn(hot_t, rest)
+        hot = one_hot(ids[0], vocab)
+        g_emb[...] += tn(hot, mixed_low) + tn(hot, rest)
         mixed_o[...] = mixed_low
 
         low_half = lax.broadcasted_iota(jnp.int32, (ROWS, chunk), 0) < ROWS // 2
@@ -1360,7 +1366,8 @@
 
 
 def run_mid(depth, ids, mixed, normed, final, lifted, keep, p, q, conv, gains, w_out, w_up, small, g_down, vocab):
-    blocks, _, rows = ids.shape
+    blocks = ids.shape[0]
+    rows = mixed.shape[0] // blocks
     width, ff = w_up.shape
     hidden = w_out.shape[0]
     total = blocks * rows
@@ -1378,7 +1385,7 @@
         functools.partial(mid_kernel, depth, plans, [len(m) for m in moving]),
         grid=(2 * blocks,),
         in_specs=[
-            pl.BlockSpec((1, ROWS, rows), lambda i: (jnp.minimum(2 * blocks - 1 - i, last), 0, 0)),
+            pl.BlockSpec((1,) + ids.shape[1:], lambda i: (jnp.minimum(2 * blocks - 1 - i, last), 0, 0)),
             back(width), once, back(width), both, back(hidden), back(hidden), back(hidden), back(width),
         ]
         + [whole(a.shape) for a in (gains, w_out, w_up, small)]
@@ -1441,27 +1448,17 @@
     )(*args)
 
 
-def spread_ids(tokens, targets, counted, depth):
-    seqs, span = tokens.shape
-    ways = 2 * depth
-    three = jnp.stack([tokens, targets, counted]).reshape(3, ways, seqs // ways, 2, span // 2)
-    rows = three.transpose(1, 0, 4, 3, 2).reshape(ways, 6, -1)
-    return jnp.pad(rows, ((0, 0), (0, ROWS - 6), (0, 0)))
-
-
 def body_moved(depth, *args):
-    tokens, targets, counted = args[:3]
     weights, firsts, seconds = args[3:11], args[11:19], args[19:27]
     table, w_in, w_out, w_up, w_down, gains, conv_taps, gate_bias = weights
     width = table.shape[1]
     taps = conv_taps[0]
-    ids = spread_ids(tokens, targets, counted, depth)
     keep, p, q, state_low, ids, tab, count, conv, *full = run_front(
-        depth, ids, table, (w_in[0], w_out[0], w_up[0], w_down[0]), gains, taps, gate_bias
+        depth, args[:3], table, (w_in[0], w_out[0], w_up[0], w_down[0]), gains, taps, gate_bias
     )
     conv = conv.reshape(-1, width)
     full = [a.reshape(-1, a.shape[-1]) for a in full]
-    mixed, normed, final, lifted, g_down, g_head, small = run_tail(1, ids, state_low, tab, count, gains, *full[1:])
+    mixed, normed, final, lifted, g_down, g_head, small = run_tail(ids, state_low, tab, count, gains, *full[1:])
     owned = lambda g: g.reshape((2, 2, depth, 2, -1, g.shape[-1]))
     d_pre, mixed_low, g_in, g_emb, small, r_down, r_up = run_mid(
         depth, ids, mixed, normed, final, lifted, keep, p, q, conv, gains, full[1], full[2], small, owned(g_down),

time: 268 us -> 253 us (0.944)
  Pallas kernels: 263 us -> 252 us
  local copies, waits for them, and re-layouts: 3.73 us -> 0 us
    pallas_call x1, Pallas kernels: 62.4 us -> 57.2 us  [run_last(): pl.pallas_call(functools.partial(last_kernel, depth, plans, [len(m) for m...]
    pallas_call x1, Pallas kernels: 70.9 us -> 65.9 us  [run_mid(): pl.pallas_call(functools.partial(mid_kernel, depth, plans, [len(m) for m...]
where the time goes in v5:
time: 253 us
  Pallas kernels  252 us (100%)
    pallas_call x1, Pallas kernels, run_mid(): pl.pallas_call(functools.partial(mid_kernel, depth, plans, [len(m) for m...  65.9 us
    pallas_call x1, Pallas kernels, run_tail(): pl.pallas_call(tail_kernel, grid=(blocks,), in_specs=[pl.BlockSpec((1,) +...  64.5 us
    pallas_call x1, Pallas kernels, run_front(): pl.pallas_call(functools.partial(front_kernel, depth, now, later), grid=(...  60.9 us
    pallas_call x1, Pallas kernels, run_last(): pl.pallas_call(functools.partial(last_kernel, depth, plans, [len(m) for m...  57.2 us

profile of v5, /device:TPU:0, one launch (start us, length us, event | category | flops | bytes accessed | tf_op | source)
XLA Modules:
  0.0 252.6 jit_solution(4334563301340808171)
XLA Ops:
  0.7 60.9 %gather_and_front.1 = (f32[4096,1024]{1,0:T(8,128)}, f32[4096,1024]{1,0:T(8,128)}, f32[4096,1024]{1,0:T(8,128)}, bf16[4096,1024]{1,0:T(8,128)(2,1)}, s32[8,16,12...) custom-call(s32[32,128]{1,0:T(8,128)} %tokens.1, ...), custom_call_target="tpu_custom_call" | custom-call | tf_op jit(solution)/shard_map/gather_and_front/pallas_call | solution.py:1133
  61.6 64.5 %tail_and_head.1 = (f32[4096,512]{1,0:T(8,128)}, bf16[4096,512]{1,0:T(8,128)(2,1)}, f32[4096,512]{1,0:T(8,128)}, bf16[4096,2048]{1,0:T(8,128)(2,1)}, f32[2048,51...) custom-call(s32[8,16,128]{2,1,0:T(8,128)} %get-tuple-element.85.ids.refs_0_, ...), custom_call_target="tpu_custom_call" | custom-call | tf_op jit(solution)/shard_map/tail_and_head/pallas_call | solution.py:1249
  126.1 65.9 %mid_back_and_reduce.1 = (bf16[4096,2048]{1,0:T(8,128)(2,1)}, bf16[4096,512]{1,0:T(8,128)(2,1)}, f32[512,2048]{1,0:T(8,128)}, f32[256,512]{1,0:T(8,128)}, f32[8,...) custom-call(s32[8,16,128]{2,1,0:T(8,128)} %get-tuple-element.85.ids.refs_0_, ...), custom_call_target="tpu_custom_call" | custom-call | tf_op jit(solution)/shard_map/mid_back_and_reduce/pallas_call | solution.py:1384
  192.0 57.2 %last_back_and_reduce.1 = (f32[16,2048]{1,0:T(8,128)}, f32[32,512]{1,0:T(8,128)}, f32[8,512]{1,0:T(8,128)}, f32[16,512]{1,0:T(8,128)}, f32[8,128]{1,0:T(8,128)}) custom-call(s32[8,16,128]{2,1,0:T(8,128)} %get-tuple-element.85.ids.refs_0_, bf16[4096,2048]{1,0:T(8,128)(2,1)} %get-tuple-element.102.refs_1_, ...), custom_call_target="tpu_custom_call" | custom-call | tf_op jit(solution)/shard_map/last_back_and_reduce/pallas_call | solution.py:846
  249.3 3.2 %adam_update.1 = (f32[1,1]{1,0:T(1,128)}, f32[1,1]{1,0:T(1,128)}, f32[1,1]{1,0:T(1,128)}, f32[8,512]{1,0:T(8,128)}, f32[16,2048]{1,0:T(8,128)}, /*index=5*/f32[3...) custom-call(f32[16,512]{1,0:T(8,128)} %get-tuple-element.111.small, ...), custom_call_target="tpu_custom_call" | custom-call | tf_op jit(solution)/shard_map/adam_update/pallas_call | solution.py:1440

commit v6 on v5

--- a/solution.py
+++ b/solution.py
@@ -432,6 +432,15 @@
     return (y * 2 + x, z * 2 + core)
 
 
+def greet_all(y, x, z, core, depth):
+    barrier = pltpu.get_barrier_semaphore()
+    for n in range(1, 8 * depth):
+        dy, dx, dz, dc = n // (4 * depth), n // (2 * depth) % 2, n // 2 % depth, n % 2
+        peer = device((y + dy) % 2, (x + dx) % 2, (z + dz) % depth, (core + dc) % 2)
+        pl.semaphore_signal(barrier, inc=1, device_id=peer, device_id_type=pl.DeviceIdType.MESH)
+    pl.semaphore_wait(barrier, 8 * depth - 1)
+
+
 def greet(y, x, z, core, depth):
     barrier = pltpu.get_barrier_semaphore()
     peers = [device(1 - y, x, z, core), device(y, 1 - x, z, core), device(1 - y, 1 - x, z, core)]
@@ -626,44 +635,27 @@
 class Everywhere:
     def __init__(self, slots, sends, recvs, depth, at):
         y, x, z, core = at
-        self.slots, self.ways = slots, 2 * depth
-        self.me, self.other = z * 2 + core, self.ways + y * 2 + x
-        self.near, self.far = [], []
+        self.slots, self.count = slots, 8 * depth
+        self.me = ((y * 2 + x) * depth + z) * 2 + core
+        self.copies = []
         mine = slots.at[self.me]
-        for dz in range(depth):
-            for dc in range(2):
-                if dz or dc:
-                    n = dz * 2 + dc
-                    peer = device(y, x, (z + dz) % depth, (core + dc) % 2)
-                    self.near.append(remote(mine, mine, sends.at[n], recvs.at[n], peer))
-        mine = slots.at[self.other]
-        for n, (dy, dx) in enumerate(((0, 1), (1, 0), (1, 1))):
-            n += self.ways
-            peer = device((y + dy) % 2, (x + dx) % 2, z, core)
-            self.far.append(remote(mine, mine, sends.at[n], recvs.at[n], peer))
-
-    def total(self, lo, hi):
-        value = self.slots[lo]
-        for n in range(lo + 1, hi):
+        for n in range(1, self.count):
+            dy, dx, dz, dc = n // (4 * depth), n // (2 * depth) % 2, n // 2 % depth, n % 2
+            peer = device((y + dy) % 2, (x + dx) % 2, (z + dz) % depth, (core + dc) % 2)
+            self.copies.append(remote(mine, mine, sends.at[n], recvs.at[n], peer))
+
+    def begin(self, value):
+        self.slots[self.me] = value
+        for copy in self.copies:
+            copy.start()
+
+    def end(self):
+        for copy in self.copies:
+            copy.wait()
+        value = self.slots[0]
+        for n in range(1, self.count):
             value = value + self.slots[n]
         return value
-
-    def begin(self, value):
-        self.slots[self.me] = value
-        for copy in self.near:
-            copy.start()
-
-    def middle(self):
-        for copy in self.near:
-            copy.wait()
-        self.slots[self.other] = self.total(0, self.ways)
-        for copy in self.far:
-            copy.start()
-
-    def end(self):
-        for copy in self.far:
-            copy.wait()
-        return self.total(self.ways, self.ways + 4)
 
 
 class EverywhereHalved:
@@ -728,18 +720,22 @@
 
 
 def last_kernel(depth, plans, counts, *refs):
-    ids, d_pre, state_low, mixed_low, tab, gains, taps, w_in, g_tab_a, g_tab_b, small_in, r_down, r_up, g_in = refs[:14]
+    ids, d_pre, state_low, mixed_low, tab, gains, taps, small_in, r_down, r_up, w_in_h, g_tab_ah, g_tab_bh, g_in = refs[:14]
     r_in, r_out, r_tab, small_o, squares_o = refs[14:19]
-    small, g_out, g_tab, qtab, ext, head_s, hot_sum = refs[19:26]
-    whole_s, part_s, sq_slots, sends, recvs, sq_sends, sq_recvs = refs[26:33]
+    small, g_out, g_tab, qtab, ext, head_s, hot_sum, w_in, g_tab_a, g_tab_b, kept_sem = refs[19:30]
+    whole_s, part_s, sq_slots, sends, recvs, sq_sends, sq_recvs = refs[30:37]
     spot = place()
-    sums, at = [], 33
+    sums, at = [], 37
     for n, (source, out) in enumerate(((g_in, r_in), (g_out, r_out), (g_tab, r_tab))):
         sums.append(Reduce(plans[n], depth, source, n > 0, out, refs[at : at + counts[n]], spot))
         at += counts[n]
     smalls = EverywhereHalved(whole_s, part_s, sends, recvs, depth, spot)
     squares = Everywhere(sq_slots, sq_sends, sq_recvs, depth, spot)
     step = pl.program_id(0)
+    kept = [
+        pltpu.make_async_copy(src, dst, kept_sem.at[n])
+        for n, (src, dst) in enumerate(((w_in_h, w_in), (g_tab_ah, g_tab_a), (g_tab_bh, g_tab_b)))
+    ]
     blocks = pl.num_programs(0) // 2
     rows = d_pre.shape[0]
     vocab, width = tab.shape
@@ -755,8 +751,10 @@
 
     @pl.when(step == 0)
     def _():
-        greet(*spot, depth)
+        greet_all(*spot, depth)
         sums[0].begin()
+        for copy in kept:
+            copy.start()
         wide = tab[...].astype(BF).astype(F32)
         qtab[...] = (wide * inv_rms(wide) * gains[0:1]).astype(BF)
         g_out[...] = jnp.zeros_like(g_out)
@@ -778,6 +776,8 @@
     @pl.when(step == blocks - 1)
     def _():
         sums[1].begin()
+        for copy in kept:
+            copy.wait()
 
     @pl.when(step >= blocks)
     def _():
@@ -818,10 +818,9 @@
         for out in (r_in, r_out, r_tab, r_down, r_up):
             value = out[...]
             square = square + jnp.sum(jnp.sum(value * value, axis=1, keepdims=True), axis=0, keepdims=True)
-        squares.begin(jnp.broadcast_to(square, (ROWS, LANES)))
+        squares.begin(jnp.broadcast_to(square, (1, LANES)))
         small_o[...] = smalls.step(4)
-        squares.middle()
-        squares_o[...] = squares.end()
+        squares_o[...] = jnp.broadcast_to(squares.end(), (ROWS, LANES))
         for one in sums:
             one.finish()
 
@@ -842,7 +841,7 @@
     moving = [Reduce.scratch(shape, plan, depth, n > 0) for n, (shape, plan) in enumerate(zip(shapes, plans))]
     out = [s[-2:] for s in shapes] + [(2 * ROWS, width), (ROWS, LANES)]
     dma = lambda *shape: pltpu.SemaphoreType.DMA(shape)
-    fixed = (tab, gains, taps, w_in) + tuple(g_tabs) + (small,) + tuple(done)
+    fixed = (tab, gains, taps, small) + tuple(done)
     return pl.pallas_call(
         functools.partial(last_kernel, depth, plans, [len(m) for m in moving]),
         grid=(2 * blocks,),
@@ -853,7 +852,7 @@
             once(width),
         ]
         + [whole(a.shape) for a in fixed]
-        + [pl.BlockSpec(memory_space=pl.ANY)],
+        + [pl.BlockSpec(memory_space=pl.ANY)] * 4,
         out_specs=[whole(s) for s in out],
         out_shape=[jax.ShapeDtypeStruct(s, F32) for s in out],
         scratch_shapes=[
@@ -864,20 +863,24 @@
             pltpu.VMEM((rim + rows, width), F32),
             pltpu.VMEM((rim, width), F32),
             pltpu.VMEM((vocab, width), F32),
+            pltpu.VMEM(w_in.shape, BF),
+            pltpu.VMEM((vocab, width), F32),
+            pltpu.VMEM((vocab, width), F32),
+            dma(3),
             pltpu.VMEM((3, 2, ROWS, width), F32),
             pltpu.VMEM((depth + 4, ROWS, width), F32),
-            pltpu.VMEM((2 * depth + 4, ROWS, LANES), F32),
+            pltpu.VMEM((8 * depth, 1, LANES), F32),
             dma(depth + 4),
             dma(depth + 4),
-            dma(2 * depth + 4),
-            dma(2 * depth + 4),
+            dma(8 * depth),
+            dma(8 * depth),
         ]
         + [piece for group in moving for piece in group],
         compiler_params=pltpu.CompilerParams(
             dimension_semantics=("arbitrary",), collective_id=1, has_side_effects=True, vmem_limit_bytes=62 * MIB
         ),
         name="last_back_and_reduce",
-    )(ids, d_pre, state_low, mixed_low, *fixed, g_in)
+    )(ids, d_pre, state_low, mixed_low, *fixed, w_in, *g_tabs, g_in)
 
 
 def conv_block(block, ids_s, qtab, taps, conv_s, padq, tail_s):

time: 253 us -> 251 us (level)
  no operation moved by 1% of the time
where the time goes in v6:
time: 251 us
  Pallas kernels  250 us (100%)
    pallas_call x1, Pallas kernels, run_mid(): pl.pallas_call(functools.partial(mid_kernel, depth, plans, [len(m) for m...  65.9 us
    pallas_call x1, Pallas kernels, run_tail(): pl.pallas_call(tail_kernel, grid=(blocks,), in_specs=[pl.BlockSpec((1,) +...  64.5 us
    pallas_call x1, Pallas kernels, run_front(): pl.pallas_call(functools.partial(front_kernel, depth, now, later), grid=(...  60.9 us
    pallas_call x1, Pallas kernels, run_last(): pl.pallas_call(functools.partial(last_kernel, depth, plans, [len(m) for m...  55.5 us

profile of v6, /device:TPU:0, one launch (start us, length us, event | category | flops | bytes accessed | tf_op | source)
XLA Modules:
  0.0 250.9 jit_solution(17564402525367731038)
XLA Ops:
  0.7 60.9 %gather_and_front.1 = (f32[4096,1024]{1,0:T(8,128)}, f32[4096,1024]{1,0:T(8,128)}, f32[4096,1024]{1,0:T(8,128)}, bf16[4096,1024]{1,0:T(8,128)(2,1)}, s32[8,16,12...) custom-call(s32[32,128]{1,0:T(8,128)} %tokens.1, ...), custom_call_target="tpu_custom_call" | custom-call | tf_op jit(solution)/shard_map/gather_and_front/pallas_call | solution.py:1136
  61.6 64.5 %tail_and_head.1 = (f32[4096,512]{1,0:T(8,128)}, bf16[4096,512]{1,0:T(8,128)(2,1)}, f32[4096,512]{1,0:T(8,128)}, bf16[4096,2048]{1,0:T(8,128)(2,1)}, f32[2048,51...) custom-call(s32[8,16,128]{2,1,0:T(8,128)} %get-tuple-element.85.ids.refs_0_, ...), custom_call_target="tpu_custom_call" | custom-call | tf_op jit(solution)/shard_map/tail_and_head/pallas_call | solution.py:1252
  126.1 65.9 %mid_back_and_reduce.1 = (bf16[4096,2048]{1,0:T(8,128)(2,1)}, bf16[4096,512]{1,0:T(8,128)(2,1)}, f32[512,2048]{1,0:T(8,128)}, f32[256,512]{1,0:T(8,128)}, f32[8,...) custom-call(s32[8,16,128]{2,1,0:T(8,128)} %get-tuple-element.85.ids.refs_0_, ...), custom_call_target="tpu_custom_call" | custom-call | tf_op jit(solution)/shard_map/mid_back_and_reduce/pallas_call | solution.py:1387
  192.0 55.5 %last_back_and_reduce.1 = (f32[16,2048]{1,0:T(8,128)}, f32[32,512]{1,0:T(8,128)}, f32[8,512]{1,0:T(8,128)}, f32[16,512]{1,0:T(8,128)}, f32[8,128]{1,0:T(8,128)}) custom-call(s32[8,16,128]{2,1,0:T(8,128)} %get-tuple-element.85.ids.refs_0_, bf16[4096,2048]{1,0:T(8,128)(2,1)} %get-tuple-element.102.refs_1_, ...), custom_call_target="tpu_custom_call" | custom-call | tf_op jit(solution)/shard_map/last_back_and_reduce/pallas_call | solution.py:845
  247.5 3.2 %adam_update.1 = (f32[1,1]{1,0:T(1,128)}, f32[1,1]{1,0:T(1,128)}, f32[1,1]{1,0:T(1,128)}, f32[8,512]{1,0:T(8,128)}, f32[16,2048]{1,0:T(8,128)}, /*index=5*/f32[3...) custom-call(f32[16,512]{1,0:T(8,128)} %get-tuple-element.111.small, ...), custom_call_target="tpu_custom_call" | custom-call | tf_op jit(solution)/shard_map/adam_update/pallas_call | solution.py:1443
